TPU v7x, 256 devices: a whole 4x4x8 slice. The times are simulated.
256 devices in a mesh: stack: 16 (over y, z_lo, core), tile: 16 (over z_hi, x).
Axes of the slice: x: 4, y: 4, z: 8 (z_hi: 4, z_lo: 2; z = z_hi * 2 + z_lo), core: 2. Of those that a mesh axis runs over, the one named last changes fastest.
Arguments:
- patches: bfloat16 [128, 4096, 128], P('stack', 'tile'), may hold values from -6 to 6
- candidates: int32 [128, 2, 8, 4096], P('stack', None, None, 'tile'), may hold values from 0 to 4095, as said below
- offsets: int32 [128, 2, 2, 8, 4096], P('stack', None, None, None, 'tile'), may hold values from -64 to 63
- pairs: int32 [128, 2], P('stack'), may hold values 0 or 1
- start: float32 [128, 2, 4096], P('stack', None, 'tile'), may hold values from -3 to 3
Outputs:
- aligned: float32 [128, 2, 4096], P('stack', None, 'tile')
- targets: float32 [128, 2, 2, 4096], P('stack', None, None, 'tile')
Inputs may be any that keep to these rules, and one draw needn't show every extreme that they name: Each candidate of a vertex lies at most 2 mesh rows and 2 mesh columns from the vertex, clipped to the mesh; the candidates of one vertex differ except where clipping merges them.
All inputs are finite; a program needn't handle non-finite values. No bound on the sum of `pairs` on one device may be relied on, other than what follows from the above.
Results may differ from a plain program's by a relative error of at most 0.00045.
Values may be sent and summed in bfloat16 or wider, within the bound.
No kernel may reach another device: no remote copies, remote signals or barrier semaphores. Data moves between devices by JAX's collectives and lax.ppermute only.
A program may use at most 64 MiB of HBM per device.

v0:
```python
import jax
import jax.numpy as jnp
from jax import lax
from jax.sharding import PartitionSpec as P

TILE_SIDE = 16
GRID_COLS = 4
PATCH = 128
REACH = 2
ROUNDS = 2
VT = 256


pixel_pitch = 128.0
relax_step = 0.1


def shifted_2(block, axis, distance):
    devices = range(lax.axis_size(axis))
    route = [(i - distance, i) for i in devices if i - distance in devices]
    return lax.ppermute(block, axis, route)


def extended_2(cells, sides, width):
    for axis, dim in sides:
        count = lax.axis_size(axis)
        ends = count - 1
        head = lax.slice_in_dim(cells, 0, width, axis=dim)
        tail = lax.slice_in_dim(cells, cells.shape[dim] - width, cells.shape[dim], axis=dim)
        cells = jnp.concatenate(
            [
                lax.ppermute(tail, axis, [(i, (i + 1) % count) for i in range(ends)]),
                cells,
                lax.ppermute(head, axis, [((i + 1) % count, i) for i in range(ends)]),
            ],
            axis=dim,
        )
    return cells


def place(ids):
    tile = ids // VT
    inner = ids % VT
    row = tile // GRID_COLS * TILE_SIDE + inner // TILE_SIDE
    col = tile % GRID_COLS * TILE_SIDE + inner % TILE_SIDE
    return (row, col)


def widen(field, width, row_dim, mover, tile_col):
    col_dim = row_dim + 1
    side = field.shape[col_dim]
    left = mover(lax.slice_in_dim(field, side - width, side, axis=col_dim), 1)
    right = mover(lax.slice_in_dim(field, 0, width, axis=col_dim), -1)
    left = jnp.where(tile_col > 0, left, jnp.zeros_like(left))
    right = jnp.where(tile_col < GRID_COLS - 1, right, jnp.zeros_like(right))
    field = jnp.concatenate([left, field, right], axis=col_dim)
    height = field.shape[row_dim]
    above = mover(lax.slice_in_dim(field, height - width, height, axis=row_dim), GRID_COLS)
    below = mover(lax.slice_in_dim(field, 0, width, axis=row_dim), -GRID_COLS)
    return jnp.concatenate([above, field, below], axis=row_dim)


def score_rows(own, table, index):

    def per_section(items):
        sec, mine, rows_index = items
        result = []
        for zed in range(2):
            other = lax.dynamic_index_in_dim(table, sec + zed + 1, 0, keepdims=False)
            picked = jnp.take(other, rows_index[zed], axis=0)
            result.append(
                jnp.einsum("kvp,vp->kv", picked, mine, preferred_element_type=jnp.float32)
            )
        return jnp.stack(result)

    return lax.map(per_section, (jnp.arange(own.shape[0], dtype=jnp.int32), own, index))


def on_device(patches, candidates, offsets, pairs, start):
    sec_dev = patches.shape[0]
    sections = sec_dev * lax.axis_size("stack")
    stack_pos = lax.axis_index("stack")
    tile_pos = lax.axis_index("tile")
    tile_row = tile_pos // GRID_COLS
    tile_col = tile_pos % GRID_COLS
    span = TILE_SIDE + 2 * REACH

    def patch_mover(strip, by):
        return shifted_2(strip, "tile", by)

    upper = shifted_2(patches[:2], "stack", -1)
    extended = jnp.concatenate([patches, upper], axis=0)
    grid = extended.reshape(sec_dev + 2, TILE_SIDE, TILE_SIDE, PATCH)
    table = widen(grid, REACH, 1, patch_mover, tile_col).reshape(sec_dev + 2, span * span, PATCH)
    cand_r, cand_c = place(candidates)
    local_r = cand_r - tile_row * TILE_SIDE + REACH
    local_c = cand_c - tile_col * TILE_SIDE + REACH
    scores = score_rows(patches, table, local_r * span + local_c)
    weights = jax.nn.softmax(scores * PATCH ** (-0.5), axis=2)
    own_r, own_c = place(tile_pos * VT + jnp.arange(VT, dtype=jnp.int32))
    shifted = offsets.astype(jnp.float32) / pixel_pitch
    row = jnp.sum(weights * (cand_r.astype(jnp.float32) + shifted[:, :, 0]), axis=2) - own_r.astype(
        jnp.float32
    )
    col = jnp.sum(weights * (cand_c.astype(jnp.float32) + shifted[:, :, 1]), axis=2) - own_c.astype(
        jnp.float32
    )
    global_sec = stack_pos * sec_dev + jnp.arange(sec_dev, dtype=jnp.int32)
    zeds = jnp.arange(2, dtype=jnp.int32)[None, :]
    valid = global_sec[:, None] + zeds + 1 < sections
    targets = jnp.stack([row, col], axis=2)
    targets = jnp.where(valid[:, :, None, None], targets, jnp.float32(0.0))
    coupling = jnp.where(valid, pairs.astype(jnp.float32), jnp.float32(0.0))
    lower_t, lower_c = shifted_2((targets[-2:], coupling[-2:]), "stack", 1)
    all_t = jnp.concatenate([lower_t, targets], axis=0)
    all_c = jnp.concatenate([lower_c, coupling], axis=0)
    mesh_rows = lax.axis_size("tile") // GRID_COLS * TILE_SIDE
    mesh_cols = GRID_COLS * TILE_SIDE
    grid_r = tile_row * TILE_SIDE + jnp.arange(TILE_SIDE, dtype=jnp.int32)[:, None]
    grid_c = tile_col * TILE_SIDE + jnp.arange(TILE_SIDE, dtype=jnp.int32)[None, :]
    has_up = grid_r > 0
    has_down = grid_r < mesh_rows - 1
    has_left = grid_c > 0
    has_right = grid_c < mesh_cols - 1

    def edge_mover(strip, by):
        return shifted_2(strip, "tile", by)

    u = start
    for step in range(ROUNDS):
        wide_u = extended_2(u, (("stack", 0),), 2)
        zforce = jnp.zeros_like(u)
        for zed in range(2):
            upward = all_c[2:, zed, None, None] * (
                wide_u[3 + zed : 3 + zed + sec_dev] - u - targets[:, zed]
            )
            low = 1 - zed
            downward = all_c[low : low + sec_dev, zed, None, None] * (
                u - wide_u[low : low + sec_dev] - all_t[low : low + sec_dev, zed]
            )
            zforce = zforce + upward - downward
        field = u.reshape(sec_dev, 2, TILE_SIDE, TILE_SIDE)
        wide = widen(field, 1, 2, edge_mover, tile_col)
        above = wide[:, :, :-2, 1:-1]
        below = wide[:, :, 2:, 1:-1]
        left = wide[:, :, 1:-1, :-2]
        right = wide[:, :, 1:-1, 2:]
        zero = jnp.float32(0.0)
        lap_r = jnp.where(has_down, below - field, zero) - jnp.where(has_up, field - above, zero)
        lap_c = jnp.where(has_right, right - field, zero) - jnp.where(has_left, field - left, zero)
        plane = (lap_r + lap_c).reshape(sec_dev, 2, VT)
        u = u + relax_step * (plane + zforce)
    return (u, targets)


def solution(mesh):
    placed = (
        P("stack", "tile", None),
        P("stack", None, None, "tile"),
        P("stack", None, None, None, "tile"),
        P("stack", None),
        P("stack", None, "tile"),
    )
    return jax.shard_map(
        on_device,
        mesh=mesh,
        in_specs=placed,
        out_specs=(P("stack", None, "tile"), P("stack", None, None, "tile")),
        check_vma=False,
    )
```

profile of v0, /device:TPU:88, one launch (start us, length us, event | category | flops | bytes accessed | tf_op | source)
XLA Modules:
  0.0 262.8 jit_solution(9116154430718425874)
XLA Ops:
  1.6 3.4 %collective-permute-start.5 = (bf16[2,256,128]{2,1,0:T(8,128)(2,1)S(1)}, bf16[2,256,128]{2,1,0:T(8,128)(2,1)S(1)}, u32[]{:S(2)}, u32[]{:S(2)}) collective-permute-start(bf16[2,256,128]{2,1,0:T(8,128)(2,1)S(1)} %slice.190), channel_id=1, source_target_pairs={{16,0},{32,16},{48,32},{64,48},{80,64},{96,80},{112,96},{128,112},... | collective-permute-start | bytes 393224 | tf_op jit(solution)/shard_map/ppermute | solution.py:21
  6.0 3.9 %collective-permute-start.1 = (f32[8,2,16,1]{3,2,0,1:T(8,128)S(1)}, f32[8,2,16,1]{3,2,0,1:T(8,128)S(1)}, u32[]{:S(2)}, u32[]{:S(2)}) collective-permute-start(f32[8,2,16,1]{3,2,0,1:T(8,128)S(1)} %get-tuple-element.166), channel_id=1, source_target_pairs={{1,0},{2,1},{3,2},{4,3},{5,4},{6,5},{7,6},{8,7},{9,8},{10,9},{11,1... | collective-permute-start | bytes 3080 | tf_op jit(solution)/shard_map/ppermute | solution.py:21
  9.9 2.1 collective-permute-start
  16.0 4.5 %collective-permute-start.4 = (f32[2,2,256]{2,0,1:T(2,128)}, f32[2,2,256]{2,0,1:T(2,128)}, u32[]{:S(2)}, u32[]{:S(2)}) collective-permute-start(f32[2,2,256]{2,0,1:T(2,128)} %get-tuple-element.170), channel_id=1, source_target_pairs={{16,0},{32,16},{48,32},{64,48},{80,64},{96,80},{112,96},{128,112},... | collective-permute-start | bytes 12296 | tf_op jit(solution)/shard_map/ppermute | solution.py:34
  27.7 6.8 %collective-permute-start.7 = (bf16[10,16,2,128]{3,2,1,0:T(2,128)(2,1)S(1)}, bf16[10,16,2,128]{3,2,1,0:T(2,128)(2,1)S(1)}, u32[]{:S(2)}, u32[]{:S(2)}) collective-permute-start(bf16[10,16,2,128]{3,2,1,0:T(2,128)(2,1)S(1)} %get-tuple-element.159), channel_id=1, source_target_pairs={{1,0},{2,1},{3,2},{4,3},{5,4},{6,5},{7,6},{8,7},{9,8},{10,9},{11,1... | collective-permute-start | bytes 245768 | tf_op jit(solution)/shard_map/ppermute | solution.py:21
  36.5 7.6 %collective-permute-start.3 = (f32[8,2,1,18]{3,2,0,1:T(1,128)S(1)}, f32[8,2,1,18]{3,2,0,1:T(1,128)S(1)}, u32[]{:S(2)}, u32[]{:S(2)}) collective-permute-start(f32[8,2,1,18]{3,2,0,1:T(1,128)S(1)} %get-tuple-element.163), channel_id=1, source_target_pairs={{0,4},{1,5},{2,6},{3,7},{4,8},{5,9},{6,10},{7,11},{8,12},{9,13},{1... | collective-permute-start | bytes 3464 | tf_op jit(solution)/shard_map/ppermute | solution.py:21
  46.1 7.3 %collective-permute-done.6 = bf16[10,16,2,128]{3,2,1,0:T(2,128)(2,1)S(1)} collective-permute-done((bf16[10,16,2,128]{3,2,1,0:T(2,128)(2,1)S(1)}, bf16[10,16,2,128]{3,2,1,0:T(2,128)(2,1)S(1)}, u32[]{:S(2)}, u32[]{:S(2)}) %collective-permute-start.6) | collective-permute-done | bytes 81952 | tf_op jit(solution)/shard_map/ppermute | solution.py:21
  53.7 7.5 %collective-permute-start.8 = (bf16[10,2,20,128]{3,2,1,0:T(8,128)(2,1)S(1)}, bf16[10,2,20,128]{3,2,1,0:T(8,128)(2,1)S(1)}, u32[]{:S(2)}, u32[]{:S(2)}) collective-permute-start(bf16[10,2,20,128]{3,2,1,0:T(8,128)(2,1)S(1)} %get-tuple-element.156), channel_id=1, source_target_pairs={{0,4},{1,5},{2,6},{3,7},{4,8},{5,9},{6,10},{7,11},{8,12},{9,13},{1... | collective-permute-start | bytes 307208 | tf_op jit(solution)/shard_map/ppermute | solution.py:21
  63.6 7.7 %collective-permute-done.9 = bf16[10,2,20,128]{3,2,1,0:T(8,128)(2,1)S(1)} collective-permute-done((bf16[10,2,20,128]{3,2,1,0:T(8,128)(2,1)S(1)}, bf16[10,2,20,128]{3,2,1,0:T(8,128)(2,1)S(1)}, u32[]{:S(2)}, u32[]{:S(2)}) %collective-permute-start.9) | collective-permute-done | bytes 102432 | tf_op jit(solution)/shard_map/ppermute | solution.py:21
  72.8 150.7 %while.14 = (s32[]{:T(128)}, f32[8,2,8,256]{3,2,1,0:T(8,128)}, bf16[8,256,128]{2,1,0:T(8,128)(2,1)S(1)}, s32[8]{0:T(128)}, bf16[10,400,128]{2,1,0:T(8,128)(2,1)S...) while((s32[]{:T(128)}, f32[8,2,8,256]{3,2,1,0:T(8,128)}, ...), condition=%wide.region_1.3_spmd, body=%wide.region_0.2_spmd.sunk | while | flops 1617931 | bytes 6136589 | solution.py:76
  76.7 6.2 %gather_fusion.1 = bf16[2048,128]{1,0:T(8,128)(2,1)S(1)} fusion(bf16[400,128]{1,0:T(8,128)(2,1)S(1)} %get-tuple-element.232, s32[2048]{0:T(1024)S(1)} %broadcast_clamp_fusion.5), kind=kCustom, calls=%fused_computation.clone.clone.1 | custom fusion | bytes 1056768 | tf_op jit(solution)/shard_map/while/body/eval_jaxpr/jit(_take)/gather | solution.py:70
  82.9 6.2 %gather_fusion = bf16[2048,128]{1,0:T(8,128)(2,1)S(1)} fusion(bf16[400,128]{1,0:T(8,128)(2,1)S(1)} %get-tuple-element.229, s32[2048]{0:T(1024)S(1)} %broadcast_clamp_fusion.4), kind=kCustom, calls=%fused_computation.1.clone.clone.1 | custom fusion | bytes 1056768 | tf_op jit(solution)/shard_map/while/body/eval_jaxpr/jit(_take)/gather | solution.py:70
  95.5 6.2 %gather_fusion.1 = bf16[2048,128]{1,0:T(8,128)(2,1)S(1)} fusion(bf16[400,128]{1,0:T(8,128)(2,1)S(1)} %get-tuple-element.232, s32[2048]{0:T(1024)S(1)} %broadcast_clamp_fusion.5), kind=kCustom, calls=%fused_computation.clone.clone.1 | custom fusion | bytes 1056768 | tf_op jit(solution)/shard_map/while/body/eval_jaxpr/jit(_take)/gather | solution.py:70
  101.8 6.2 %gather_fusion = bf16[2048,128]{1,0:T(8,128)(2,1)S(1)} fusion(bf16[400,128]{1,0:T(8,128)(2,1)S(1)} %get-tuple-element.229, s32[2048]{0:T(1024)S(1)} %broadcast_clamp_fusion.4), kind=kCustom, calls=%fused_computation.1.clone.clone.1 | custom fusion | bytes 1056768 | tf_op jit(solution)/shard_map/while/body/eval_jaxpr/jit(_take)/gather | solution.py:70
  114.4 6.2 %gather_fusion.1 = bf16[2048,128]{1,0:T(8,128)(2,1)S(1)} fusion(bf16[400,128]{1,0:T(8,128)(2,1)S(1)} %get-tuple-element.232, s32[2048]{0:T(1024)S(1)} %broadcast_clamp_fusion.5), kind=kCustom, calls=%fused_computation.clone.clone.1 | custom fusion | bytes 1056768 | tf_op jit(solution)/shard_map/while/body/eval_jaxpr/jit(_take)/gather | solution.py:70
  120.6 6.2 %gather_fusion = bf16[2048,128]{1,0:T(8,128)(2,1)S(1)} fusion(bf16[400,128]{1,0:T(8,128)(2,1)S(1)} %get-tuple-element.229, s32[2048]{0:T(1024)S(1)} %broadcast_clamp_fusion.4), kind=kCustom, calls=%fused_computation.1.clone.clone.1 | custom fusion | bytes 1056768 | tf_op jit(solution)/shard_map/while/body/eval_jaxpr/jit(_take)/gather | solution.py:70
  133.2 6.2 %gather_fusion.1 = bf16[2048,128]{1,0:T(8,128)(2,1)S(1)} fusion(bf16[400,128]{1,0:T(8,128)(2,1)S(1)} %get-tuple-element.232, s32[2048]{0:T(1024)S(1)} %broadcast_clamp_fusion.5), kind=kCustom, calls=%fused_computation.clone.clone.1 | custom fusion | bytes 1056768 | tf_op jit(solution)/shard_map/while/body/eval_jaxpr/jit(_take)/gather | solution.py:70
  139.4 6.2 %gather_fusion = bf16[2048,128]{1,0:T(8,128)(2,1)S(1)} fusion(bf16[400,128]{1,0:T(8,128)(2,1)S(1)} %get-tuple-element.229, s32[2048]{0:T(1024)S(1)} %broadcast_clamp_fusion.4), kind=kCustom, calls=%fused_computation.1.clone.clone.1 | custom fusion | bytes 1056768 | tf_op jit(solution)/shard_map/while/body/eval_jaxpr/jit(_take)/gather | solution.py:70
  152.0 6.2 %gather_fusion.1 = bf16[2048,128]{1,0:T(8,128)(2,1)S(1)} fusion(bf16[400,128]{1,0:T(8,128)(2,1)S(1)} %get-tuple-element.232, s32[2048]{0:T(1024)S(1)} %broadcast_clamp_fusion.5), kind=kCustom, calls=%fused_computation.clone.clone.1 | custom fusion | bytes 1056768 | tf_op jit(solution)/shard_map/while/body/eval_jaxpr/jit(_take)/gather | solution.py:70
  158.3 6.2 %gather_fusion = bf16[2048,128]{1,0:T(8,128)(2,1)S(1)} fusion(bf16[400,128]{1,0:T(8,128)(2,1)S(1)} %get-tuple-element.229, s32[2048]{0:T(1024)S(1)} %broadcast_clamp_fusion.4), kind=kCustom, calls=%fused_computation.1.clone.clone.1 | custom fusion | bytes 1056768 | tf_op jit(solution)/shard_map/while/body/eval_jaxpr/jit(_take)/gather | solution.py:70
  170.9 6.2 %gather_fusion.1 = bf16[2048,128]{1,0:T(8,128)(2,1)S(1)} fusion(bf16[400,128]{1,0:T(8,128)(2,1)S(1)} %get-tuple-element.232, s32[2048]{0:T(1024)S(1)} %broadcast_clamp_fusion.5), kind=kCustom, calls=%fused_computation.clone.clone.1 | custom fusion | bytes 1056768 | tf_op jit(solution)/shard_map/while/body/eval_jaxpr/jit(_take)/gather | solution.py:70
  177.1 6.2 %gather_fusion = bf16[2048,128]{1,0:T(8,128)(2,1)S(1)} fusion(bf16[400,128]{1,0:T(8,128)(2,1)S(1)} %get-tuple-element.229, s32[2048]{0:T(1024)S(1)} %broadcast_clamp_fusion.4), kind=kCustom, calls=%fused_computation.1.clone.clone.1 | custom fusion | bytes 1056768 | tf_op jit(solution)/shard_map/while/body/eval_jaxpr/jit(_take)/gather | solution.py:70
  189.7 6.2 %gather_fusion.1 = bf16[2048,128]{1,0:T(8,128)(2,1)S(1)} fusion(bf16[400,128]{1,0:T(8,128)(2,1)S(1)} %get-tuple-element.232, s32[2048]{0:T(1024)S(1)} %broadcast_clamp_fusion.5), kind=kCustom, calls=%fused_computation.clone.clone.1 | custom fusion | bytes 1056768 | tf_op jit(solution)/shard_map/while/body/eval_jaxpr/jit(_take)/gather | solution.py:70
  195.9 6.2 %gather_fusion = bf16[2048,128]{1,0:T(8,128)(2,1)S(1)} fusion(bf16[400,128]{1,0:T(8,128)(2,1)S(1)} %get-tuple-element.229, s32[2048]{0:T(1024)S(1)} %broadcast_clamp_fusion.4), kind=kCustom, calls=%fused_computation.1.clone.clone.1 | custom fusion | bytes 1056768 | tf_op jit(solution)/shard_map/while/body/eval_jaxpr/jit(_take)/gather | solution.py:70
  208.5 6.2 %gather_fusion.1 = bf16[2048,128]{1,0:T(8,128)(2,1)S(1)} fusion(bf16[400,128]{1,0:T(8,128)(2,1)S(1)} %get-tuple-element.232, s32[2048]{0:T(1024)S(1)} %broadcast_clamp_fusion.5), kind=kCustom, calls=%fused_computation.clone.clone.1 | custom fusion | bytes 1056768 | tf_op jit(solution)/shard_map/while/body/eval_jaxpr/jit(_take)/gather | solution.py:70
  214.8 6.2 %gather_fusion = bf16[2048,128]{1,0:T(8,128)(2,1)S(1)} fusion(bf16[400,128]{1,0:T(8,128)(2,1)S(1)} %get-tuple-element.229, s32[2048]{0:T(1024)S(1)} %broadcast_clamp_fusion.4), kind=kCustom, calls=%fused_computation.1.clone.clone.1 | custom fusion | bytes 1056768 | tf_op jit(solution)/shard_map/while/body/eval_jaxpr/jit(_take)/gather | solution.py:70
  228.8 3.2 %collective-permute-done.12 = f32[2,2,2,256]{3,0,2,1:T(2,128)S(1)} collective-permute-done((f32[2,2,2,256]{3,0,2,1:T(2,128)S(1)}, f32[2,2,2,256]{3,0,2,1:T(2,128)S(1)}, u32[]{:S(2)}, u32[]{:S(2)}) %collective-permute-start.12) | collective-permute-done | bytes 8224 | tf_op jit(solution)/shard_map/ppermute | solution.py:21
  235.6 3.9 %collective-permute-start.13 = (f32[8,2,16,1]{3,2,0,1:T(8,128)S(1)}, f32[8,2,16,1]{3,2,0,1:T(8,128)S(1)}, u32[]{:S(2)}, u32[]{:S(2)}) collective-permute-start(f32[8,2,16,1]{3,2,0,1:T(8,128)S(1)} %get-tuple-element.165), channel_id=1, source_target_pairs={{0,1},{1,2},{2,3},{3,4},{4,5},{5,6},{6,7},{7,8},{8,9},{9,10},{10,1... | collective-permute-start | bytes 3080 | tf_op jit(solution)/shard_map/ppermute | solution.py:21
  240.0 5.5 %collective-permute-done.13 = f32[8,2,16,1]{3,2,0,1:T(8,128)S(1)} collective-permute-done((f32[8,2,16,1]{3,2,0,1:T(8,128)S(1)}, f32[8,2,16,1]{3,2,0,1:T(8,128)S(1)}, u32[]{:S(2)}, u32[]{:S(2)}) %collective-permute-start.13) | collective-permute-done | bytes 1056 | tf_op jit(solution)/shard_map/ppermute | solution.py:21
  247.6 6.0 %collective-permute-start.16 = (f32[8,2,1,18]{3,2,0,1:T(1,128)S(1)}, f32[8,2,1,18]{3,2,0,1:T(1,128)S(1)}, u32[]{:S(2)}, u32[]{:S(2)}) collective-permute-start(f32[8,2,1,18]{3,2,0,1:T(1,128)S(1)} %get-tuple-element.161), channel_id=1, source_target_pairs={{0,4},{1,5},{2,6},{3,7},{4,8},{5,9},{6,10},{7,11},{8,12},{9,13},{1... | collective-permute-start | bytes 3464 | tf_op jit(solution)/shard_map/ppermute | solution.py:21
  253.6 2.7 %collective-permute-start.17 = (f32[2,2,256]{2,0,1:T(2,128)S(1)}, f32[2,2,256]{2,0,1:T(2,128)S(1)}, u32[]{:S(2)}, u32[]{:S(2)}) collective-permute-start(f32[2,2,256]{2,0,1:T(2,128)S(1)} %get-tuple-element.168), channel_id=1, source_target_pairs={{16,0},{32,16},{48,32},{64,48},{80,64},{96,80},{112,96},{128,112},... | collective-permute-start | bytes 12296 | tf_op jit(solution)/shard_map/ppermute | solution.py:34
  258.8 3.4 %collective-permute-done.18 = f32[2,2,256]{2,0,1:T(2,128)S(1)} collective-permute-done((f32[2,2,256]{2,0,1:T(2,128)S(1)}, f32[2,2,256]{2,0,1:T(2,128)S(1)}, u32[]{:S(2)}, u32[]{:S(2)}) %collective-permute-start.18) | collective-permute-done | bytes 4128 | tf_op jit(solution)/shard_map/ppermute | solution.py:32
  (221 shorter events, 65.9 us)
Async XLA Ops:
  0.6 22.3 %copy-start.2 = (s32[8,2,8,256]{3,2,1,0:T(8,128)S(1)}, s32[8,2,8,256]{3,2,1,0:T(8,128)}, u32[]{:S(2)}) copy-start(s32[8,2,8,256]{3,2,1,0:T(8,128)} %param.10) | copy-start | bytes 393220
  0.6 23.4 %copy-start.1 = (s32[8,2,2,8,256]{4,3,2,1,0:T(8,128)S(1)}, s32[8,2,2,8,256]{4,3,2,1,0:T(8,128)}, u32[]{:S(2)}) copy-start(s32[8,2,2,8,256]{4,3,2,1,0:T(8,128)} %param.11) | copy-start | bytes 786436
  1.6 25.8 %collective-permute-start.5 = (bf16[2,256,128]{2,1,0:T(8,128)(2,1)S(1)}, bf16[2,256,128]{2,1,0:T(8,128)(2,1)S(1)}, u32[]{:S(2)}, u32[]{:S(2)}) collective-permute-start(bf16[2,256,128]{2,1,0:T(8,128)(2,1)S(1)} %slice.190), channel_id=1, source_target_pairs={{16,0},{32,16},{48,32},{64,48},{80,64},{96,80},{112,96},{128,112},... | collective-permute-start | bytes 393224 | tf_op jit(solution)/shard_map/ppermute | solution.py:21
  5.9 21.5 %copy-start = (bf16[8,256,128]{2,1,0:T(8,128)(2,1)S(1)}, bf16[8,256,128]{2,1,0:T(8,128)(2,1)}, u32[]{:S(2)}) copy-start(bf16[8,256,128]{2,1,0:T(8,128)(2,1)} %param.9) | copy-start | bytes 1572868
  6.0 21.4 %collective-permute-start.1 = (f32[8,2,16,1]{3,2,0,1:T(8,128)S(1)}, f32[8,2,16,1]{3,2,0,1:T(8,128)S(1)}, u32[]{:S(2)}, u32[]{:S(2)}) collective-permute-start(f32[8,2,16,1]{3,2,0,1:T(8,128)S(1)} %get-tuple-element.166), channel_id=1, source_target_pairs={{1,0},{2,1},{3,2},{4,3},{5,4},{6,5},{7,6},{8,7},{9,8},{10,9},{11,1... | collective-permute-start | bytes 3080 | tf_op jit(solution)/shard_map/ppermute | solution.py:21
  9.9 17.5 %collective-permute-start = (f32[8,2,16,1]{3,2,0,1:T(8,128)S(1)}, f32[8,2,16,1]{3,2,0,1:T(8,128)S(1)}, u32[]{:S(2)}, u32[]{:S(2)}) collective-permute-start(f32[8,2,16,1]{3,2,0,1:T(8,128)S(1)} %get-tuple-element.167), channel_id=1, source_target_pairs={{0,1},{1,2},{2,3},{3,4},{4,5},{5,6},{6,7},{7,8},{8,9},{9,10},{10,1... | collective-permute-start | bytes 3080 | tf_op jit(solution)/shard_map/ppermute | solution.py:21
  12.8 11.9 %collective-permute-start.10 = (f32[2,2]{0,1:T(2,128)S(1)}, f32[2,2]{0,1:T(2,128)S(1)}, u32[]{:S(2)}, u32[]{:S(2)}) collective-permute-start(f32[2,2]{0,1:T(2,128)S(1)} %slice.198), channel_id=1, source_target_pairs={{0,16},{16,32},{32,48},{48,64},{64,80},{80,96},{96,112},{112,128},... | collective-permute-start | bytes 56 | tf_op jit(solution)/shard_map/ppermute | solution.py:21
  16.0 212.1 %collective-permute-start.4 = (f32[2,2,256]{2,0,1:T(2,128)}, f32[2,2,256]{2,0,1:T(2,128)}, u32[]{:S(2)}, u32[]{:S(2)}) collective-permute-start(f32[2,2,256]{2,0,1:T(2,128)} %get-tuple-element.170), channel_id=1, source_target_pairs={{16,0},{32,16},{48,32},{64,48},{80,64},{96,80},{112,96},{128,112},... | collective-permute-start | bytes 12296 | tf_op jit(solution)/shard_map/ppermute | solution.py:34
  22.9 40.2 %copy-start.6 = (pred[16]{0:T(512)(128)(4,1)}, pred[16]{0:T(512)(128)(4,1)S(1)}, u32[]{:S(2)}) copy-start(pred[16]{0:T(512)(128)(4,1)S(1)} %get-tuple-element.180) | copy-start | bytes 52
  22.9 40.2 %copy-start.8 = (pred[16]{0:T(512)(128)(4,1)}, pred[16]{0:T(512)(128)(4,1)S(1)}, u32[]{:S(2)}) copy-start(pred[16]{0:T(512)(128)(4,1)S(1)} %get-tuple-element.181) | copy-start | bytes 52
  22.9 40.2 %copy-start.10 = (pred[16]{0:T(512)(128)(4,1)}, pred[16]{0:T(512)(128)(4,1)S(1)}, u32[]{:S(2)}) copy-start(pred[16]{0:T(512)(128)(4,1)S(1)} %get-tuple-element.178) | copy-start | bytes 52
  22.9 40.2 %copy-start.12 = (pred[16]{0:T(512)(128)(4,1)}, pred[16]{0:T(512)(128)(4,1)S(1)}, u32[]{:S(2)}) copy-start(pred[16]{0:T(512)(128)(4,1)S(1)} %get-tuple-element.179) | copy-start | bytes 52
  24.7 204.1 %collective-permute-start.11 = (f32[2,2,256]{2,0,1:T(2,128)}, f32[2,2,256]{2,0,1:T(2,128)}, u32[]{:S(2)}, u32[]{:S(2)}) collective-permute-start(f32[2,2,256]{2,0,1:T(2,128)} %get-tuple-element.171), channel_id=1, source_target_pairs={{0,16},{16,32},{32,48},{48,64},{64,80},{80,96},{96,112},{112,128},... | collective-permute-start | bytes 12296 | tf_op jit(solution)/shard_map/ppermute | solution.py:32
  27.7 16.5 %collective-permute-start.7 = (bf16[10,16,2,128]{3,2,1,0:T(2,128)(2,1)S(1)}, bf16[10,16,2,128]{3,2,1,0:T(2,128)(2,1)S(1)}, u32[]{:S(2)}, u32[]{:S(2)}) collective-permute-start(bf16[10,16,2,128]{3,2,1,0:T(2,128)(2,1)S(1)} %get-tuple-element.159), channel_id=1, source_target_pairs={{1,0},{2,1},{3,2},{4,3},{5,4},{6,5},{7,6},{8,7},{9,8},{10,9},{11,1... | collective-permute-start | bytes 245768 | tf_op jit(solution)/shard_map/ppermute | solution.py:21
  34.6 26.6 %collective-permute-start.2 = (f32[8,2,1,18]{3,2,0,1:T(1,128)S(1)}, f32[8,2,1,18]{3,2,0,1:T(1,128)S(1)}, u32[]{:S(2)}, u32[]{:S(2)}) collective-permute-start(f32[8,2,1,18]{3,2,0,1:T(1,128)S(1)} %get-tuple-element.162), channel_id=1, source_target_pairs={{4,0},{5,1},{6,2},{7,3},{8,4},{9,5},{10,6},{11,7},{12,8},{13,9},{1... | collective-permute-start | bytes 3464 | tf_op jit(solution)/shard_map/ppermute | solution.py:21
  36.5 26.6 %collective-permute-start.3 = (f32[8,2,1,18]{3,2,0,1:T(1,128)S(1)}, f32[8,2,1,18]{3,2,0,1:T(1,128)S(1)}, u32[]{:S(2)}, u32[]{:S(2)}) collective-permute-start(f32[8,2,1,18]{3,2,0,1:T(1,128)S(1)} %get-tuple-element.163), channel_id=1, source_target_pairs={{0,4},{1,5},{2,6},{3,7},{4,8},{5,9},{6,10},{7,11},{8,12},{9,13},{1... | collective-permute-start | bytes 3464 | tf_op jit(solution)/shard_map/ppermute | solution.py:21
  44.1 9.3 %collective-permute-start.6 = (bf16[10,16,2,128]{3,2,1,0:T(2,128)(2,1)S(1)}, bf16[10,16,2,128]{3,2,1,0:T(2,128)(2,1)S(1)}, u32[]{:S(2)}, u32[]{:S(2)}) collective-permute-start(bf16[10,16,2,128]{3,2,1,0:T(2,128)(2,1)S(1)} %get-tuple-element.158), channel_id=1, source_target_pairs={{0,1},{1,2},{2,3},{3,4},{4,5},{5,6},{6,7},{7,8},{8,9},{9,10},{10,1... | collective-permute-start | bytes 245768 | tf_op jit(solution)/shard_map/ppermute | solution.py:21
  53.7 9.9 %collective-permute-start.8 = (bf16[10,2,20,128]{3,2,1,0:T(8,128)(2,1)S(1)}, bf16[10,2,20,128]{3,2,1,0:T(8,128)(2,1)S(1)}, u32[]{:S(2)}, u32[]{:S(2)}) collective-permute-start(bf16[10,2,20,128]{3,2,1,0:T(8,128)(2,1)S(1)} %get-tuple-element.156), channel_id=1, source_target_pairs={{0,4},{1,5},{2,6},{3,7},{4,8},{5,9},{6,10},{7,11},{8,12},{9,13},{1... | collective-permute-start | bytes 307208 | tf_op jit(solution)/shard_map/ppermute | solution.py:21
  61.2 10.2 %collective-permute-start.9 = (bf16[10,2,20,128]{3,2,1,0:T(8,128)(2,1)S(1)}, bf16[10,2,20,128]{3,2,1,0:T(8,128)(2,1)S(1)}, u32[]{:S(2)}, u32[]{:S(2)}) collective-permute-start(bf16[10,2,20,128]{3,2,1,0:T(8,128)(2,1)S(1)} %get-tuple-element.157), channel_id=1, source_target_pairs={{4,0},{5,1},{6,2},{7,3},{8,4},{9,5},{10,6},{11,7},{12,8},{13,9},{1... | collective-permute-start | bytes 307208 | tf_op jit(solution)/shard_map/ppermute | solution.py:21
  223.4 8.6 %copy-start.4 = (f32[8]{0:T(128)S(1)}, f32[8]{0:T(128)}, u32[]{:S(2)}) copy-start(f32[8]{0:T(128)} %get-tuple-element.176) | copy-start | bytes 100
  223.4 8.6 %copy-start.5 = (f32[8]{0:T(128)S(1)}, f32[8]{0:T(128)}, u32[]{:S(2)}) copy-start(f32[8]{0:T(128)} %get-tuple-element.177) | copy-start | bytes 100
  224.7 33.5 %copy-start.7 = (pred[16]{0:T(512)(128)(4,1)S(1)}, pred[16]{0:T(512)(128)(4,1)}, u32[]{:S(2)}) copy-start(pred[16]{0:T(512)(128)(4,1)} %copy-done.6) | copy-start | bytes 52
  224.7 33.5 %copy-start.9 = (pred[16]{0:T(512)(128)(4,1)S(1)}, pred[16]{0:T(512)(128)(4,1)}, u32[]{:S(2)}) copy-start(pred[16]{0:T(512)(128)(4,1)} %copy-done.8) | copy-start | bytes 52
  224.7 33.5 %copy-start.11 = (pred[16]{0:T(512)(128)(4,1)S(1)}, pred[16]{0:T(512)(128)(4,1)}, u32[]{:S(2)}) copy-start(pred[16]{0:T(512)(128)(4,1)} %copy-done.10) | copy-start | bytes 52
  224.8 33.5 %copy-start.13 = (pred[16]{0:T(512)(128)(4,1)S(1)}, pred[16]{0:T(512)(128)(4,1)}, u32[]{:S(2)}) copy-start(pred[16]{0:T(512)(128)(4,1)} %copy-done.12) | copy-start | bytes 52
  226.2 5.9 %collective-permute-start.12 = (f32[2,2,2,256]{3,0,2,1:T(2,128)S(1)}, f32[2,2,2,256]{3,0,2,1:T(2,128)S(1)}, u32[]{:S(2)}, u32[]{:S(2)}) collective-permute-start(f32[2,2,2,256]{3,0,2,1:T(2,128)S(1)} %slice.240), channel_id=1, source_target_pairs={{0,16},{16,32},{32,48},{48,64},{64,80},{80,96},{96,112},{112,128},... | collective-permute-start | bytes 24584 | tf_op jit(solution)/shard_map/ppermute | solution.py:21
  233.1 6.9 %collective-permute-start.14 = (f32[8,2,16,1]{3,2,0,1:T(8,128)S(1)}, f32[8,2,16,1]{3,2,0,1:T(8,128)S(1)}, u32[]{:S(2)}, u32[]{:S(2)}) collective-permute-start(f32[8,2,16,1]{3,2,0,1:T(8,128)S(1)} %get-tuple-element.164), channel_id=1, source_target_pairs={{1,0},{2,1},{3,2},{4,3},{5,4},{6,5},{7,6},{8,7},{9,8},{10,9},{11,1... | collective-permute-start | bytes 3080 | tf_op jit(solution)/shard_map/ppermute | solution.py:21
  235.6 9.9 %collective-permute-start.13 = (f32[8,2,16,1]{3,2,0,1:T(8,128)S(1)}, f32[8,2,16,1]{3,2,0,1:T(8,128)S(1)}, u32[]{:S(2)}, u32[]{:S(2)}) collective-permute-start(f32[8,2,16,1]{3,2,0,1:T(8,128)S(1)} %get-tuple-element.165), channel_id=1, source_target_pairs={{0,1},{1,2},{2,3},{3,4},{4,5},{5,6},{6,7},{7,8},{8,9},{9,10},{10,1... | collective-permute-start | bytes 3080 | tf_op jit(solution)/shard_map/ppermute | solution.py:21
  245.7 12.6 %collective-permute-start.15 = (f32[8,2,1,18]{3,2,0,1:T(1,128)S(1)}, f32[8,2,1,18]{3,2,0,1:T(1,128)S(1)}, u32[]{:S(2)}, u32[]{:S(2)}) collective-permute-start(f32[8,2,1,18]{3,2,0,1:T(1,128)S(1)} %get-tuple-element.160), channel_id=1, source_target_pairs={{4,0},{5,1},{6,2},{7,3},{8,4},{9,5},{10,6},{11,7},{12,8},{13,9},{1... | collective-permute-start | bytes 3464 | tf_op jit(solution)/shard_map/ppermute | solution.py:21
  247.6 10.7 %collective-permute-start.16 = (f32[8,2,1,18]{3,2,0,1:T(1,128)S(1)}, f32[8,2,1,18]{3,2,0,1:T(1,128)S(1)}, u32[]{:S(2)}, u32[]{:S(2)}) collective-permute-start(f32[8,2,1,18]{3,2,0,1:T(1,128)S(1)} %get-tuple-element.161), channel_id=1, source_target_pairs={{0,4},{1,5},{2,6},{3,7},{4,8},{5,9},{6,10},{7,11},{8,12},{9,13},{1... | collective-permute-start | bytes 3464 | tf_op jit(solution)/shard_map/ppermute | solution.py:21
  253.6 5.1 %collective-permute-start.17 = (f32[2,2,256]{2,0,1:T(2,128)S(1)}, f32[2,2,256]{2,0,1:T(2,128)S(1)}, u32[]{:S(2)}, u32[]{:S(2)}) collective-permute-start(f32[2,2,256]{2,0,1:T(2,128)S(1)} %get-tuple-element.168), channel_id=1, source_target_pairs={{16,0},{32,16},{48,32},{64,48},{80,64},{96,80},{112,96},{128,112},... | collective-permute-start | bytes 12296 | tf_op jit(solution)/shard_map/ppermute | solution.py:34
  256.3 5.8 %collective-permute-start.18 = (f32[2,2,256]{2,0,1:T(2,128)S(1)}, f32[2,2,256]{2,0,1:T(2,128)S(1)}, u32[]{:S(2)}, u32[]{:S(2)}) collective-permute-start(f32[2,2,256]{2,0,1:T(2,128)S(1)} %get-tuple-element.169), channel_id=1, source_target_pairs={{0,16},{16,32},{32,48},{48,64},{64,80},{80,96},{96,112},{112,128},... | collective-permute-start | bytes 12296 | tf_op jit(solution)/shard_map/ppermute | solution.py:32
  (1 other events, 8.6 us)
where the time goes:
time: 264 us; the launch traced here: 263 us
  local copies, waits for them, and re-layouts  119 us (45%)
  starting transfers between devices  65.6 us (25%)
  waiting for transfers between devices  27.6 us (10%)
  loops' own time  21.2 us (8%)
  other arithmetic  20.8 us (8%)
  matrix products  7.53 us (3%)
    gather x16, local copies, waits for them, and re-layouts, per_section(): picked = jnp.take(other, rows_index[zed], axis=0)  98.9 us
    ppermute x15, starting transfers between devices, shifted_2(): return lax.ppermute(block, axis, route)  54.6 us
    ppermute x15, waiting for transfers between devices, shifted_2(): return lax.ppermute(block, axis, route)  24.2 us
    another operation x1, loops' own time, score_rows(): lax.map(per_section, (jnp.arange(own.shape[0], dtype=jnp.int32), own, ind...  21.2 us
    dynamic_slice x8, local copies, waits for them, and re-layouts, score_rows(): lax.map(per_section, (jnp.arange(own.shape[0], dtype=jnp.int32), own, ind...  10.5 us
    dot_general x16, matrix products, per_section(): jnp.einsum('kvp,vp->kv', picked, mine, preferred_element_type=jnp.float32)  7.53 us
    ppermute x2, starting transfers between devices, extended_2(): lax.ppermute(head, axis, [((i + 1) % count, i) for i in range(ends)])  7.18 us
    select_n x8, other arithmetic, per_section(): picked = jnp.take(other, rows_index[zed], axis=0)  5.73 us
  transfers between devices with their start and end apart: 19, of which 6 were waited for; matrix products, arithmetic and copies ran while one was open for 55% of the time, Pallas kernels for 0%

commit v1 on v0

v1 whole, which is shorter than its diff:
```python
import jax
import jax.numpy as jnp
from jax import lax
from jax.experimental import pallas as pl
from jax.experimental.pallas import tpu as pltpu
from jax.sharding import PartitionSpec as P

SIDE = 16
COLS = 4
PATCH = 128
VT = 256
HALF = 128
SEC = 8
PITCH = 128.0
STEP = 0.1
BF = jnp.bfloat16
F32 = jnp.float32
I32 = jnp.int32

X_ROWS = 8 * 32 + 64
R_ROWS = 8 * 32 + 64 + 32
S_ROWS = 816
CROSS = ((6, 1), (7, 0), (7, 1))


def swapped(block, axis, partner):
    return lax.ppermute(block, axis, [(i, partner(i)) for i in range(lax.axis_size(axis))])


def col_a(i):
    return i ^ 1


def col_b(i):
    return i // COLS * COLS + (COLS - 1 - i % COLS)


def row_a(i):
    return i ^ COLS


def row_b(i):
    return (COLS - 1 - i // COLS) * COLS + i % COLS


def stack_a(i):
    return i ^ 1


def stack_b(i):
    return (((i + 1) ^ 1) - 1) % 16


def tile_place():
    tile = lax.axis_index("tile").astype(I32)
    return tile // COLS, tile % COLS


def iota(shape, dim):
    return lax.broadcasted_iota(I32, shape, dim)


def two_parts(u):
    hi = u.astype(BF)
    return hi, (u - hi.astype(F32)).astype(BF)


def rows_of(start_ref, scr, first=0):
    for s in range(SEC):
        scr[first + 2 * s : first + 2 * s + 2, :] = start_ref[s]


def dot(a, b):
    return lax.dot_general(a, b, (((1,), (0,)), ((), ())), preferred_element_type=F32)


def dot_t(a, b):
    return lax.dot_general(a, b, (((1,), (1,)), ((), ())), preferred_element_type=F32)


def pack_cols(patches, start, xa, xb, scr):
    _, col = tile_place()
    off_a = jnp.where(col % 2 == 0, SIDE - 2, 0)
    j = iota((64, VT), 0)
    v = iota((64, VT), 1)
    off = jnp.where(j < 32, off_a, SIDE - 2 - off_a)
    source = (j % SIDE) * SIDE + off + (j % 32) // SIDE
    pick = (v == source).astype(BF)
    for s in range(SEC):
        strips = dot(pick, patches[s]).astype(BF)
        xa[s * 32 : s * 32 + 32, :] = strips[:32]
        xb[s * 32 : s * 32 + 32, :] = strips[32:]
    rows_of(start, scr)
    hi, lo = two_parts(scr[...])
    for n, part in enumerate((hi[:, :HALF], hi[:, HALF:], lo[:, :HALF], lo[:, HALF:])):
        xa[256 + 16 * n : 272 + 16 * n, :] = part
        xb[256 + 16 * n : 272 + 16 * n, :] = part


def pack_rows(patches, start, xa, xb, ra, rb, scr):
    row, col = tile_place()
    off_a = jnp.where(row % 2 == 0, SIDE - 2, 0)
    off_b = SIDE - 2 - off_a
    for out, off in ((ra, off_a), (rb, off_b)):
        first = pl.multiple_of(off * SIDE, 32)
        for s in range(SEC):
            out[s * 32 : s * 32 + 32, :] = patches[s, pl.ds(first, 32), :]
    both = jnp.concatenate([xa[0:256, :], xb[0:256, :]], axis=0)
    q = iota((128, 512), 0)
    k = iota((128, 512), 1)
    off = jnp.where(q < 64, off_a, off_b)
    side = (q % 8) // 4
    buffer = jnp.where(col % 2 == 0, 1 - side, side)
    source = buffer * 256 + (q % 64) // 8 * 32 + (q % 4) // 2 * SIDE + off + q % 2
    corners = dot((k == source).astype(BF), both).astype(BF)
    ra[256:320, :] = corners[:64]
    rb[256:320, :] = corners[64:]
    rows_of(start, scr)
    hi, lo = two_parts(scr[...])
    even = row % 2 == 0
    for out, second in ((ra, even), (rb, jnp.logical_not(even))):

        @pl.when(second)
        def _():
            out[320:336, :] = hi[:, HALF:]
            out[336:352, :] = lo[:, HALF:]

        @pl.when(jnp.logical_not(second))
        def _():
            out[320:336, :] = hi[:, :HALF]
            out[336:352, :] = lo[:, :HALF]


def local_place(ids, row, col):
    tile = ids >> 8
    lr = (tile >> 2) * SIDE + ((ids >> 4) & 15) - row * SIDE
    lc = (tile & 3) * SIDE + (ids & 15) - col * SIDE
    return lr, lc


def pack_stack(patches, cand, offs, pairs, start, xa, xb, ra, rb, sa, sb, scr):
    row, col = tile_place()
    col_even = col % 2 == 0
    row_even = row % 2 == 0
    stack_even = lax.axis_index("stack") % 2 == 0
    rows_of(start, scr)
    hi, lo = two_parts(scr[...])

    def down(out):
        for s in range(2):
            out[s * 256 : s * 256 + 256, :] = patches[s]
        for even, left, right in ((True, xb, xa), (False, xa, xb)):

            @pl.when(col_even == even)
            def _():
                for s in range(2):
                    out[512 + 64 * s : 544 + 64 * s, :] = left[32 * s : 32 * s + 32, :]
                    out[544 + 64 * s : 576 + 64 * s, :] = right[32 * s : 32 * s + 32, :]

        for even, above, below in ((True, rb, ra), (False, ra, rb)):

            @pl.when(row_even == even)
            def _():
                for s in range(2):
                    out[640 + 64 * s : 672 + 64 * s, :] = above[32 * s : 32 * s + 32, :]
                    out[672 + 64 * s : 704 + 64 * s, :] = below[32 * s : 32 * s + 32, :]
                out[768:784, :] = above[256:272, :]
                out[784:800, :] = below[256:272, :]

        ends(out, 0)

    def up(out):
        for s in range(2):
            out[s * 256 : s * 256 + 256, :] = patches[6 + s]
        for p, (s, z) in enumerate(CROSS):
            lr, lc = local_place(cand[s, z], row, col)
            for n, plane in enumerate((lr, lc, offs[s, z, 0], offs[s, z, 1])):
                at = 512 + 64 * p + 16 * n
                plane = plane.astype(F32)
                out[at : at + 16, :] = jnp.concatenate([plane[:, :HALF], plane[:, HALF:]], axis=0).astype(BF)
        r = iota((16, HALF), 0)
        tied = jnp.zeros((16, HALF), F32)
        for p, (s, z) in enumerate(CROSS):
            tied = jnp.where(r == p, pairs[s, z].astype(F32), tied)
        out[704:720, :] = tied.astype(BF)
        out[720:800, :] = jnp.zeros((80, HALF), BF)
        ends(out, 12)

    def ends(out, first):
        u = scr[first : first + 4, :]
        h, low = two_parts(u)
        h, low = h.astype(F32), low.astype(F32)
        out[800:816, :] = jnp.concatenate(
            [h[:, :HALF], h[:, HALF:], low[:, :HALF], low[:, HALF:]], axis=0
        ).astype(BF)

    @pl.when(stack_even)
    def _():
        up(sa)
        down(sb)

    @pl.when(jnp.logical_not(stack_even))
    def _():
        up(sb)
        down(sa)


def half_targets(h, mine, pieces, corner, lr, lc, off_r, off_c):
    own, left, right, above, below = pieces
    own = own[0:160] if h == 0 else own[96:256]
    centre = [above, own] if h == 0 else [own, below]
    table = jnp.concatenate(centre + [left, right, corner[0]], axis=0)
    scores = dot_t(table, mine)
    first = corner[1]
    i = lr + 2 if h == 0 else lr - 6
    outside_c = (lc < 0) | (lc >= SIDE)
    outside_r = (lr < 0) | (lr >= SIDE)
    low_c = lc & 1
    side = jnp.where(lc >= SIDE, 1, 0)
    slot = i * 2 + (lc >> 3)
    sub = lc & 7
    slot = jnp.where(outside_c, 24 + side * 4 + low_c * 2 + (lr >> 3), slot)
    sub = jnp.where(outside_c, lr & 7, sub)
    corner_hit = outside_c & outside_r
    slot = jnp.where(corner_hit, 32, slot)
    sub = jnp.where(corner_hit, side * 4 + low_c * 2 + (lr & 1), sub)
    score = jnp.zeros((8, HALF), F32)
    for n in range(33):
        at = n * 8 if n < 32 else 256 + first
        got = jnp.take_along_axis(scores[at : at + 8], sub, axis=0)
        score = jnp.where(slot == n, got, score)
    score = score * PATCH ** (-0.5)
    e = jnp.exp(score - jnp.max(score, axis=0, keepdims=True))
    lane = iota((8, HALF), 1)
    step_r = (lr - (lane >> 4) - 8 * h).astype(F32) + off_r * (1.0 / PITCH)
    step_c = (lc - (lane & 15)).astype(F32) + off_c * (1.0 / PITCH)
    total = jnp.sum(e, axis=0, keepdims=True)
    t_r = jnp.sum(e * step_r, axis=0, keepdims=True) / total
    t_c = jnp.sum(e * step_c, axis=0, keepdims=True) / total
    return jnp.concatenate([t_r, t_c], axis=0)


def own_targets(patches, cand, offs, xa, xb, ra, rb, t0, t1, left, right, above, below):
    row, col = tile_place()
    sort_halos(row, col, xa, xb, ra, rb, left, right, above, below)

    def one(s, z, store, corner_first):
        d = s + z + 1

        def strip(ref):
            return ref[pl.ds(pl.multiple_of(d * 32, 32), 32), :]

        pieces = (patches[d], strip(left), strip(right), strip(above), strip(below))
        for h in range(2):
            src = above if h == 0 else below
            at = pl.multiple_of(256 + d // 2 * 16, 16)
            corner = (src[pl.ds(at, 16), :], corner_first)
            lanes = slice(h * HALF, h * HALF + HALF)
            lr, lc = local_place(cand[s, z, :, lanes], row, col)
            got = half_targets(
                h,
                patches[s, lanes, :],
                pieces,
                corner,
                lr,
                lc,
                offs[s, z, 0, :, lanes].astype(F32),
                offs[s, z, 1, :, lanes].astype(F32),
            )
            store[s, :, lanes] = got

    def body(n, carry):
        one(2 * n, 0, t0, 8)
        one(2 * n, 1, t1, 0)
        one(2 * n + 1, 0, t0, 0)
        one(2 * n + 1, 1, t1, 8)
        return carry

    t0[7] = jnp.zeros((2, VT), F32)
    t1[6] = jnp.zeros((2, VT), F32)
    t1[7] = jnp.zeros((2, VT), F32)
    lax.fori_loop(0, 3, body, 0)
    one(6, 0, t0, 8)


def sort_halos(row, col, xa, xb, ra, rb, left, right, above, below):
    for index, first, second, p, q in ((col, left, right, xa, xb), (row, above, below, ra, rb)):

        @pl.when(index % 2 == 0)
        def _():
            first[...] = q[...]
            second[...] = p[...]

        @pl.when(index % 2 == 1)
        def _():
            first[...] = p[...]
            second[...] = q[...]


def laplace(u, left, right, above, below, row, col):
    lane = iota(u.shape, 1)
    b = lane & 15
    up = jnp.where(lane < SIDE, pltpu.roll(above, SIDE, 1), pltpu.roll(u, SIDE, 1))
    up = jnp.where((lane < SIDE) & (row == 0), u, up)
    down = jnp.where(lane >= VT - SIDE, pltpu.roll(below, VT - SIDE, 1), pltpu.roll(u, VT - SIDE, 1))
    down = jnp.where((lane >= VT - SIDE) & (row == COLS - 1), u, down)
    west = jnp.where(b == 0, pltpu.roll(left, VT - SIDE + 1, 1), pltpu.roll(u, 1, 1))
    west = jnp.where((b == 0) & (col == 0), u, west)
    east = jnp.where(b == SIDE - 1, pltpu.roll(right, SIDE - 1, 1), pltpu.roll(u, VT - 1, 1))
    east = jnp.where((b == SIDE - 1) & (col == COLS - 1), u, east)
    return ((down - u) - (u - up)) + ((east - u) - (u - west))


def relaxed(u, tall, t0, t1, c0, c1, plane):
    base = tall[0:20, :]
    s0 = c0[0:20, :] * (tall[2:22, :] - base - t0[0:20, :])
    s1 = c1[0:20, :] * (tall[4:24, :] - base - t1[0:20, :])
    zforce = s0[4:20] - s0[2:18] + s1[4:20] - s1[0:16]
    return u + STEP * (plane + zforce)


def first_round(
    patches, cand, offs, pairs, start, xa, xb, ra, rb, sa, sb, p0, p1,
    targets, u1, t0, t1, c0, c1,
    left, right, above, below, upper, lower, tall,
):
    row, col = tile_place()
    stack = lax.axis_index("stack").astype(I32)
    sort_halos(row, col, xa, xb, ra, rb, left, right, above, below)

    @pl.when(stack % 2 == 0)
    def _():
        upper[...] = sa[...]
        lower[...] = sb[...]

    @pl.when(stack % 2 == 1)
    def _():
        upper[...] = sb[...]
        lower[...] = sa[...]

    def pieces_of(d):
        if d < SEC:
            return (
                patches[d],
                left[32 * d : 32 * d + 32, :],
                right[32 * d : 32 * d + 32, :],
                above[32 * d : 32 * d + 32, :],
                below[32 * d : 32 * d + 32, :],
            ), (above[256 + d // 2 * 16 : 272 + d // 2 * 16, :], below[256 + d // 2 * 16 : 272 + d // 2 * 16, :])
        e = d - SEC
        return (
            upper[256 * e : 256 * e + 256, :],
            upper[512 + 64 * e : 544 + 64 * e, :],
            upper[544 + 64 * e : 576 + 64 * e, :],
            upper[640 + 64 * e : 672 + 64 * e, :],
            upper[672 + 64 * e : 704 + 64 * e, :],
        ), (upper[768:784, :], upper[784:800, :])

    rows_of(p0, t0, 4)
    rows_of(p1, t1, 4)
    t0[0:4, :] = jnp.zeros((4, VT), F32)
    t1[0:4, :] = jnp.zeros((4, VT), F32)
    c0[0:4, :] = jnp.zeros((4, VT), F32)
    c1[0:4, :] = jnp.zeros((4, VT), F32)
    for s in range(SEC):
        for z, c in ((0, c0), (1, c1)):
            c[4 + 2 * s : 6 + 2 * s, :] = jnp.full((2, VT), pairs[s, z], I32).astype(F32)
    last = stack == lax.axis_size("stack") - 1
    tied = jnp.where(stack == 0, 0.0, lower[704:720, :].astype(F32))
    for p, (s, z) in enumerate(CROSS):
        t, c = ((t0, c0), (t1, c1))[z]
        pieces, corners = pieces_of(s + z + 1)
        corner_first = 8 * ((s + z + 1) % 2)
        for h in range(2):
            lanes = slice(h * HALF, h * HALF + HALF)
            lr, lc = local_place(cand[s, z, :, lanes], row, col)
            got = half_targets(
                h, patches[s, lanes, :], pieces, (corners[h], corner_first), lr, lc,
                offs[s, z, 0, :, lanes].astype(F32), offs[s, z, 1, :, lanes].astype(F32),
            )
            t[4 + 2 * s : 6 + 2 * s, lanes] = jnp.where(last, 0.0, got)
        c[4 + 2 * s : 6 + 2 * s, :] = jnp.where(last, 0.0, c[4 + 2 * s : 6 + 2 * s, :])
        d = s + z + 1 - SEC
        pieces, corners = pieces_of(d)
        mine = lower[256 * (s - 6) : 256 * (s - 6) + 256, :]
        planes = [lower[512 + 64 * p + 16 * n : 528 + 64 * p + 16 * n, :].astype(F32) for n in range(4)]
        for h in range(2):
            lanes = slice(h * HALF, h * HALF + HALF)
            lr, lc, off_r, off_c = [plane[8 * h : 8 * h + 8] for plane in planes]
            got = half_targets(
                h, mine[lanes, :], pieces, (corners[h], 8 * (d % 2)),
                lr.astype(I32), lc.astype(I32), off_r, off_c,
            )
            t[2 * (s - 6) : 2 * (s - 6) + 2, lanes] = got
        line = tied[p : p + 1, :]
        c[2 * (s - 6) : 2 * (s - 6) + 2, :] = jnp.broadcast_to(
            jnp.concatenate([line, line], axis=1), (2, VT)
        )
    for s in range(SEC):
        for z, t in ((0, t0), (1, t1)):
            targets[s, z] = t[4 + 2 * s : 6 + 2 * s, :]
    rows_of(start, tall, 4)
    for at, ref in ((0, lower), (20, upper)):
        ends = ref[800:816, :].astype(F32)
        tall[at : at + 4, 0:HALF] = ends[0:4] + ends[8:12]
        tall[at : at + 4, HALF:VT] = ends[4:8] + ends[12:16]
    u = tall[4:20, :]

    def whole(ref):
        part = [ref[256 + 16 * n : 272 + 16 * n, :].astype(F32) for n in range(4)]
        return jnp.concatenate([part[0] + part[2], part[1] + part[3]], axis=1)

    def half(ref):
        part = ref[320:336, :].astype(F32) + ref[336:352, :].astype(F32)
        return jnp.concatenate([part, part], axis=1)

    plane = laplace(u, whole(left), whole(right), half(above), half(below), row, col)
    u1[...] = relaxed(u, tall, t0, t1, c0, c1, plane)


def second_round(u1, xa, xb, ra, rb, sa, sb, t0, t1, c0, c1, out, tall):
    row, col = tile_place()
    stack = lax.axis_index("stack").astype(I32)
    col_even, row_even, stack_even = col % 2 == 0, row % 2 == 0, stack % 2 == 0
    u = u1[...]
    tall[4:20, :] = u
    tall[0:4, :] = jnp.where(stack_even, sb[12:16, :], sa[12:16, :])
    tall[20:24, :] = jnp.where(stack_even, sa[0:4, :], sb[0:4, :])
    plane = laplace(
        u,
        jnp.where(col_even, xb[...], xa[...]),
        jnp.where(col_even, xa[...], xb[...]),
        jnp.where(row_even, rb[...], ra[...]),
        jnp.where(row_even, ra[...], rb[...]),
        row,
        col,
    )
    u = relaxed(u, tall, t0, t1, c0, c1, plane)
    for s in range(SEC):
        out[s] = u[2 * s : 2 * s + 2]


def shape(*dims, dtype=F32):
    return jax.ShapeDtypeStruct(dims, dtype)


def call(body, outs, scratch, name, flops, smem=(), n_in=0, nbytes=1 << 20):
    specs = [
        pl.BlockSpec(memory_space=pltpu.SMEM) if n in smem else pl.BlockSpec(memory_space=pltpu.VMEM)
        for n in range(n_in)
    ]
    return pl.pallas_call(
        body,
        out_shape=outs,
        in_specs=specs,
        out_specs=[pl.BlockSpec(memory_space=pltpu.VMEM) for _ in outs],
        scratch_shapes=scratch,
        name=name,
        compiler_params=pltpu.CompilerParams(vmem_limit_bytes=24 << 20),
        cost_estimate=pl.CostEstimate(flops=flops, bytes_accessed=nbytes, transcendentals=0),
    )


def on_device(patches, cand, offs, pairs, start):
    flat = pltpu.VMEM((16, VT), F32)
    xa, xb = call(pack_cols, [shape(X_ROWS, PATCH, dtype=BF)] * 2, [flat], "pack_cols", 1 << 20, n_in=2)(
        patches, start
    )
    xa = swapped(xa, "tile", col_a)
    xb = swapped(xb, "tile", col_b)
    ra, rb = call(pack_rows, [shape(R_ROWS, PATCH, dtype=BF)] * 2, [flat], "pack_rows", 1 << 20, n_in=4)(
        patches, start, xa, xb
    )
    ra = swapped(ra, "tile", row_a)
    rb = swapped(rb, "tile", row_b)
    sa, sb = call(
        pack_stack, [shape(S_ROWS, PATCH, dtype=BF)] * 2, [flat], "pack_stack", 1 << 20, smem=(3,), n_in=9
    )(patches, cand, offs, pairs, start, xa, xb, ra, rb)
    sa = swapped(sa, "stack", stack_a)
    sb = swapped(sb, "stack", stack_b)
    halos = [pltpu.VMEM((X_ROWS, PATCH), BF)] * 2 + [pltpu.VMEM((R_ROWS, PATCH), BF)] * 2
    p0, p1 = call(own_targets, [shape(SEC, 2, VT)] * 2, halos, "own_targets", 1 << 31, n_in=7)(
        patches, cand, offs, xa, xb, ra, rb
    )
    targets, u1, t0, t1, c0, c1 = call(
        first_round,
        [shape(SEC, 2, 2, VT), shape(16, VT)] + [shape(24, VT)] * 4,
        halos + [pltpu.VMEM((S_ROWS, PATCH), BF)] * 2 + [pltpu.VMEM((24, VT), F32)],
        "first_round",
        1 << 30,
        smem=(3,),
        n_in=13,
    )(patches, cand, offs, pairs, start, xa, xb, ra, rb, sa, sb, p0, p1)
    moved = [
        swapped(u1, axis, partner)
        for axis, partner in (
            ("tile", col_a), ("tile", col_b), ("tile", row_a), ("tile", row_b), ("stack", stack_a), ("stack", stack_b),
        )
    ]
    (aligned,) = call(
        second_round, [shape(SEC, 2, VT)], [pltpu.VMEM((24, VT), F32)], "second_round", 1 << 20, n_in=11
    )(u1, *moved, t0, t1, c0, c1)
    return aligned, targets


def solution(mesh):
    placed = (
        P("stack", "tile", None),
        P("stack", None, None, "tile"),
        P("stack", None, None, None, "tile"),
        P("stack", None),
        P("stack", None, "tile"),
    )
    return jax.shard_map(
        on_device,
        mesh=mesh,
        in_specs=placed,
        out_specs=(P("stack", None, "tile"), P("stack", None, None, "tile")),
        check_vma=False,
    )
```

time: 264 us -> 45.3 us (0.17)
  the two profiles are of different devices: /device:TPU:88 before, /device:TPU:2 now
where the time goes in v1:
time: 45.3 us; the launch traced here: 45.1 us
  starting transfers between devices  24.7 us (55%)
  waiting for transfers between devices  12.4 us (27%)
  Pallas kernels  5.42 us (12%)
  local copies, waits for them, and re-layouts  1.85 us (4%)
  between operations  0.73 us (2%)
    ppermute x12, starting transfers between devices, swapped(): lax.ppermute(block, axis, [(i, partner(i)) for i in range(lax.axis_size(a...  24.7 us
    ppermute x12, waiting for transfers between devices, swapped(): lax.ppermute(block, axis, [(i, partner(i)) for i in range(lax.axis_size(a...  12.4 us
    pallas_call x1, Pallas kernels, on_device(): call(first_round, [shape(SEC, 2, 2, VT), shape(16, VT)] + [shape(24, VT)]...  1.88 us
    unnamed x15, local copies, waits for them, and re-layouts  1.85 us
    pallas_call x1, Pallas kernels, on_device(): call(own_targets, [shape(SEC, 2, VT)] * 2, halos, 'own_targets', 1 << 31,...  1.71 us
  transfers between devices with their start and end apart: 12, of which 6 were waited for; matrix products, arithmetic and copies ran while one was open for 0% of the time, Pallas kernels for 4%

profile of v1, /device:TPU:2, one launch (start us, length us, event | category | flops | bytes accessed | tf_op | source)
XLA Modules:
  0.0 45.1 jit_solution(11105638626088948476)
XLA Ops:
  0.6 1.0 %copy-done = bf16[8,256,128]{2,1,0:T(8,128)(2,1)S(1)} copy-done((bf16[8,256,128]{2,1,0:T(8,128)(2,1)S(1)}, bf16[8,256,128]{2,1,0:T(8,128)(2,1)}, u32[]{:S(2)}) %copy-start) | copy-done | bytes 524312
  1.7 0.7 %copy-done.3 = f32[8,2,256]{2,1,0:T(2,128)S(1)} copy-done((f32[8,2,256]{2,1,0:T(2,128)S(1)}, f32[8,2,256]{2,1,0:T(2,128)}, u32[]{:S(2)}) %copy-start.3) | copy-done | bytes 16408
  2.4 0.2 pack_cols.1
  2.6 2.4 %collective-permute-start = (bf16[320,128]{1,0:T(8,128)(2,1)S(1)}, bf16[320,128]{1,0:T(8,128)(2,1)S(1)}, u32[]{:S(2)}, u32[]{:S(2)}) collective-permute-start(bf16[320,128]{1,0:T(8,128)(2,1)S(1)} %get-tuple-element.16), channel_id=1, source_target_pairs={{0,1},{1,0},{2,3},{3,2},{4,5},{5,4},{6,7},{7,6},{8,9},{9,8},{10,11... | collective-permute-start | bytes 245768 | tf_op jit(solution)/shard_map/ppermute | solution.py:27
  5.0 0.4 collective-permute-start.1
  5.4 2.0 %collective-permute-done.xa = bf16[320,128]{1,0:T(8,128)(2,1)S(1)} collective-permute-done((bf16[320,128]{1,0:T(8,128)(2,1)S(1)}, bf16[320,128]{1,0:T(8,128)(2,1)S(1)}, u32[]{:S(2)}, u32[]{:S(2)}) %collective-permute-start) | collective-permute-done | bytes 81952 | tf_op jit(solution)/shard_map/ppermute | solution.py:27
  7.4 2.0 %collective-permute-done.1.xb = bf16[320,128]{1,0:T(8,128)(2,1)S(1)} collective-permute-done((bf16[320,128]{1,0:T(8,128)(2,1)S(1)}, bf16[320,128]{1,0:T(8,128)(2,1)S(1)}, u32[]{:S(2)}, u32[]{:S(2)}) %collective-permute-start.1) | collective-permute-done | bytes 81952 | tf_op jit(solution)/shard_map/ppermute | solution.py:27
  9.4 0.2 pack_rows.1
  9.6 0.0 copy-start.6
  9.7 1.8 %collective-permute-start.2 = (bf16[352,128]{1,0:T(8,128)(2,1)S(1)}, bf16[352,128]{1,0:T(8,128)(2,1)S(1)}, u32[]{:S(2)}, u32[]{:S(2)}) collective-permute-start(bf16[352,128]{1,0:T(8,128)(2,1)S(1)} %get-tuple-element.18), channel_id=1, source_target_pairs={{0,4},{1,5},{2,6},{3,7},{4,0},{5,1},{6,2},{7,3},{8,12},{9,13},{10,... | collective-permute-start | bytes 270344 | tf_op jit(solution)/shard_map/ppermute | solution.py:27
  11.4 4.5 %collective-permute-start.3 = (bf16[352,128]{1,0:T(8,128)(2,1)S(1)}, bf16[352,128]{1,0:T(8,128)(2,1)S(1)}, u32[]{:S(2)}, u32[]{:S(2)}) collective-permute-start(bf16[352,128]{1,0:T(8,128)(2,1)S(1)} %get-tuple-element.19), channel_id=1, source_target_pairs={{0,12},{1,13},{2,14},{3,15},{4,8},{5,9},{6,10},{7,11},{8,4},{9,5},... | collective-permute-start | bytes 270344 | tf_op jit(solution)/shard_map/ppermute | solution.py:27
  15.9 0.1 copy.8.pairs
  16.0 0.2 collective-permute-done.2.ra
  16.1 3.2 %collective-permute-done.3.rb = bf16[352,128]{1,0:T(8,128)(2,1)S(1)} collective-permute-done((bf16[352,128]{1,0:T(8,128)(2,1)S(1)}, bf16[352,128]{1,0:T(8,128)(2,1)S(1)}, u32[]{:S(2)}, u32[]{:S(2)}) %collective-permute-start.3) | collective-permute-done | bytes 90144 | tf_op jit(solution)/shard_map/ppermute | solution.py:27
  19.4 0.7 %pack_stack.1 = (bf16[816,128]{1,0:T(8,128)(2,1)S(1)}, bf16[816,128]{1,0:T(8,128)(2,1)S(1)}) custom-call(bf16[8,256,128]{2,1,0:T(8,128)(2,1)S(1)} %copy-done.1, s32[8,2,8,256]{3,2,1,0:T(8,128)S(1)} %copy-done.5, s32[8,2,2,8,256]{4,3,2,1,0:T(8,128)S(1)} %copy-done.2, s32[8,2]{1,0:T(8,128)S(1)} %copy.8.pairs, f32[8,2,256]{2,1,0:T(2,128)S(1)} %copy-done.4, ...), custom_call_target="tpu_custom_call" | custom-call | flops 1048576 | bytes 1048576 | tf_op jit(solution)/shard_map/pack_stack/pallas_call | solution.py:476
  20.1 0.1 collective-permute-start.4
  20.2 4.1 %collective-permute-start.5 = (bf16[816,128]{1,0:T(8,128)(2,1)S(1)}, bf16[816,128]{1,0:T(8,128)(2,1)S(1)}, u32[]{:S(2)}, u32[]{:S(2)}) collective-permute-start(bf16[816,128]{1,0:T(8,128)(2,1)S(1)} %get-tuple-element.21), channel_id=1, source_target_pairs={{0,240},{16,32},{32,16},{48,64},{64,48},{80,96},{96,80},{112,128},... | collective-permute-start | bytes 626696 | tf_op jit(solution)/shard_map/ppermute | solution.py:27
  24.3 1.7 %own_targets.1 = (f32[8,2,256]{2,1,0:T(2,128)S(1)}, f32[8,2,256]{2,1,0:T(2,128)S(1)}) custom-call(bf16[8,256,128]{2,1,0:T(8,128)(2,1)S(1)} %copy-done.1, s32[8,2,8,256]{3,2,1,0:T(8,128)S(1)} %copy-done.5, s32[8,2,2,8,256]{4,3,2,1,0:T(8,128)S(1)} %copy-done.2, bf16[320,128]{1,0:T(8,128)(2,1)S(1)} %collective-permute-done.xa, ...), custom_call_target="tpu_custom_call" | custom-call | flops 2147483648 | bytes 1048576 | tf_op jit(solution)/shard_map/own_targets/pallas_call | solution.py:482
  26.0 0.0 collective-permute-done.4.sa
  26.0 3.3 %collective-permute-done.5.sb = bf16[816,128]{1,0:T(8,128)(2,1)S(1)} collective-permute-done((bf16[816,128]{1,0:T(8,128)(2,1)S(1)}, bf16[816,128]{1,0:T(8,128)(2,1)S(1)}, u32[]{:S(2)}, u32[]{:S(2)}) %collective-permute-start.5) | collective-permute-done | bytes 208928 | tf_op jit(solution)/shard_map/ppermute | solution.py:27
  29.3 1.9 %first_round.1 = (f32[8,2,2,256]{3,2,1,0:T(2,128)}, f32[16,256]{1,0:T(8,128)S(1)}, f32[24,256]{1,0:T(8,128)S(1)}, f32[24,256]{1,0:T(8,128)S(1)}, f32[24,256]{1,0:T(8,128)S(1)}, /*index=5*/f32[24,256]{1,0:T(8,128)S(1)}) custom-call(bf16[8,256,128]{2,1,0:T(8,128)(2,1)S(1)} %copy-done.1, s32[8,2,8,256]{3,2,1,0:T(8,128)S(1)} %copy-done.5, ...), custom_call_target="tpu_custom_call" | custom-call | flops 1073741824 | bytes 1048576 | tf_op jit(solution)/shard_map/first_round/pallas_call | solution.py:485
  31.2 0.0 collective-permute-start.10
  31.2 2.3 %collective-permute-start.11 = (f32[16,256]{1,0:T(8,128)S(1)}, f32[16,256]{1,0:T(8,128)S(1)}, u32[]{:S(2)}, u32[]{:S(2)}) collective-permute-start(f32[16,256]{1,0:T(8,128)S(1)} %get-tuple-element.24.u1), channel_id=1, source_target_pairs={{0,240},{16,32},{32,16},{48,64},{64,48},{80,96},{96,80},{112,128},... | collective-permute-start | bytes 49160 | tf_op jit(solution)/shard_map/ppermute | solution.py:27
  33.5 2.4 %collective-permute-start.6 = (f32[16,256]{1,0:T(8,128)S(1)}, f32[16,256]{1,0:T(8,128)S(1)}, u32[]{:S(2)}, u32[]{:S(2)}) collective-permute-start(f32[16,256]{1,0:T(8,128)S(1)} %get-tuple-element.24.u1), channel_id=1, source_target_pairs={{0,1},{1,0},{2,3},{3,2},{4,5},{5,4},{6,7},{7,6},{8,9},{9,8},{10,11... | collective-permute-start | bytes 49160 | tf_op jit(solution)/shard_map/ppermute | solution.py:27
  35.9 1.5 %collective-permute-start.7 = (f32[16,256]{1,0:T(8,128)S(1)}, f32[16,256]{1,0:T(8,128)S(1)}, u32[]{:S(2)}, u32[]{:S(2)}) collective-permute-start(f32[16,256]{1,0:T(8,128)S(1)} %get-tuple-element.24.u1), channel_id=1, source_target_pairs={{0,3},{1,2},{2,1},{3,0},{4,7},{5,6},{6,5},{7,4},{8,11},{9,10},{10,... | collective-permute-start | bytes 49160 | tf_op jit(solution)/shard_map/ppermute | solution.py:27
  37.3 1.1 %collective-permute-start.8 = (f32[16,256]{1,0:T(8,128)S(1)}, f32[16,256]{1,0:T(8,128)S(1)}, u32[]{:S(2)}, u32[]{:S(2)}) collective-permute-start(f32[16,256]{1,0:T(8,128)S(1)} %get-tuple-element.24.u1), channel_id=1, source_target_pairs={{0,4},{1,5},{2,6},{3,7},{4,0},{5,1},{6,2},{7,3},{8,12},{9,13},{10,... | collective-permute-start | bytes 49160 | tf_op jit(solution)/shard_map/ppermute | solution.py:27
  38.5 0.0 collective-permute-done.10.sa
  38.5 4.1 %collective-permute-start.9 = (f32[16,256]{1,0:T(8,128)S(1)}, f32[16,256]{1,0:T(8,128)S(1)}, u32[]{:S(2)}, u32[]{:S(2)}) collective-permute-start(f32[16,256]{1,0:T(8,128)S(1)} %get-tuple-element.24.u1), channel_id=1, source_target_pairs={{0,12},{1,13},{2,14},{3,15},{4,8},{5,9},{6,10},{7,11},{8,4},{9,5},... | collective-permute-start | bytes 49160 | tf_op jit(solution)/shard_map/ppermute | solution.py:27
  42.6 0.0 collective-permute-done.11.sb
  42.6 0.0 collective-permute-done.8.ra
  42.7 1.7 %collective-permute-done.9.rb = f32[16,256]{1,0:T(8,128)S(1)} collective-permute-done((f32[16,256]{1,0:T(8,128)S(1)}, f32[16,256]{1,0:T(8,128)S(1)}, u32[]{:S(2)}, u32[]{:S(2)}) %collective-permute-start.9) | collective-permute-done | bytes 16416 | tf_op jit(solution)/shard_map/ppermute | solution.py:27
  44.4 0.7 %second_round.1 = f32[8,2,256]{2,1,0:T(2,128)} custom-call(f32[16,256]{1,0:T(8,128)S(1)} %get-tuple-element.24.u1, f32[16,256]{1,0:T(8,128)S(1)} %collective-permute-done.6.xa, f32[16,256]{1,0:T(8,128)S(1)} %collective-permute-done.7.xb, f32[16,256]{1,0:T(8,128)S(1)} %collective-permute-done.8.ra, f32[16,256]{1,0:T(8,128)S(1)} %collective-permute-done.9.rb, ...), custom_call_target="tpu_custom_call" | custom-call | flops 1048576 | bytes 1048576 | tf_op jit(solution)/shard_map/second_round/pallas_call | solution.py:500
  (13 shorter events, 0.0 us)
Async XLA Ops:
  0.6 1.0 %copy-start = (bf16[8,256,128]{2,1,0:T(8,128)(2,1)S(1)}, bf16[8,256,128]{2,1,0:T(8,128)(2,1)}, u32[]{:S(2)}) copy-start(bf16[8,256,128]{2,1,0:T(8,128)(2,1)} %patches.9) | copy-start | bytes 1572868
  1.7 0.7 %copy-start.3 = (f32[8,2,256]{2,1,0:T(2,128)S(1)}, f32[8,2,256]{2,1,0:T(2,128)}, u32[]{:S(2)}) copy-start(f32[8,2,256]{2,1,0:T(2,128)} %start.7) | copy-start | bytes 49156
  2.4 17.0 %copy-start.1 = (bf16[8,256,128]{2,1,0:T(8,128)(2,1)S(1)}, bf16[8,256,128]{2,1,0:T(8,128)(2,1)}, u32[]{:S(2)}) copy-start(bf16[8,256,128]{2,1,0:T(8,128)(2,1)} %patches.9) | copy-start | bytes 1572868
  2.6 4.8 %collective-permute-start = (bf16[320,128]{1,0:T(8,128)(2,1)S(1)}, bf16[320,128]{1,0:T(8,128)(2,1)S(1)}, u32[]{:S(2)}, u32[]{:S(2)}) collective-permute-start(bf16[320,128]{1,0:T(8,128)(2,1)S(1)} %get-tuple-element.16), channel_id=1, source_target_pairs={{0,1},{1,0},{2,3},{3,2},{4,5},{5,4},{6,7},{7,6},{8,9},{9,8},{10,11... | collective-permute-start | bytes 245768 | tf_op jit(solution)/shard_map/ppermute | solution.py:27
  5.0 14.4 %copy-start.2 = (s32[8,2,2,8,256]{4,3,2,1,0:T(8,128)S(1)}, s32[8,2,2,8,256]{4,3,2,1,0:T(8,128)}, u32[]{:S(2)}) copy-start(s32[8,2,2,8,256]{4,3,2,1,0:T(8,128)} %offs.5) | copy-start | bytes 786436
  5.0 14.4 %copy-start.5 = (s32[8,2,8,256]{3,2,1,0:T(8,128)S(1)}, s32[8,2,8,256]{3,2,1,0:T(8,128)}, u32[]{:S(2)}) copy-start(s32[8,2,8,256]{3,2,1,0:T(8,128)} %cand.5) | copy-start | bytes 393220
  5.0 4.4 %collective-permute-start.1 = (bf16[320,128]{1,0:T(8,128)(2,1)S(1)}, bf16[320,128]{1,0:T(8,128)(2,1)S(1)}, u32[]{:S(2)}, u32[]{:S(2)}) collective-permute-start(bf16[320,128]{1,0:T(8,128)(2,1)S(1)} %get-tuple-element.17), channel_id=1, source_target_pairs={{0,3},{1,2},{2,1},{3,0},{4,7},{5,6},{6,5},{7,4},{8,11},{9,10},{10,... | collective-permute-start | bytes 245768 | tf_op jit(solution)/shard_map/ppermute | solution.py:27
  9.4 9.9 %copy-start.4 = (f32[8,2,256]{2,1,0:T(2,128)S(1)}, f32[8,2,256]{2,1,0:T(2,128)}, u32[]{:S(2)}) copy-start(f32[8,2,256]{2,1,0:T(2,128)} %start.7) | copy-start | bytes 49156
  9.6 6.2 %copy-start.6 = (s32[8,2]{0,1:T(2,128)S(1)}, s32[8,2]{0,1:T(2,128)}, u32[]{:S(2)}) copy-start(s32[8,2]{0,1:T(2,128)} %param.8) | copy-start | bytes 196
  9.7 6.5 %collective-permute-start.2 = (bf16[352,128]{1,0:T(8,128)(2,1)S(1)}, bf16[352,128]{1,0:T(8,128)(2,1)S(1)}, u32[]{:S(2)}, u32[]{:S(2)}) collective-permute-start(bf16[352,128]{1,0:T(8,128)(2,1)S(1)} %get-tuple-element.18), channel_id=1, source_target_pairs={{0,4},{1,5},{2,6},{3,7},{4,0},{5,1},{6,2},{7,3},{8,12},{9,13},{10,... | collective-permute-start | bytes 270344 | tf_op jit(solution)/shard_map/ppermute | solution.py:27
  11.4 7.9 %collective-permute-start.3 = (bf16[352,128]{1,0:T(8,128)(2,1)S(1)}, bf16[352,128]{1,0:T(8,128)(2,1)S(1)}, u32[]{:S(2)}, u32[]{:S(2)}) collective-permute-start(bf16[352,128]{1,0:T(8,128)(2,1)S(1)} %get-tuple-element.19), channel_id=1, source_target_pairs={{0,12},{1,13},{2,14},{3,15},{4,8},{5,9},{6,10},{7,11},{8,4},{9,5},... | collective-permute-start | bytes 270344 | tf_op jit(solution)/shard_map/ppermute | solution.py:27
  20.1 5.9 %collective-permute-start.4 = (bf16[816,128]{1,0:T(8,128)(2,1)S(1)}, bf16[816,128]{1,0:T(8,128)(2,1)S(1)}, u32[]{:S(2)}, u32[]{:S(2)}) collective-permute-start(bf16[816,128]{1,0:T(8,128)(2,1)S(1)} %get-tuple-element.20), channel_id=1, source_target_pairs={{0,16},{16,0},{32,48},{48,32},{64,80},{80,64},{96,112},{112,96},{1... | collective-permute-start | bytes 626696 | tf_op jit(solution)/shard_map/ppermute | solution.py:27
  20.2 9.1 %collective-permute-start.5 = (bf16[816,128]{1,0:T(8,128)(2,1)S(1)}, bf16[816,128]{1,0:T(8,128)(2,1)S(1)}, u32[]{:S(2)}, u32[]{:S(2)}) collective-permute-start(bf16[816,128]{1,0:T(8,128)(2,1)S(1)} %get-tuple-element.21), channel_id=1, source_target_pairs={{0,240},{16,32},{32,16},{48,64},{64,48},{80,96},{96,80},{112,128},... | collective-permute-start | bytes 626696 | tf_op jit(solution)/shard_map/ppermute | solution.py:27
  31.2 7.3 %collective-permute-start.10 = (f32[16,256]{1,0:T(8,128)S(1)}, f32[16,256]{1,0:T(8,128)S(1)}, u32[]{:S(2)}, u32[]{:S(2)}) collective-permute-start(f32[16,256]{1,0:T(8,128)S(1)} %get-tuple-element.24.u1), channel_id=1, source_target_pairs={{0,16},{16,0},{32,48},{48,32},{64,80},{80,64},{96,112},{112,96},{1... | collective-permute-start | bytes 49160 | tf_op jit(solution)/shard_map/ppermute | solution.py:27
  31.2 11.5 %collective-permute-start.11 = (f32[16,256]{1,0:T(8,128)S(1)}, f32[16,256]{1,0:T(8,128)S(1)}, u32[]{:S(2)}, u32[]{:S(2)}) collective-permute-start(f32[16,256]{1,0:T(8,128)S(1)} %get-tuple-element.24.u1), channel_id=1, source_target_pairs={{0,240},{16,32},{32,16},{48,64},{64,48},{80,96},{96,80},{112,128},... | collective-permute-start | bytes 49160 | tf_op jit(solution)/shard_map/ppermute | solution.py:27
  33.5 9.1 %collective-permute-start.6 = (f32[16,256]{1,0:T(8,128)S(1)}, f32[16,256]{1,0:T(8,128)S(1)}, u32[]{:S(2)}, u32[]{:S(2)}) collective-permute-start(f32[16,256]{1,0:T(8,128)S(1)} %get-tuple-element.24.u1), channel_id=1, source_target_pairs={{0,1},{1,0},{2,3},{3,2},{4,5},{5,4},{6,7},{7,6},{8,9},{9,8},{10,11... | collective-permute-start | bytes 49160 | tf_op jit(solution)/shard_map/ppermute | solution.py:27
  35.9 6.8 %collective-permute-start.7 = (f32[16,256]{1,0:T(8,128)S(1)}, f32[16,256]{1,0:T(8,128)S(1)}, u32[]{:S(2)}, u32[]{:S(2)}) collective-permute-start(f32[16,256]{1,0:T(8,128)S(1)} %get-tuple-element.24.u1), channel_id=1, source_target_pairs={{0,3},{1,2},{2,1},{3,0},{4,7},{5,6},{6,5},{7,4},{8,11},{9,10},{10,... | collective-permute-start | bytes 49160 | tf_op jit(solution)/shard_map/ppermute | solution.py:27
  37.3 5.3 %collective-permute-start.8 = (f32[16,256]{1,0:T(8,128)S(1)}, f32[16,256]{1,0:T(8,128)S(1)}, u32[]{:S(2)}, u32[]{:S(2)}) collective-permute-start(f32[16,256]{1,0:T(8,128)S(1)} %get-tuple-element.24.u1), channel_id=1, source_target_pairs={{0,4},{1,5},{2,6},{3,7},{4,0},{5,1},{6,2},{7,3},{8,12},{9,13},{10,... | collective-permute-start | bytes 49160 | tf_op jit(solution)/shard_map/ppermute | solution.py:27
  38.5 5.9 %collective-permute-start.9 = (f32[16,256]{1,0:T(8,128)S(1)}, f32[16,256]{1,0:T(8,128)S(1)}, u32[]{:S(2)}, u32[]{:S(2)}) collective-permute-start(f32[16,256]{1,0:T(8,128)S(1)} %get-tuple-element.24.u1), channel_id=1, source_target_pairs={{0,12},{1,13},{2,14},{3,15},{4,8},{5,9},{6,10},{7,11},{8,4},{9,5},... | collective-permute-start | bytes 49160 | tf_op jit(solution)/shard_map/ppermute | solution.py:27

commit v2 on v0

v2 whole, which is shorter than its diff:
```python
import jax
import jax.numpy as jnp
from jax import lax
from jax.experimental import pallas as pl
from jax.experimental.pallas import tpu as pltpu
from jax.sharding import PartitionSpec as P

SIDE = 16
COLS = 4
PATCH = 128
VT = 256
HALF = 128
SEC = 8
PITCH = 128.0
STEP = 0.1
BF = jnp.bfloat16
F32 = jnp.float32
I32 = jnp.int32

X_ROWS = 8 * 32 + 64
C_ROWS = 64 + 32
S_ROWS = 736
CROSS = ((6, 1), (7, 0), (7, 1))


def swapped(block, axis, partner):
    return lax.ppermute(block, axis, [(i, partner(i)) for i in range(lax.axis_size(axis))])


def col_a(i):
    return i ^ 1


def col_b(i):
    return i // COLS * COLS + (COLS - 1 - i % COLS)


def row_a(i):
    return i ^ COLS


def row_b(i):
    return (COLS - 1 - i // COLS) * COLS + i % COLS


def stack_a(i):
    return i ^ 1


def stack_b(i):
    return (((i + 1) ^ 1) - 1) % 16


def tile_place():
    tile = lax.axis_index("tile").astype(I32)
    return tile // COLS, tile % COLS


def iota(shape, dim):
    return lax.broadcasted_iota(I32, shape, dim)


def two_parts(u):
    hi = u.astype(BF)
    return hi, (u - hi.astype(F32)).astype(BF)


def rows_of(start_ref, scr, first=0):
    for s in range(SEC):
        scr[first + 2 * s : first + 2 * s + 2, :] = start_ref[s]


def dot(a, b):
    return lax.dot_general(a, b, (((1,), (0,)), ((), ())), preferred_element_type=F32)


def dot_t(a, b):
    return lax.dot_general(a, b, (((1,), (1,)), ((), ())), preferred_element_type=F32)


def pack_first(
    patches, cand, offs, pairs, start, ra, rb, xa, xb, lower,
    scr, held, held_c, held_o, held_p, held_u, sems,
):
    sources = [(start, held_u), (pairs, held_p), (cand.at[6:8], held_c), (offs.at[6:8], held_o)]
    sources += [(patches.at[s : s + 8], held.at[s : s + 8]) for s in range(0, SEC, 8)]
    copies = [pltpu.make_async_copy(src, dst, sems.at[n]) for n, (src, dst) in enumerate(sources)]
    for copy in copies:
        copy.start()
    row, col = tile_place()
    off_a = jnp.where(col % 2 == 0, SIDE - 2, 0)
    j = iota((64, VT), 0)
    v = iota((64, VT), 1)
    off = jnp.where(j < 32, off_a, SIDE - 2 - off_a)
    source = (j % SIDE) * SIDE + off + (j % 32) // SIDE
    pick = (v == source).astype(BF)
    for copy in copies[:4]:
        copy.wait()
    rows_of(held_u, scr)
    hi, lo = two_parts(scr[...])
    for n, part in enumerate((hi[:, :HALF], hi[:, HALF:], lo[:, :HALF], lo[:, HALF:])):
        xa[256 + 16 * n : 272 + 16 * n, :] = part
        xb[256 + 16 * n : 272 + 16 * n, :] = part
    r = iota((16, HALF), 0)
    tied = jnp.zeros((16, HALF), F32)
    for p, (s, z) in enumerate(CROSS):
        lr, lc = local_place(held_c[s - 6, z], row, col)
        for n, plane in enumerate((lr, lc, held_o[s - 6, z, 0], held_o[s - 6, z, 1])):
            at = 512 + 64 * p + 16 * n
            plane = plane.astype(F32)
            lower[at : at + 16, :] = jnp.concatenate([plane[:, :HALF], plane[:, HALF:]], axis=0).astype(BF)
        tied = jnp.where(r == p, held_p[z : z + 1, s : s + 1].astype(F32), tied)
    lower[704:720, :] = tied.astype(BF)
    h, low = two_parts(scr[12:16, :])
    h, low = h.astype(F32), low.astype(F32)
    lower[720:736, :] = jnp.concatenate(
        [h[:, :HALF], h[:, HALF:], low[:, :HALF], low[:, HALF:]], axis=0
    ).astype(BF)
    first = jnp.where(row % 2 == 0, VT - 32, 0)
    for s in range(SEC):
        if s % 8 == 0:
            copies[4 + s // 8].wait()
        strips = dot(pick, held[s]).astype(BF)
        xa[s * 32 : s * 32 + 32, :] = strips[:32]
        xb[s * 32 : s * 32 + 32, :] = strips[32:]
        ra[s] = held[s, pl.ds(pl.multiple_of(first, 32), 32), :]
        rb[s] = held[s, pl.ds(pl.multiple_of(VT - 32 - first, 32), 32), :]
        if s >= 6:
            lower[(s - 6) * 256 : (s - 5) * 256, :] = held[s]


def pack_corners(start, xa, xb, ca, cb, scr):
    row, col = tile_place()
    off_a = jnp.where(row % 2 == 0, SIDE - 2, 0)
    both = jnp.concatenate([xa[0:256, :], xb[0:256, :]], axis=0)
    q = iota((128, 512), 0)
    k = iota((128, 512), 1)
    off = jnp.where(q < 64, off_a, SIDE - 2 - off_a)
    side = (q % 8) // 4
    buffer = jnp.where(col % 2 == 0, 1 - side, side)
    source = buffer * 256 + (q % 64) // 8 * 32 + (q % 4) // 2 * SIDE + off + q % 2
    corners = dot((k == source).astype(BF), both).astype(BF)
    ca[0:64, :] = corners[:64]
    cb[0:64, :] = corners[64:]
    rows_of(start, scr)
    hi, lo = two_parts(scr[...])
    even = row % 2 == 0
    for out, second in ((ca, even), (cb, jnp.logical_not(even))):

        @pl.when(second)
        def _():
            out[64:80, :] = hi[:, HALF:]
            out[80:96, :] = lo[:, HALF:]

        @pl.when(jnp.logical_not(second))
        def _():
            out[64:80, :] = hi[:, :HALF]
            out[80:96, :] = lo[:, :HALF]


def local_place(ids, row, col):
    tile = ids >> 8
    lr = (tile >> 2) * SIDE + ((ids >> 4) & 15) - row * SIDE
    lc = (tile & 3) * SIDE + (ids & 15) - col * SIDE
    return lr, lc


def picked(scores, slot, sub, vregs, score):
    for n, at in enumerate(vregs):
        got = jnp.take_along_axis(scores[at : at + 8], sub, axis=0)
        score = jnp.where(slot == n, got, score)
    return score


def inner_half(h, mine, own, left, right, lr, lc):
    table = jnp.concatenate([own[0:160] if h == 0 else own[96:256], left, right], axis=0)
    scores = dot_t(table, mine)
    i = lr if h == 0 else lr - 6
    outside_c = (lc < 0) | (lc >= SIDE)
    side = jnp.where(lc >= SIDE, 1, 0)
    slot = jnp.where(outside_c, 20 + side * 4 + (lc & 1) * 2 + (lr >> 3), i * 2 + (lc >> 3))
    slot = jnp.where((lr < 0) | (lr >= SIDE), -1, slot)
    sub = jnp.where(outside_c, lr & 7, lc & 7)
    return picked(scores, slot, sub, range(0, 224, 8), jnp.zeros((8, HALF), F32))


def half_targets(h, mine, score, strip, corner, lr, lc, off_r, off_c):
    rows, first = corner
    scores = dot_t(jnp.concatenate([strip, rows], axis=0), mine)
    outside_c = (lc < 0) | (lc >= SIDE)
    side = jnp.where(lc >= SIDE, 1, 0)
    beyond = lr < 0 if h == 0 else lr >= SIDE
    slot = jnp.where(outside_c, 4, (lr & 1) * 2 + (lc >> 3))
    slot = jnp.where(beyond, slot, -1)
    sub = jnp.where(outside_c, side * 4 + (lc & 1) * 2 + (lr & 1), lc & 7)
    score = picked(scores, slot, sub, (0, 8, 16, 24, 32 + first), score)
    score = score * PATCH ** (-0.5)
    e = jnp.exp(score - jnp.max(score, axis=0, keepdims=True))
    lane = iota((8, HALF), 1)
    step_r = (lr - (lane >> 4) - 8 * h).astype(F32) + off_r * (1.0 / PITCH)
    step_c = (lc - (lane & 15)).astype(F32) + off_c * (1.0 / PITCH)
    total = jnp.sum(e, axis=0, keepdims=True)
    t_r = jnp.sum(e * step_r, axis=0, keepdims=True) / total
    t_c = jnp.sum(e * step_c, axis=0, keepdims=True) / total
    return jnp.concatenate([t_r, t_c], axis=0)


def lower_planes(lower, p):
    return [lower[512 + 64 * p + 16 * n : 528 + 64 * p + 16 * n, :].astype(F32) for n in range(4)]


def inner_scores(patches, cand, xa, xb, lower, inner, left, right):
    row, col = tile_place()
    sort_halos(col, left, right, xa, xb)

    def sides(d):
        at = slice(d * 32, d * 32 + 32)
        return patches[d], left[at, :], right[at, :]

    def one(s, z):
        pieces = sides(s + z + 1)
        for h in range(2):
            lanes = slice(h * HALF, h * HALF + HALF)
            lr, lc = local_place(cand[s, z, :, lanes], row, col)
            inner[z, s, h] = inner_half(h, patches[s, lanes, :], *pieces, lr, lc)

    for s in range(SEC - 1):
        one(s, 0)
        if s < SEC - 2:
            one(s, 1)
    for p, (s, z) in enumerate(CROSS):
        pieces = sides(s + z + 1 - SEC)
        planes = lower_planes(lower, p)
        for h in range(2):
            mine = lower[256 * (s - 6) + HALF * h : 256 * (s - 6) + HALF * h + HALF, :]
            lr, lc = [plane[8 * h : 8 * h + 8].astype(I32) for plane in planes[:2]]
            inner[z, s + 2, h] = inner_half(h, mine, *pieces, lr, lc)


def lower_targets(start, ra, rb, ca, cb, lower, inner, sent):
    row, _ = tile_place()
    even = row % 2 == 0

    def pick(p, q, at):
        return jnp.where(even, q[at], p[at]), jnp.where(even, p[at], q[at])

    strips = [pick(ra, rb, d) for d in range(2)]
    corners = pick(ca, cb, slice(0, 16))
    for p, (s, z) in enumerate(CROSS):
        d = s + z + 1 - SEC
        mine = lower[256 * (s - 6) : 256 * (s - 6) + 256, :]
        planes = lower_planes(lower, p)
        for h in range(2):
            lanes = slice(h * HALF, h * HALF + HALF)
            lr, lc, off_r, off_c = [plane[8 * h : 8 * h + 8] for plane in planes]
            sent[2 * p : 2 * p + 2, lanes] = half_targets(
                h, mine[lanes, :], inner[z, s + 2, h], strips[d][h], (corners[h], 8 * d),
                lr.astype(I32), lc.astype(I32), off_r, off_c,
            )
    sent[6:8, :] = start[0]
    sent[8:10, :] = start[1]
    sent[10:16, :] = jnp.zeros((6, VT), F32)


def own_targets(
    patches, cand, offs, pairs, start, xa, xb, ra, rb, ca, cb, lower, inner, sent,
    p0, p1, u1, t0, t1, c0, c1, cross, low,
    left, right, above, below, top, bottom, tall,
):
    row, col = tile_place()
    stack = lax.axis_index("stack").astype(I32)
    sort_halos(col, left, right, xa, xb)
    sort_halos(row, above, below, ra, rb)
    sort_halos(row, top, bottom, ca, cb)

    def one(s, z, store, corner_first):
        d = s + z + 1

        for h in range(2):
            strip, src = (above, top) if h == 0 else (below, bottom)
            at = slice(d // 2 * 16, d // 2 * 16 + 16)
            lanes = slice(h * HALF, h * HALF + HALF)
            lr, lc = local_place(cand[s, z, :, lanes], row, col)
            store[s, :, lanes] = half_targets(
                h, patches[s, lanes, :], inner[z, s, h], strip[d], (src[at, :], corner_first), lr, lc,
                offs[s, z, 0, :, lanes].astype(F32), offs[s, z, 1, :, lanes].astype(F32),
            )

    for s in range(SEC - 1):
        one(s, 0, p0, 8 * ((s + 1) % 2))
        if s < SEC - 2:
            one(s, 1, p1, 8 * (s % 2))

    nothing = jnp.zeros((2, VT), F32)
    p0[7] = nothing
    p1[6] = nothing
    p1[7] = nothing

    tied = jnp.where(stack == 0, 0.0, lower[704:720, :].astype(F32))
    last = stack == lax.axis_size("stack") - 1
    for z, p, t, c in ((0, p0, t0, c0), (1, p1, t1, c1)):
        rows_of(p, t, 4)
        t[0:4, :] = jnp.zeros((4, VT), F32)
        c[0:4, :] = jnp.zeros((4, VT), F32)
        for s in range(SEC):
            here = jnp.full((2, VT), pairs[z, s], I32).astype(F32)
            if (s, z) in CROSS:
                n = CROSS.index((s, z))
                cross[2 * n : 2 * n + 2, :] = jnp.where(last, 0.0, here)
                here = nothing
            c[4 + 2 * s : 6 + 2 * s, :] = here
    cross[6:8, :] = nothing
    for p, (s, z) in enumerate(CROSS):
        t, c = ((t0, c0), (t1, c1))[z]
        at = 2 * (s - 6)
        t[at : at + 2, :] = sent[2 * p : 2 * p + 2, :]
        line = tied[p : p + 1, :]
        c[at : at + 2, :] = jnp.broadcast_to(jnp.concatenate([line, line], axis=1), (2, VT))
    ends = lower[720:736, :].astype(F32)
    tall[0:4, 0:HALF] = ends[0:4] + ends[8:12]
    tall[0:4, HALF:VT] = ends[4:8] + ends[12:16]
    rows_of(start, tall, 4)
    tall[20:24, :] = jnp.zeros((4, VT), F32)
    u = tall[4:20, :]

    def whole(ref):
        part = [ref[256 + 16 * n : 272 + 16 * n, :].astype(F32) for n in range(4)]
        return jnp.concatenate([part[0] + part[2], part[1] + part[3]], axis=1)

    def half(ref):
        part = ref[64:80, :].astype(F32) + ref[80:96, :].astype(F32)
        return jnp.concatenate([part, part], axis=1)

    plane = laplace(u, whole(left), whole(right), half(top), half(bottom), row, col)
    u1[...] = relaxed(u, tall, t0, t1, c0, c1, plane)
    base, own = tall[0:4, :], tall[4:8, :]
    near = jnp.concatenate([own[0:2], own[0:2]], axis=0)
    far = jnp.concatenate([jnp.zeros((2, VT), F32), own[2:4]], axis=0)
    got0 = jnp.concatenate([sent[0:2, :], sent[2:4, :]], axis=0)
    got1 = jnp.concatenate([nothing, sent[4:6, :]], axis=0)
    tied0 = jnp.concatenate([c1[0:2, :], c0[2:4, :]], axis=0)
    tied1 = jnp.concatenate([nothing, c1[2:4, :]], axis=0)
    low[0:4, :] = STEP * (tied0 * (near - base - got0) + tied1 * (far - base - got1))
    low[4:8, :] = jnp.zeros((4, VT), F32)


def sort_halos(index, first, second, p, q):
    @pl.when(index % 2 == 0)
    def _():
        first[...] = q[...]
        second[...] = p[...]

    @pl.when(index % 2 == 1)
    def _():
        first[...] = p[...]
        second[...] = q[...]


def laplace(u, left, right, above, below, row, col):
    lane = iota(u.shape, 1)
    b = lane & 15
    up = jnp.where(lane < SIDE, pltpu.roll(above, SIDE, 1), pltpu.roll(u, SIDE, 1))
    up = jnp.where((lane < SIDE) & (row == 0), u, up)
    down = jnp.where(lane >= VT - SIDE, pltpu.roll(below, VT - SIDE, 1), pltpu.roll(u, VT - SIDE, 1))
    down = jnp.where((lane >= VT - SIDE) & (row == COLS - 1), u, down)
    west = jnp.where(b == 0, pltpu.roll(left, VT - SIDE + 1, 1), pltpu.roll(u, 1, 1))
    west = jnp.where((b == 0) & (col == 0), u, west)
    east = jnp.where(b == SIDE - 1, pltpu.roll(right, SIDE - 1, 1), pltpu.roll(u, VT - 1, 1))
    east = jnp.where((b == SIDE - 1) & (col == COLS - 1), u, east)
    return ((down - u) - (u - up)) + ((east - u) - (u - west))


def relaxed(u, tall, t0, t1, c0, c1, plane):
    base = tall[0:20, :]
    s0 = c0[0:20, :] * (tall[2:22, :] - base - t0[0:20, :])
    s1 = c1[0:20, :] * (tall[4:24, :] - base - t1[0:20, :])
    zforce = s0[4:20] - s0[2:18] + s1[4:20] - s1[0:16]
    return u + STEP * (plane + zforce)


def cross_force(u, upper, got, cross):
    near, far = upper[0:2], upper[2:4]
    six = cross[0:2, :] * (near - u[12:14] - got[0:2, :])
    seven = cross[2:4, :] * (near - u[14:16] - got[2:4, :]) + cross[4:6, :] * (far - u[14:16] - got[4:6, :])
    return jnp.concatenate([jnp.zeros((12, VT), F32), six, seven], axis=0)


def first_round(start, part, got, cross, u1):
    u0 = jnp.concatenate([jnp.zeros((12, VT), F32), start[6], start[7]], axis=0)
    u1[...] = part[...] + STEP * cross_force(u0, got[6:10, :], got, cross)


def all_targets(p0, p1, got, targets):
    stack = lax.axis_index("stack").astype(I32)
    last = stack == lax.axis_size("stack") - 1
    for s in range(SEC):
        for z, p in ((0, p0), (1, p1)):
            if (s, z) in CROSS:
                n = CROSS.index((s, z))
                targets[s, z] = jnp.where(last, 0.0, got[2 * n : 2 * n + 2, :])
            else:
                targets[s, z] = p[s]


def second_round(u1, sa, sb, xa, xb, ra, rb, t0, t1, c0, c1, cross, low, got, out, tall):
    row, col = tile_place()
    stack = lax.axis_index("stack").astype(I32)
    col_even, row_even, stack_even = col % 2 == 0, row % 2 == 0, stack % 2 == 0
    u = u1[...]
    tall[4:20, :] = u
    below_rows = jnp.where(stack_even, sb[12:16, :], sa[12:16, :])
    upper = jnp.where(stack_even, sa[0:4, :], sb[0:4, :])
    tall[0:4, :] = below_rows + low[0:4, :]
    tall[20:24, :] = jnp.zeros((4, VT), F32)
    plane = laplace(
        u,
        jnp.where(col_even, xb[...], xa[...]),
        jnp.where(col_even, xa[...], xb[...]),
        jnp.where(row_even, rb[...], ra[...]),
        jnp.where(row_even, ra[...], rb[...]),
        row,
        col,
    )
    u = relaxed(u, tall, t0, t1, c0, c1, plane + cross_force(u, upper, got, cross))
    for s in range(SEC):
        out[s] = u[2 * s : 2 * s + 2]


def shape(*dims, dtype=F32):
    return jax.ShapeDtypeStruct(dims, dtype)


def call(body, outs, scratch, flops, n_in, smem=(), far=(), vmem=24 << 20):
    def space(n):
        return pltpu.SMEM if n in smem else pltpu.HBM if n in far else pltpu.VMEM

    return pl.pallas_call(
        body,
        out_shape=outs,
        in_specs=[pl.BlockSpec(memory_space=space(n)) for n in range(n_in)],
        out_specs=[pl.BlockSpec(memory_space=pltpu.VMEM) for _ in outs],
        scratch_shapes=scratch,
        name=body.__name__,
        compiler_params=pltpu.CompilerParams(vmem_limit_bytes=vmem),
        cost_estimate=pl.CostEstimate(flops=flops, bytes_accessed=1 << 20, transcendentals=0),
    )


def on_device(patches, cand, offs, pairs, start):
    pairs = pairs.T
    flat = pltpu.VMEM((16, VT), F32)
    held = [
        pltpu.VMEM((SEC, VT, PATCH), BF),
        pltpu.VMEM((2, 2, 8, VT), I32),
        pltpu.VMEM((2, 2, 2, 8, VT), I32),
        pltpu.VMEM((2, SEC), I32),
        pltpu.VMEM((SEC, 2, VT), F32),
        pltpu.SemaphoreType.DMA((4 + SEC,)),
    ]
    outs = [shape(SEC, 32, PATCH, dtype=BF)] * 2 + [shape(X_ROWS, PATCH, dtype=BF)] * 2 + [shape(S_ROWS, PATCH, dtype=BF)]
    ra, rb, xa, xb, lower = call(pack_first, outs, [flat] + held, 1 << 20, 5, far=(0, 1, 2, 3, 4), vmem=62 << 20)(
        patches, cand, offs, pairs, start
    )
    ra = swapped(ra, "tile", row_a)
    rb = swapped(rb, "tile", row_b)
    xa = swapped(xa, "tile", col_a)
    xb = swapped(xb, "tile", col_b)
    lower = swapped(lower, "stack", lambda i: (i + 1) % 16)
    ca, cb = call(pack_corners, [shape(C_ROWS, PATCH, dtype=BF)] * 2, [flat], 1 << 20, 3)(start, xa, xb)
    ca = swapped(ca, "tile", row_a)
    cb = swapped(cb, "tile", row_b)
    halos = (xa, xb, ra, rb, ca, cb)
    (inner,) = call(
        inner_scores, [shape(2, SEC + 2, 2, 8, HALF)], [pltpu.VMEM((X_ROWS, PATCH), BF)] * 2, 1 << 31, 5
    )(patches, cand, xa, xb, lower)
    (sent,) = call(lower_targets, [shape(16, VT)], [], 1 << 20, 7)(start, ra, rb, ca, cb, lower, inner)
    got = swapped(sent, "stack", lambda i: (i - 1) % 16)
    p0, p1, part, t0, t1, c0, c1, cross, low = call(
        own_targets,
        [shape(SEC, 2, VT)] * 2 + [shape(16, VT)] + [shape(24, VT)] * 4 + [shape(8, VT)] * 2,
        [pltpu.VMEM(a.shape, BF) for a in halos] + [pltpu.VMEM((24, VT), F32)],
        1 << 31,
        14,
        smem=(3,),
    )(patches, cand, offs, pairs, start, *halos, lower, inner, sent)
    stacked = [swapped(part, "stack", stack_a), swapped(part, "stack", stack_b)]
    (u1,) = call(first_round, [shape(16, VT)], [], 1 << 16, 4)(start, part, got, cross)
    moved = [swapped(u1, "tile", partner) for partner in (col_a, col_b, row_a, row_b)]
    (targets,) = call(all_targets, [shape(SEC, 2, 2, VT)], [], 1 << 20, 3)(p0, p1, got)
    (aligned,) = call(second_round, [shape(SEC, 2, VT)], [pltpu.VMEM((24, VT), F32)], 1 << 20, 14)(
        u1, *stacked, *moved, t0, t1, c0, c1, cross, low, got
    )
    return aligned, targets


def solution(mesh):
    placed = (
        P("stack", "tile", None),
        P("stack", None, None, "tile"),
        P("stack", None, None, None, "tile"),
        P("stack", None),
        P("stack", None, "tile"),
    )
    return jax.shard_map(
        on_device,
        mesh=mesh,
        in_specs=placed,
        out_specs=(P("stack", None, "tile"), P("stack", None, None, "tile")),
        check_vma=False,
    )
```

time: 264 us -> 38.3 us (0.15)
  the two profiles are of different devices: /device:TPU:88 before, /device:TPU:1 now
where the time goes in v2:
time: 38.3 us; the launch traced here: 38.2 us
  starting transfers between devices  27.5 us (72%)
  Pallas kernels  6.22 us (16%)
  waiting for transfers between devices  3.7 us (10%)
  between operations  0.76 us (2%)
    ppermute x14, starting transfers between devices, swapped(): lax.ppermute(block, axis, [(i, partner(i)) for i in range(lax.axis_size(a...  27.5 us
    ppermute x14, waiting for transfers between devices, swapped(): lax.ppermute(block, axis, [(i, partner(i)) for i in range(lax.axis_size(a...  3.7 us
    pallas_call x1, Pallas kernels, on_device(): call(pack_first, outs, [flat] + held, 1 << 20, 5, far=(0, 1, 2, 3, 4), vm...  2.23 us
    pallas_call x1, Pallas kernels, on_device(): call(own_targets, [shape(SEC, 2, VT)] * 2 + [shape(16, VT)] + [shape(24,...  1.39 us
  transfers between devices with their start and end apart: 14, of which 3 were waited for; matrix products, arithmetic and copies ran while one was open for 0% of the time, Pallas kernels for 8%

profile of v2, /device:TPU:1, one launch (start us, length us, event | category | flops | bytes accessed | tf_op | source)
XLA Modules:
  0.0 38.2 jit_solution(2814743292570316925)
XLA Ops:
  0.6 2.2 %pack_first.1 = (bf16[8,32,128]{2,1,0:T(8,128)(2,1)}, bf16[8,32,128]{2,1,0:T(8,128)(2,1)}, bf16[320,128]{1,0:T(8,128)(2,1)}, bf16[320,128]{1,0:T(8,128)(2,1)}, bf16[736,128]{1,0:T(8,128)(2,1)}) custom-call(bf16[8,256,128]{2,1,0:T(8,128)(2,1)} %patches.5, s32[8,2,8,256]{3,2,1,0:T(8,128)} %cand.5, s32[8,2,2,8,256]{4,3,2,1,0:T(8,128)} %offs.3, s32[2,8]{1,0:T(2,128)} %bitcast.1, ...), custom_call_target="tpu_custom_call" | custom-call | flops 1048576 | bytes 1048576 | tf_op jit(solution)/shard_map/pack_first/pallas_call | solution.py:461
  2.9 0.0 copy-start.3
  2.9 3.1 %collective-permute-start.6 = (bf16[736,128]{1,0:T(8,128)(2,1)}, bf16[736,128]{1,0:T(8,128)(2,1)S(1)}, u32[]{:S(2)}, u32[]{:S(2)}) collective-permute-start(bf16[736,128]{1,0:T(8,128)(2,1)} %get-tuple-element.24), channel_id=1, source_target_pairs={{0,16},{16,32},{32,48},{48,64},{64,80},{80,96},{96,112},{112,128},... | collective-permute-start | bytes 565256 | tf_op jit(solution)/shard_map/ppermute | solution.py:27
  6.0 1.2 %collective-permute-start = (bf16[320,128]{1,0:T(8,128)(2,1)}, bf16[320,128]{1,0:T(8,128)(2,1)S(1)}, u32[]{:S(2)}, u32[]{:S(2)}) collective-permute-start(bf16[320,128]{1,0:T(8,128)(2,1)} %get-tuple-element.18), channel_id=1, source_target_pairs={{0,1},{1,0},{2,3},{3,2},{4,5},{5,4},{6,7},{7,6},{8,9},{9,8},{10,11... | collective-permute-start | bytes 245768 | tf_op jit(solution)/shard_map/ppermute | solution.py:27
  7.2 1.8 %collective-permute-start.1 = (bf16[320,128]{1,0:T(8,128)(2,1)}, bf16[320,128]{1,0:T(8,128)(2,1)S(1)}, u32[]{:S(2)}, u32[]{:S(2)}) collective-permute-start(bf16[320,128]{1,0:T(8,128)(2,1)} %get-tuple-element.19), channel_id=1, source_target_pairs={{0,3},{1,2},{2,1},{3,0},{4,7},{5,6},{6,5},{7,4},{8,11},{9,10},{10,... | collective-permute-start | bytes 245768 | tf_op jit(solution)/shard_map/ppermute | solution.py:27
  9.0 3.0 %collective-permute-start.2 = (bf16[8,32,128]{2,1,0:T(8,128)(2,1)}, bf16[8,32,128]{2,1,0:T(8,128)(2,1)S(1)}, u32[]{:S(2)}, u32[]{:S(2)}) collective-permute-start(bf16[8,32,128]{2,1,0:T(8,128)(2,1)} %get-tuple-element.20), channel_id=1, source_target_pairs={{0,4},{1,5},{2,6},{3,7},{4,0},{5,1},{6,2},{7,3},{8,12},{9,13},{10,... | collective-permute-start | bytes 196616 | tf_op jit(solution)/shard_map/ppermute | solution.py:27
  12.0 3.3 %collective-permute-start.3 = (bf16[8,32,128]{2,1,0:T(8,128)(2,1)}, bf16[8,32,128]{2,1,0:T(8,128)(2,1)S(1)}, u32[]{:S(2)}, u32[]{:S(2)}) collective-permute-start(bf16[8,32,128]{2,1,0:T(8,128)(2,1)} %get-tuple-element.21), channel_id=1, source_target_pairs={{0,12},{1,13},{2,14},{3,15},{4,8},{5,9},{6,10},{7,11},{8,4},{9,5},... | collective-permute-start | bytes 196616 | tf_op jit(solution)/shard_map/ppermute | solution.py:27
  15.3 0.0 collective-permute-done.xa
  15.3 0.2 pack_corners.1
  15.6 1.3 %collective-permute-start.4 = (bf16[96,128]{1,0:T(8,128)(2,1)S(1)}, bf16[96,128]{1,0:T(8,128)(2,1)S(1)}, u32[]{:S(2)}, u32[]{:S(2)}) collective-permute-start(bf16[96,128]{1,0:T(8,128)(2,1)S(1)} %get-tuple-element.22), channel_id=1, source_target_pairs={{0,4},{1,5},{2,6},{3,7},{4,0},{5,1},{6,2},{7,3},{8,12},{9,13},{10,... | collective-permute-start | bytes 73736 | tf_op jit(solution)/shard_map/ppermute | solution.py:27
  16.8 2.6 %collective-permute-start.5 = (bf16[96,128]{1,0:T(8,128)(2,1)S(1)}, bf16[96,128]{1,0:T(8,128)(2,1)S(1)}, u32[]{:S(2)}, u32[]{:S(2)}) collective-permute-start(bf16[96,128]{1,0:T(8,128)(2,1)S(1)} %get-tuple-element.23), channel_id=1, source_target_pairs={{0,12},{1,13},{2,14},{3,15},{4,8},{5,9},{6,10},{7,11},{8,4},{9,5},... | collective-permute-start | bytes 73736 | tf_op jit(solution)/shard_map/ppermute | solution.py:27
  19.5 0.0 collective-permute-done.6.lower
  19.5 0.7 %inner_scores.1.inner = f32[2,10,2,8,128]{4,3,2,1,0:T(8,128)S(1)} custom-call(bf16[8,256,128]{2,1,0:T(8,128)(2,1)S(1)} %copy-done, s32[8,2,8,256]{3,2,1,0:T(8,128)S(1)} %copy-done.3, bf16[320,128]{1,0:T(8,128)(2,1)S(1)} %collective-permute-done.xa, bf16[320,128]{1,0:T(8,128)(2,1)S(1)} %collective-permute-done.1.xb, ...), custom_call_target="tpu_custom_call" | custom-call | flops 2147483648 | bytes 1048576 | tf_op jit(solution)/shard_map/inner_scores/pallas_call | solution.py:473
  20.2 0.0 copy-start.2
  20.3 0.0 copy-start.4
  20.3 0.0 collective-permute-done.3.rb
  20.3 1.4 %collective-permute-done.5.cb = bf16[96,128]{1,0:T(8,128)(2,1)S(1)} collective-permute-done((bf16[96,128]{1,0:T(8,128)(2,1)S(1)}, bf16[96,128]{1,0:T(8,128)(2,1)S(1)}, u32[]{:S(2)}, u32[]{:S(2)}) %collective-permute-start.5) | collective-permute-done | bytes 24608 | tf_op jit(solution)/shard_map/ppermute | solution.py:27
  21.7 0.3 lower_targets.1.sent
  22.0 2.0 %collective-permute-start.7 = (f32[16,256]{1,0:T(8,128)S(1)}, f32[16,256]{1,0:T(8,128)S(1)}, u32[]{:S(2)}, u32[]{:S(2)}) collective-permute-start(f32[16,256]{1,0:T(8,128)S(1)} %lower_targets.1.sent), channel_id=1, source_target_pairs={{0,240},{16,0},{32,16},{48,32},{64,48},{80,64},{96,80},{112,96},{1... | collective-permute-start | bytes 49160 | tf_op jit(solution)/shard_map/ppermute | solution.py:27
  24.0 1.4 %own_targets.1 = (f32[8,2,256]{2,1,0:T(2,128)S(1)}, f32[8,2,256]{2,1,0:T(2,128)S(1)}, f32[16,256]{1,0:T(8,128)S(1)}, f32[24,256]{1,0:T(8,128)S(1)}, f32[24,256]{...) custom-call(bf16[8,256,128]{2,1,0:T(8,128)(2,1)S(1)} %copy-done, ...), custom_call_target="tpu_custom_call" | custom-call | flops 2147483648 | bytes 1048576 | tf_op jit(solution)/shard_map/own_targets/pallas_call | solution.py:478
  25.4 0.7 %collective-permute-start.9 = (f32[16,256]{1,0:T(8,128)S(1)}, f32[16,256]{1,0:T(8,128)S(1)}, u32[]{:S(2)}, u32[]{:S(2)}) collective-permute-start(f32[16,256]{1,0:T(8,128)S(1)} %get-tuple-element.25.part), channel_id=1, source_target_pairs={{0,240},{16,32},{32,16},{48,64},{64,48},{80,96},{96,80},{112,128},... | collective-permute-start | bytes 49160 | tf_op jit(solution)/shard_map/ppermute | solution.py:27
  26.2 2.9 %collective-permute-start.8 = (f32[16,256]{1,0:T(8,128)S(1)}, f32[16,256]{1,0:T(8,128)S(1)}, u32[]{:S(2)}, u32[]{:S(2)}) collective-permute-start(f32[16,256]{1,0:T(8,128)S(1)} %get-tuple-element.25.part), channel_id=1, source_target_pairs={{0,16},{16,0},{32,48},{48,32},{64,80},{80,64},{96,112},{112,96},{1... | collective-permute-start | bytes 49160 | tf_op jit(solution)/shard_map/ppermute | solution.py:27
  29.1 0.0 collective-permute-done.7.got
  29.1 2.5 %collective-permute-start.13 = (f32[16,256]{1,0:T(8,128)S(1)}, f32[16,256]{1,0:T(8,128)S(1)}, u32[]{:S(2)}, u32[]{:S(2)}) collective-permute-start(f32[16,256]{1,0:T(8,128)S(1)} %first_round.1.u1), channel_id=1, source_target_pairs={{0,12},{1,13},{2,14},{3,15},{4,8},{5,9},{6,10},{7,11},{8,4},{9,5},... | collective-permute-start | bytes 49160 | tf_op jit(solution)/shard_map/ppermute | solution.py:27
  31.6 1.1 %collective-permute-start.12 = (f32[16,256]{1,0:T(8,128)S(1)}, f32[16,256]{1,0:T(8,128)S(1)}, u32[]{:S(2)}, u32[]{:S(2)}) collective-permute-start(f32[16,256]{1,0:T(8,128)S(1)} %first_round.1.u1), channel_id=1, source_target_pairs={{0,4},{1,5},{2,6},{3,7},{4,0},{5,1},{6,2},{7,3},{8,12},{9,13},{10,... | collective-permute-start | bytes 49160 | tf_op jit(solution)/shard_map/ppermute | solution.py:27
  32.7 1.8 %collective-permute-start.11 = (f32[16,256]{1,0:T(8,128)S(1)}, f32[16,256]{1,0:T(8,128)S(1)}, u32[]{:S(2)}, u32[]{:S(2)}) collective-permute-start(f32[16,256]{1,0:T(8,128)S(1)} %first_round.1.u1), channel_id=1, source_target_pairs={{0,3},{1,2},{2,1},{3,0},{4,7},{5,6},{6,5},{7,4},{8,11},{9,10},{10,... | collective-permute-start | bytes 49160 | tf_op jit(solution)/shard_map/ppermute | solution.py:27
  34.5 0.0 collective-permute-done.9.sb
  34.6 0.0 collective-permute-start.10
  34.6 0.6 %all_targets.1 = f32[8,2,2,256]{3,2,1,0:T(2,128)} custom-call(f32[8,2,256]{2,1,0:T(2,128)S(1)} %get-tuple-element.32.p0, f32[8,2,256]{2,1,0:T(2,128)S(1)} %get-tuple-element.33.p1, f32[16,256]{1,0:T(8,128)S(1)} %collective-permute-done.7.got), custom_call_target="tpu_custom_call" | custom-call | flops 1048576 | bytes 1048576 | tf_op jit(solution)/shard_map/all_targets/pallas_call | solution.py:489
  35.2 1.3 %collective-permute-done.11.xb = f32[16,256]{1,0:T(8,128)S(1)} collective-permute-done((f32[16,256]{1,0:T(8,128)S(1)}, f32[16,256]{1,0:T(8,128)S(1)}, u32[]{:S(2)}, u32[]{:S(2)}) %collective-permute-start.11) | collective-permute-done | bytes 16416 | tf_op jit(solution)/shard_map/ppermute | solution.py:27
  36.5 0.9 %collective-permute-done.10.xa = f32[16,256]{1,0:T(8,128)S(1)} collective-permute-done((f32[16,256]{1,0:T(8,128)S(1)}, f32[16,256]{1,0:T(8,128)S(1)}, u32[]{:S(2)}, u32[]{:S(2)}) %collective-permute-start.10) | collective-permute-done | bytes 16416 | tf_op jit(solution)/shard_map/ppermute | solution.py:27
  37.4 0.7 %second_round.1 = f32[8,2,256]{2,1,0:T(2,128)} custom-call(f32[16,256]{1,0:T(8,128)S(1)} %first_round.1.u1, f32[16,256]{1,0:T(8,128)S(1)} %collective-permute-done.8.sa, f32[16,256]{1,0:T(8,128)S(1)} %collective-permute-done.9.sb, f32[16,256]{1,0:T(8,128)S(1)} %collective-permute-done.10.xa, f32[16,256]{1,0:T(8,128)S(1)} %collective-permute-done.11.xb, ...), custom_call_target="tpu_custom_call" | custom-call | flops 1048576 | bytes 1048576 | tf_op jit(solution)/shard_map/second_round/pallas_call | solution.py:490
  (14 shorter events, 0.0 us)
Async XLA Ops:
  0.6 14.7 %copy-start.1 = (f32[8,2,256]{2,1,0:T(2,128)S(1)}, f32[8,2,256]{2,1,0:T(2,128)}, u32[]{:S(2)}) copy-start(f32[8,2,256]{2,1,0:T(2,128)} %start.9) | copy-start | bytes 49156
  0.6 18.9 %copy-start = (bf16[8,256,128]{2,1,0:T(8,128)(2,1)S(1)}, bf16[8,256,128]{2,1,0:T(8,128)(2,1)}, u32[]{:S(2)}) copy-start(bf16[8,256,128]{2,1,0:T(8,128)(2,1)} %patches.5) | copy-start | bytes 1572868
  2.9 16.6 %copy-start.3 = (s32[8,2,8,256]{3,2,1,0:T(8,128)S(1)}, s32[8,2,8,256]{3,2,1,0:T(8,128)}, u32[]{:S(2)}) copy-start(s32[8,2,8,256]{3,2,1,0:T(8,128)} %cand.5) | copy-start | bytes 393220
  2.9 16.6 %collective-permute-start.6 = (bf16[736,128]{1,0:T(8,128)(2,1)}, bf16[736,128]{1,0:T(8,128)(2,1)S(1)}, u32[]{:S(2)}, u32[]{:S(2)}) collective-permute-start(bf16[736,128]{1,0:T(8,128)(2,1)} %get-tuple-element.24), channel_id=1, source_target_pairs={{0,16},{16,32},{32,48},{48,64},{64,80},{80,96},{96,112},{112,128},... | collective-permute-start | bytes 565256 | tf_op jit(solution)/shard_map/ppermute | solution.py:27
  6.0 9.3 %collective-permute-start = (bf16[320,128]{1,0:T(8,128)(2,1)}, bf16[320,128]{1,0:T(8,128)(2,1)S(1)}, u32[]{:S(2)}, u32[]{:S(2)}) collective-permute-start(bf16[320,128]{1,0:T(8,128)(2,1)} %get-tuple-element.18), channel_id=1, source_target_pairs={{0,1},{1,0},{2,3},{3,2},{4,5},{5,4},{6,7},{7,6},{8,9},{9,8},{10,11... | collective-permute-start | bytes 245768 | tf_op jit(solution)/shard_map/ppermute | solution.py:27
  7.2 8.1 %collective-permute-start.1 = (bf16[320,128]{1,0:T(8,128)(2,1)}, bf16[320,128]{1,0:T(8,128)(2,1)S(1)}, u32[]{:S(2)}, u32[]{:S(2)}) collective-permute-start(bf16[320,128]{1,0:T(8,128)(2,1)} %get-tuple-element.19), channel_id=1, source_target_pairs={{0,3},{1,2},{2,1},{3,0},{4,7},{5,6},{6,5},{7,4},{8,11},{9,10},{10,... | collective-permute-start | bytes 245768 | tf_op jit(solution)/shard_map/ppermute | solution.py:27
  9.0 11.2 %collective-permute-start.2 = (bf16[8,32,128]{2,1,0:T(8,128)(2,1)}, bf16[8,32,128]{2,1,0:T(8,128)(2,1)S(1)}, u32[]{:S(2)}, u32[]{:S(2)}) collective-permute-start(bf16[8,32,128]{2,1,0:T(8,128)(2,1)} %get-tuple-element.20), channel_id=1, source_target_pairs={{0,4},{1,5},{2,6},{3,7},{4,0},{5,1},{6,2},{7,3},{8,12},{9,13},{10,... | collective-permute-start | bytes 196616 | tf_op jit(solution)/shard_map/ppermute | solution.py:27
  12.0 8.3 %collective-permute-start.3 = (bf16[8,32,128]{2,1,0:T(8,128)(2,1)}, bf16[8,32,128]{2,1,0:T(8,128)(2,1)S(1)}, u32[]{:S(2)}, u32[]{:S(2)}) collective-permute-start(bf16[8,32,128]{2,1,0:T(8,128)(2,1)} %get-tuple-element.21), channel_id=1, source_target_pairs={{0,12},{1,13},{2,14},{3,15},{4,8},{5,9},{6,10},{7,11},{8,4},{9,5},... | collective-permute-start | bytes 196616 | tf_op jit(solution)/shard_map/ppermute | solution.py:27
  15.6 4.7 %collective-permute-start.4 = (bf16[96,128]{1,0:T(8,128)(2,1)S(1)}, bf16[96,128]{1,0:T(8,128)(2,1)S(1)}, u32[]{:S(2)}, u32[]{:S(2)}) collective-permute-start(bf16[96,128]{1,0:T(8,128)(2,1)S(1)} %get-tuple-element.22), channel_id=1, source_target_pairs={{0,4},{1,5},{2,6},{3,7},{4,0},{5,1},{6,2},{7,3},{8,12},{9,13},{10,... | collective-permute-start | bytes 73736 | tf_op jit(solution)/shard_map/ppermute | solution.py:27
  16.8 4.9 %collective-permute-start.5 = (bf16[96,128]{1,0:T(8,128)(2,1)S(1)}, bf16[96,128]{1,0:T(8,128)(2,1)S(1)}, u32[]{:S(2)}, u32[]{:S(2)}) collective-permute-start(bf16[96,128]{1,0:T(8,128)(2,1)S(1)} %get-tuple-element.23), channel_id=1, source_target_pairs={{0,12},{1,13},{2,14},{3,15},{4,8},{5,9},{6,10},{7,11},{8,4},{9,5},... | collective-permute-start | bytes 73736 | tf_op jit(solution)/shard_map/ppermute | solution.py:27
  20.2 3.8 %copy-start.2 = (s32[8,2,2,8,256]{4,3,2,1,0:T(8,128)S(1)}, s32[8,2,2,8,256]{4,3,2,1,0:T(8,128)}, u32[]{:S(2)}) copy-start(s32[8,2,2,8,256]{4,3,2,1,0:T(8,128)} %offs.3) | copy-start | bytes 786436
  20.3 3.8 %copy-start.4 = (s32[8,2]{0,1:T(2,128)S(1)}, s32[8,2]{0,1:T(2,128)}, u32[]{:S(2)}) copy-start(s32[8,2]{0,1:T(2,128)} %param.8) | copy-start | bytes 196
  22.0 7.1 %collective-permute-start.7 = (f32[16,256]{1,0:T(8,128)S(1)}, f32[16,256]{1,0:T(8,128)S(1)}, u32[]{:S(2)}, u32[]{:S(2)}) collective-permute-start(f32[16,256]{1,0:T(8,128)S(1)} %lower_targets.1.sent), channel_id=1, source_target_pairs={{0,240},{16,0},{32,16},{48,32},{64,48},{80,64},{96,80},{112,96},{1... | collective-permute-start | bytes 49160 | tf_op jit(solution)/shard_map/ppermute | solution.py:27
  25.4 9.1 %collective-permute-start.9 = (f32[16,256]{1,0:T(8,128)S(1)}, f32[16,256]{1,0:T(8,128)S(1)}, u32[]{:S(2)}, u32[]{:S(2)}) collective-permute-start(f32[16,256]{1,0:T(8,128)S(1)} %get-tuple-element.25.part), channel_id=1, source_target_pairs={{0,240},{16,32},{32,16},{48,64},{64,48},{80,96},{96,80},{112,128},... | collective-permute-start | bytes 49160 | tf_op jit(solution)/shard_map/ppermute | solution.py:27
  26.2 9.0 %collective-permute-start.8 = (f32[16,256]{1,0:T(8,128)S(1)}, f32[16,256]{1,0:T(8,128)S(1)}, u32[]{:S(2)}, u32[]{:S(2)}) collective-permute-start(f32[16,256]{1,0:T(8,128)S(1)} %get-tuple-element.25.part), channel_id=1, source_target_pairs={{0,16},{16,0},{32,48},{48,32},{64,80},{80,64},{96,112},{112,96},{1... | collective-permute-start | bytes 49160 | tf_op jit(solution)/shard_map/ppermute | solution.py:27
  29.1 6.1 %collective-permute-start.13 = (f32[16,256]{1,0:T(8,128)S(1)}, f32[16,256]{1,0:T(8,128)S(1)}, u32[]{:S(2)}, u32[]{:S(2)}) collective-permute-start(f32[16,256]{1,0:T(8,128)S(1)} %first_round.1.u1), channel_id=1, source_target_pairs={{0,12},{1,13},{2,14},{3,15},{4,8},{5,9},{6,10},{7,11},{8,4},{9,5},... | collective-permute-start | bytes 49160 | tf_op jit(solution)/shard_map/ppermute | solution.py:27
  31.6 3.6 %collective-permute-start.12 = (f32[16,256]{1,0:T(8,128)S(1)}, f32[16,256]{1,0:T(8,128)S(1)}, u32[]{:S(2)}, u32[]{:S(2)}) collective-permute-start(f32[16,256]{1,0:T(8,128)S(1)} %first_round.1.u1), channel_id=1, source_target_pairs={{0,4},{1,5},{2,6},{3,7},{4,0},{5,1},{6,2},{7,3},{8,12},{9,13},{10,... | collective-permute-start | bytes 49160 | tf_op jit(solution)/shard_map/ppermute | solution.py:27
  32.7 3.8 %collective-permute-start.11 = (f32[16,256]{1,0:T(8,128)S(1)}, f32[16,256]{1,0:T(8,128)S(1)}, u32[]{:S(2)}, u32[]{:S(2)}) collective-permute-start(f32[16,256]{1,0:T(8,128)S(1)} %first_round.1.u1), channel_id=1, source_target_pairs={{0,3},{1,2},{2,1},{3,0},{4,7},{5,6},{6,5},{7,4},{8,11},{9,10},{10,... | collective-permute-start | bytes 49160 | tf_op jit(solution)/shard_map/ppermute | solution.py:27
  34.6 2.9 %collective-permute-start.10 = (f32[16,256]{1,0:T(8,128)S(1)}, f32[16,256]{1,0:T(8,128)S(1)}, u32[]{:S(2)}, u32[]{:S(2)}) collective-permute-start(f32[16,256]{1,0:T(8,128)S(1)} %first_round.1.u1), channel_id=1, source_target_pairs={{0,1},{1,0},{2,3},{3,2},{4,5},{5,4},{6,7},{7,6},{8,9},{9,8},{10,11... | collective-permute-start | bytes 49160 | tf_op jit(solution)/shard_map/ppermute | solution.py:27

commit v3 on v2

--- a/solution.py
+++ b/solution.py
@@ -79,7 +79,7 @@
 
 
 def pack_first(
-    patches, cand, offs, pairs, start, ra, rb, xa, xb, lower,
+    patches, cand, offs, pairs, start, rb, ra, xb, xa, lower,
     scr, held, held_c, held_o, held_p, held_u, sems,
 ):
     sources = [(start, held_u), (pairs, held_p), (cand.at[6:8], held_c), (offs.at[6:8], held_o)]
@@ -129,7 +129,7 @@
             lower[(s - 6) * 256 : (s - 5) * 256, :] = held[s]
 
 
-def pack_corners(start, xa, xb, ca, cb, scr):
+def pack_corners(start, xb, xa, cb, ca, scr):
     row, col = tile_place()
     off_a = jnp.where(row % 2 == 0, SIDE - 2, 0)
     both = jnp.concatenate([xa[0:256, :], xb[0:256, :]], axis=0)
@@ -209,7 +209,7 @@
     return [lower[512 + 64 * p + 16 * n : 528 + 64 * p + 16 * n, :].astype(F32) for n in range(4)]
 
 
-def inner_scores(patches, cand, xa, xb, lower, inner, left, right):
+def inner_scores(patches, cand, xb, xa, lower, inner, left, right):
     row, col = tile_place()
     sort_halos(col, left, right, xa, xb)
 
@@ -237,7 +237,7 @@
             inner[z, s + 2, h] = inner_half(h, mine, *pieces, lr, lc)
 
 
-def lower_targets(start, ra, rb, ca, cb, lower, inner, sent):
+def lower_targets(start, rb, ra, cb, ca, lower, inner, sent):
     row, _ = tile_place()
     even = row % 2 == 0
 
@@ -263,7 +263,7 @@
 
 
 def own_targets(
-    patches, cand, offs, pairs, start, xa, xb, ra, rb, ca, cb, lower, inner, sent,
+    patches, cand, offs, pairs, start, xb, xa, rb, ra, cb, ca, lower, inner, sent,
     p0, p1, u1, t0, t1, c0, c1, cross, low,
     left, right, above, below, top, bottom, tall,
 ):
@@ -402,7 +402,7 @@
                 targets[s, z] = p[s]
 
 
-def second_round(u1, sa, sb, xa, xb, ra, rb, t0, t1, c0, c1, cross, low, got, out, tall):
+def second_round(u1, sb, sa, xa, xb, ra, rb, t0, t1, c0, c1, cross, low, got, out, tall):
     row, col = tile_place()
     stack = lax.axis_index("stack").astype(I32)
     col_even, row_even, stack_even = col % 2 == 0, row % 2 == 0, stack % 2 == 0
@@ -458,22 +458,22 @@
         pltpu.SemaphoreType.DMA((4 + SEC,)),
     ]
     outs = [shape(SEC, 32, PATCH, dtype=BF)] * 2 + [shape(X_ROWS, PATCH, dtype=BF)] * 2 + [shape(S_ROWS, PATCH, dtype=BF)]
-    ra, rb, xa, xb, lower = call(pack_first, outs, [flat] + held, 1 << 20, 5, far=(0, 1, 2, 3, 4), vmem=62 << 20)(
+    rb, ra, xb, xa, lower = call(pack_first, outs, [flat] + held, 1 << 20, 5, far=(0, 1, 2, 3, 4), vmem=62 << 20)(
         patches, cand, offs, pairs, start
     )
+    rb = swapped(rb, "tile", row_b)
     ra = swapped(ra, "tile", row_a)
-    rb = swapped(rb, "tile", row_b)
     xa = swapped(xa, "tile", col_a)
     xb = swapped(xb, "tile", col_b)
     lower = swapped(lower, "stack", lambda i: (i + 1) % 16)
-    ca, cb = call(pack_corners, [shape(C_ROWS, PATCH, dtype=BF)] * 2, [flat], 1 << 20, 3)(start, xa, xb)
+    cb, ca = call(pack_corners, [shape(C_ROWS, PATCH, dtype=BF)] * 2, [flat], 1 << 20, 3)(start, xb, xa)
+    cb = swapped(cb, "tile", row_b)
     ca = swapped(ca, "tile", row_a)
-    cb = swapped(cb, "tile", row_b)
-    halos = (xa, xb, ra, rb, ca, cb)
+    halos = (xb, xa, rb, ra, cb, ca)
     (inner,) = call(
         inner_scores, [shape(2, SEC + 2, 2, 8, HALF)], [pltpu.VMEM((X_ROWS, PATCH), BF)] * 2, 1 << 31, 5
-    )(patches, cand, xa, xb, lower)
-    (sent,) = call(lower_targets, [shape(16, VT)], [], 1 << 20, 7)(start, ra, rb, ca, cb, lower, inner)
+    )(patches, cand, xb, xa, lower)
+    (sent,) = call(lower_targets, [shape(16, VT)], [], 1 << 20, 7)(start, rb, ra, cb, ca, lower, inner)
     got = swapped(sent, "stack", lambda i: (i - 1) % 16)
     p0, p1, part, t0, t1, c0, c1, cross, low = call(
         own_targets,
@@ -483,12 +483,13 @@
         14,
         smem=(3,),
     )(patches, cand, offs, pairs, start, *halos, lower, inner, sent)
-    stacked = [swapped(part, "stack", stack_a), swapped(part, "stack", stack_b)]
+    sa = swapped(part, "stack", stack_a)
+    sb = swapped(part, "stack", stack_b)
     (u1,) = call(first_round, [shape(16, VT)], [], 1 << 16, 4)(start, part, got, cross)
     moved = [swapped(u1, "tile", partner) for partner in (col_a, col_b, row_a, row_b)]
     (targets,) = call(all_targets, [shape(SEC, 2, 2, VT)], [], 1 << 20, 3)(p0, p1, got)
     (aligned,) = call(second_round, [shape(SEC, 2, VT)], [pltpu.VMEM((24, VT), F32)], 1 << 20, 14)(
-        u1, *stacked, *moved, t0, t1, c0, c1, cross, low, got
+        u1, sb, sa, *moved, t0, t1, c0, c1, cross, low, got
     )
     return aligned, targets
 

time: 38.3 us -> 35.6 us (0.930)
  the two profiles are of different devices: /device:TPU:1 before, /device:TPU:2 now
where the time goes in v3:
time: 35.6 us; the launch traced here: 35 us
  starting transfers between devices  24.4 us (69%)
  Pallas kernels  6.24 us (18%)
  waiting for transfers between devices  3.62 us (10%)
  between operations  0.76 us (2%)
    ppermute x14, starting transfers between devices, swapped(): lax.ppermute(block, axis, [(i, partner(i)) for i in range(lax.axis_size(a...  24.4 us
    ppermute x14, waiting for transfers between devices, swapped(): lax.ppermute(block, axis, [(i, partner(i)) for i in range(lax.axis_size(a...  3.62 us
    pallas_call x1, Pallas kernels, on_device(): call(pack_first, outs, [flat] + held, 1 << 20, 5, far=(0, 1, 2, 3, 4), vm...  2.24 us
    pallas_call x1, Pallas kernels, on_device(): call(own_targets, [shape(SEC, 2, VT)] * 2 + [shape(16, VT)] + [shape(24,...  1.39 us
    pallas_call x1, Pallas kernels, on_device(): call(inner_scores, [shape(2, SEC + 2, 2, 8, HALF)], [pltpu.VMEM((X_ROWS,...  0.75 us
    pallas_call x1, Pallas kernels, on_device(): call(second_round, [shape(SEC, 2, VT)], [pltpu.VMEM((24, VT), F32)], 1 <<...  0.73 us
  transfers between devices with their start and end apart: 14, of which 6 were waited for; matrix products, arithmetic and copies ran while one was open for 0% of the time, Pallas kernels for 9%

profile of v3, /device:TPU:2, one launch (start us, length us, event | category | flops | bytes accessed | tf_op | source)
XLA Modules:
  0.0 35.0 jit_solution(16194380707161658122)
XLA Ops:
  0.6 2.2 %pack_first.1 = (bf16[8,32,128]{2,1,0:T(8,128)(2,1)}, bf16[8,32,128]{2,1,0:T(8,128)(2,1)}, bf16[320,128]{1,0:T(8,128)(2,1)}, bf16[320,128]{1,0:T(8,128)(2,1)}, bf16[736,128]{1,0:T(8,128)(2,1)}) custom-call(bf16[8,256,128]{2,1,0:T(8,128)(2,1)} %patches.5, s32[8,2,8,256]{3,2,1,0:T(8,128)} %cand.5, s32[8,2,2,8,256]{4,3,2,1,0:T(8,128)} %offs.3, s32[2,8]{1,0:T(2,128)} %bitcast.1, ...), custom_call_target="tpu_custom_call" | custom-call | flops 1048576 | bytes 1048576 | tf_op jit(solution)/shard_map/pack_first/pallas_call | solution.py:461
  2.9 0.0 copy-start.3
  2.9 0.1 collective-permute-start.6
  3.0 1.6 %collective-permute-start = (bf16[320,128]{1,0:T(8,128)(2,1)}, bf16[320,128]{1,0:T(8,128)(2,1)S(1)}, u32[]{:S(2)}, u32[]{:S(2)}) collective-permute-start(bf16[320,128]{1,0:T(8,128)(2,1)} %get-tuple-element.18), channel_id=1, source_target_pairs={{0,3},{1,2},{2,1},{3,0},{4,7},{5,6},{6,5},{7,4},{8,11},{9,10},{10,... | collective-permute-start | bytes 245768 | tf_op jit(solution)/shard_map/ppermute | solution.py:27
  4.6 1.8 %collective-permute-start.1 = (bf16[320,128]{1,0:T(8,128)(2,1)}, bf16[320,128]{1,0:T(8,128)(2,1)S(1)}, u32[]{:S(2)}, u32[]{:S(2)}) collective-permute-start(bf16[320,128]{1,0:T(8,128)(2,1)} %get-tuple-element.19), channel_id=1, source_target_pairs={{0,1},{1,0},{2,3},{3,2},{4,5},{5,4},{6,7},{7,6},{8,9},{9,8},{10,11... | collective-permute-start | bytes 245768 | tf_op jit(solution)/shard_map/ppermute | solution.py:27
  6.4 6.3 %collective-permute-start.2 = (bf16[8,32,128]{2,1,0:T(8,128)(2,1)}, bf16[8,32,128]{2,1,0:T(8,128)(2,1)S(1)}, u32[]{:S(2)}, u32[]{:S(2)}) collective-permute-start(bf16[8,32,128]{2,1,0:T(8,128)(2,1)} %get-tuple-element.20), channel_id=1, source_target_pairs={{0,12},{1,13},{2,14},{3,15},{4,8},{5,9},{6,10},{7,11},{8,4},{9,5},... | collective-permute-start | bytes 196616 | tf_op jit(solution)/shard_map/ppermute | solution.py:27
  12.7 1.5 %collective-permute-start.3 = (bf16[8,32,128]{2,1,0:T(8,128)(2,1)}, bf16[8,32,128]{2,1,0:T(8,128)(2,1)S(1)}, u32[]{:S(2)}, u32[]{:S(2)}) collective-permute-start(bf16[8,32,128]{2,1,0:T(8,128)(2,1)} %get-tuple-element.21), channel_id=1, source_target_pairs={{0,4},{1,5},{2,6},{3,7},{4,0},{5,1},{6,2},{7,3},{8,12},{9,13},{10,... | collective-permute-start | bytes 196616 | tf_op jit(solution)/shard_map/ppermute | solution.py:27
  14.1 0.0 collective-permute-done.xb
  14.1 0.0 collective-permute-done.1.xa
  14.1 0.2 pack_corners.1
  14.4 2.2 %collective-permute-start.4 = (bf16[96,128]{1,0:T(8,128)(2,1)S(1)}, bf16[96,128]{1,0:T(8,128)(2,1)S(1)}, u32[]{:S(2)}, u32[]{:S(2)}) collective-permute-start(bf16[96,128]{1,0:T(8,128)(2,1)S(1)} %get-tuple-element.22), channel_id=1, source_target_pairs={{0,12},{1,13},{2,14},{3,15},{4,8},{5,9},{6,10},{7,11},{8,4},{9,5},... | collective-permute-start | bytes 73736 | tf_op jit(solution)/shard_map/ppermute | solution.py:27
  16.6 1.5 %collective-permute-start.5 = (bf16[96,128]{1,0:T(8,128)(2,1)S(1)}, bf16[96,128]{1,0:T(8,128)(2,1)S(1)}, u32[]{:S(2)}, u32[]{:S(2)}) collective-permute-start(bf16[96,128]{1,0:T(8,128)(2,1)S(1)} %get-tuple-element.23), channel_id=1, source_target_pairs={{0,4},{1,5},{2,6},{3,7},{4,0},{5,1},{6,2},{7,3},{8,12},{9,13},{10,... | collective-permute-start | bytes 73736 | tf_op jit(solution)/shard_map/ppermute | solution.py:27
  18.0 0.8 %inner_scores.1.inner = f32[2,10,2,8,128]{4,3,2,1,0:T(8,128)S(1)} custom-call(bf16[8,256,128]{2,1,0:T(8,128)(2,1)S(1)} %copy-done, s32[8,2,8,256]{3,2,1,0:T(8,128)S(1)} %copy-done.3, bf16[320,128]{1,0:T(8,128)(2,1)S(1)} %collective-permute-done.xb, bf16[320,128]{1,0:T(8,128)(2,1)S(1)} %collective-permute-done.1.xa, ...), custom_call_target="tpu_custom_call" | custom-call | flops 2147483648 | bytes 1048576 | tf_op jit(solution)/shard_map/inner_scores/pallas_call | solution.py:473
  18.8 0.0 copy-start.2
  18.8 0.0 copy-start.4
  18.8 0.6 %collective-permute-done.3.ra = bf16[8,32,128]{2,1,0:T(8,128)(2,1)S(1)} collective-permute-done((bf16[8,32,128]{2,1,0:T(8,128)(2,1)}, bf16[8,32,128]{2,1,0:T(8,128)(2,1)S(1)}, u32[]{:S(2)}, u32[]{:S(2)}) %collective-permute-start.3) | collective-permute-done | bytes 65568 | tf_op jit(solution)/shard_map/ppermute | solution.py:27
  19.5 1.0 %collective-permute-done.4.cb = bf16[96,128]{1,0:T(8,128)(2,1)S(1)} collective-permute-done((bf16[96,128]{1,0:T(8,128)(2,1)S(1)}, bf16[96,128]{1,0:T(8,128)(2,1)S(1)}, u32[]{:S(2)}, u32[]{:S(2)}) %collective-permute-start.4) | collective-permute-done | bytes 24608 | tf_op jit(solution)/shard_map/ppermute | solution.py:27
  20.4 0.9 %collective-permute-done.5.ca = bf16[96,128]{1,0:T(8,128)(2,1)S(1)} collective-permute-done((bf16[96,128]{1,0:T(8,128)(2,1)S(1)}, bf16[96,128]{1,0:T(8,128)(2,1)S(1)}, u32[]{:S(2)}, u32[]{:S(2)}) %collective-permute-start.5) | collective-permute-done | bytes 24608 | tf_op jit(solution)/shard_map/ppermute | solution.py:27
  21.3 0.3 lower_targets.1.sent
  21.6 1.0 %collective-permute-start.7 = (f32[16,256]{1,0:T(8,128)S(1)}, f32[16,256]{1,0:T(8,128)S(1)}, u32[]{:S(2)}, u32[]{:S(2)}) collective-permute-start(f32[16,256]{1,0:T(8,128)S(1)} %lower_targets.1.sent), channel_id=1, source_target_pairs={{0,240},{16,0},{32,16},{48,32},{64,48},{80,64},{96,80},{112,96},{1... | collective-permute-start | bytes 49160 | tf_op jit(solution)/shard_map/ppermute | solution.py:27
  22.6 1.4 %own_targets.1 = (f32[8,2,256]{2,1,0:T(2,128)S(1)}, f32[8,2,256]{2,1,0:T(2,128)S(1)}, f32[16,256]{1,0:T(8,128)S(1)}, f32[24,256]{1,0:T(8,128)S(1)}, f32[24,256]{...) custom-call(bf16[8,256,128]{2,1,0:T(8,128)(2,1)S(1)} %copy-done, ...), custom_call_target="tpu_custom_call" | custom-call | flops 2147483648 | bytes 1048576 | tf_op jit(solution)/shard_map/own_targets/pallas_call | solution.py:478
  24.0 0.1 collective-permute-start.9
  24.1 2.5 %collective-permute-start.8 = (f32[16,256]{1,0:T(8,128)S(1)}, f32[16,256]{1,0:T(8,128)S(1)}, u32[]{:S(2)}, u32[]{:S(2)}) collective-permute-start(f32[16,256]{1,0:T(8,128)S(1)} %get-tuple-element.25.part), channel_id=1, source_target_pairs={{0,240},{16,32},{32,16},{48,64},{64,48},{80,96},{96,80},{112,128},... | collective-permute-start | bytes 49160 | tf_op jit(solution)/shard_map/ppermute | solution.py:27
  26.6 0.0 collective-permute-done.7.got
  26.7 2.3 %collective-permute-start.13 = (f32[16,256]{1,0:T(8,128)S(1)}, f32[16,256]{1,0:T(8,128)S(1)}, u32[]{:S(2)}, u32[]{:S(2)}) collective-permute-start(f32[16,256]{1,0:T(8,128)S(1)} %first_round.1.u1), channel_id=1, source_target_pairs={{0,12},{1,13},{2,14},{3,15},{4,8},{5,9},{6,10},{7,11},{8,4},{9,5},... | collective-permute-start | bytes 49160 | tf_op jit(solution)/shard_map/ppermute | solution.py:27
  29.0 1.5 %collective-permute-start.12 = (f32[16,256]{1,0:T(8,128)S(1)}, f32[16,256]{1,0:T(8,128)S(1)}, u32[]{:S(2)}, u32[]{:S(2)}) collective-permute-start(f32[16,256]{1,0:T(8,128)S(1)} %first_round.1.u1), channel_id=1, source_target_pairs={{0,4},{1,5},{2,6},{3,7},{4,0},{5,1},{6,2},{7,3},{8,12},{9,13},{10,... | collective-permute-start | bytes 49160 | tf_op jit(solution)/shard_map/ppermute | solution.py:27
  30.5 2.1 %collective-permute-start.10 = (f32[16,256]{1,0:T(8,128)S(1)}, f32[16,256]{1,0:T(8,128)S(1)}, u32[]{:S(2)}, u32[]{:S(2)}) collective-permute-start(f32[16,256]{1,0:T(8,128)S(1)} %first_round.1.u1), channel_id=1, source_target_pairs={{0,1},{1,0},{2,3},{3,2},{4,5},{5,4},{6,7},{7,6},{8,9},{9,8},{10,11... | collective-permute-start | bytes 49160 | tf_op jit(solution)/shard_map/ppermute | solution.py:27
  32.6 0.6 %all_targets.1 = f32[8,2,2,256]{3,2,1,0:T(2,128)} custom-call(f32[8,2,256]{2,1,0:T(2,128)S(1)} %get-tuple-element.32.p0, f32[8,2,256]{2,1,0:T(2,128)S(1)} %get-tuple-element.33.p1, f32[16,256]{1,0:T(8,128)S(1)} %collective-permute-done.7.got), custom_call_target="tpu_custom_call" | custom-call | flops 1048576 | bytes 1048576 | tf_op jit(solution)/shard_map/all_targets/pallas_call | solution.py:490
  33.2 0.4 %collective-permute-done.12.ra = f32[16,256]{1,0:T(8,128)S(1)} collective-permute-done((f32[16,256]{1,0:T(8,128)S(1)}, f32[16,256]{1,0:T(8,128)S(1)}, u32[]{:S(2)}, u32[]{:S(2)}) %collective-permute-start.12) | collective-permute-done | bytes 16416 | tf_op jit(solution)/shard_map/ppermute | solution.py:27
  33.6 0.6 %collective-permute-done.11.xb = f32[16,256]{1,0:T(8,128)S(1)} collective-permute-done((f32[16,256]{1,0:T(8,128)S(1)}, f32[16,256]{1,0:T(8,128)S(1)}, u32[]{:S(2)}, u32[]{:S(2)}) %collective-permute-start.11) | collective-permute-done | bytes 16416 | tf_op jit(solution)/shard_map/ppermute | solution.py:27
  34.2 0.1 collective-permute-done.10.xa
  34.3 0.7 %second_round.1 = f32[8,2,256]{2,1,0:T(2,128)} custom-call(f32[16,256]{1,0:T(8,128)S(1)} %first_round.1.u1, f32[16,256]{1,0:T(8,128)S(1)} %collective-permute-done.8.sb, f32[16,256]{1,0:T(8,128)S(1)} %collective-permute-done.9.sa, f32[16,256]{1,0:T(8,128)S(1)} %collective-permute-done.10.xa, f32[16,256]{1,0:T(8,128)S(1)} %collective-permute-done.11.xb, ...), custom_call_target="tpu_custom_call" | custom-call | flops 1048576 | bytes 1048576 | tf_op jit(solution)/shard_map/second_round/pallas_call | solution.py:491
  (14 shorter events, 0.0 us)
Async XLA Ops:
  0.6 13.5 %copy-start.1 = (f32[8,2,256]{2,1,0:T(2,128)S(1)}, f32[8,2,256]{2,1,0:T(2,128)}, u32[]{:S(2)}) copy-start(f32[8,2,256]{2,1,0:T(2,128)} %start.9) | copy-start | bytes 49156
  0.6 17.4 %copy-start = (bf16[8,256,128]{2,1,0:T(8,128)(2,1)S(1)}, bf16[8,256,128]{2,1,0:T(8,128)(2,1)}, u32[]{:S(2)}) copy-start(bf16[8,256,128]{2,1,0:T(8,128)(2,1)} %patches.5) | copy-start | bytes 1572868
  2.9 15.1 %copy-start.3 = (s32[8,2,8,256]{3,2,1,0:T(8,128)S(1)}, s32[8,2,8,256]{3,2,1,0:T(8,128)}, u32[]{:S(2)}) copy-start(s32[8,2,8,256]{3,2,1,0:T(8,128)} %cand.5) | copy-start | bytes 393220
  2.9 15.1 %collective-permute-start.6 = (bf16[736,128]{1,0:T(8,128)(2,1)}, bf16[736,128]{1,0:T(8,128)(2,1)S(1)}, u32[]{:S(2)}, u32[]{:S(2)}) collective-permute-start(bf16[736,128]{1,0:T(8,128)(2,1)} %get-tuple-element.24), channel_id=1, source_target_pairs={{0,16},{16,32},{32,48},{48,64},{64,80},{80,96},{96,112},{112,128},... | collective-permute-start | bytes 565256 | tf_op jit(solution)/shard_map/ppermute | solution.py:27
  3.0 11.1 %collective-permute-start = (bf16[320,128]{1,0:T(8,128)(2,1)}, bf16[320,128]{1,0:T(8,128)(2,1)S(1)}, u32[]{:S(2)}, u32[]{:S(2)}) collective-permute-start(bf16[320,128]{1,0:T(8,128)(2,1)} %get-tuple-element.18), channel_id=1, source_target_pairs={{0,3},{1,2},{2,1},{3,0},{4,7},{5,6},{6,5},{7,4},{8,11},{9,10},{10,... | collective-permute-start | bytes 245768 | tf_op jit(solution)/shard_map/ppermute | solution.py:27
  4.6 9.6 %collective-permute-start.1 = (bf16[320,128]{1,0:T(8,128)(2,1)}, bf16[320,128]{1,0:T(8,128)(2,1)S(1)}, u32[]{:S(2)}, u32[]{:S(2)}) collective-permute-start(bf16[320,128]{1,0:T(8,128)(2,1)} %get-tuple-element.19), channel_id=1, source_target_pairs={{0,1},{1,0},{2,3},{3,2},{4,5},{5,4},{6,7},{7,6},{8,9},{9,8},{10,11... | collective-permute-start | bytes 245768 | tf_op jit(solution)/shard_map/ppermute | solution.py:27
  6.4 12.4 %collective-permute-start.2 = (bf16[8,32,128]{2,1,0:T(8,128)(2,1)}, bf16[8,32,128]{2,1,0:T(8,128)(2,1)S(1)}, u32[]{:S(2)}, u32[]{:S(2)}) collective-permute-start(bf16[8,32,128]{2,1,0:T(8,128)(2,1)} %get-tuple-element.20), channel_id=1, source_target_pairs={{0,12},{1,13},{2,14},{3,15},{4,8},{5,9},{6,10},{7,11},{8,4},{9,5},... | collective-permute-start | bytes 196616 | tf_op jit(solution)/shard_map/ppermute | solution.py:27
  12.7 6.8 %collective-permute-start.3 = (bf16[8,32,128]{2,1,0:T(8,128)(2,1)}, bf16[8,32,128]{2,1,0:T(8,128)(2,1)S(1)}, u32[]{:S(2)}, u32[]{:S(2)}) collective-permute-start(bf16[8,32,128]{2,1,0:T(8,128)(2,1)} %get-tuple-element.21), channel_id=1, source_target_pairs={{0,4},{1,5},{2,6},{3,7},{4,0},{5,1},{6,2},{7,3},{8,12},{9,13},{10,... | collective-permute-start | bytes 196616 | tf_op jit(solution)/shard_map/ppermute | solution.py:27
  14.4 6.1 %collective-permute-start.4 = (bf16[96,128]{1,0:T(8,128)(2,1)S(1)}, bf16[96,128]{1,0:T(8,128)(2,1)S(1)}, u32[]{:S(2)}, u32[]{:S(2)}) collective-permute-start(bf16[96,128]{1,0:T(8,128)(2,1)S(1)} %get-tuple-element.22), channel_id=1, source_target_pairs={{0,12},{1,13},{2,14},{3,15},{4,8},{5,9},{6,10},{7,11},{8,4},{9,5},... | collective-permute-start | bytes 73736 | tf_op jit(solution)/shard_map/ppermute | solution.py:27
  16.6 4.8 %collective-permute-start.5 = (bf16[96,128]{1,0:T(8,128)(2,1)S(1)}, bf16[96,128]{1,0:T(8,128)(2,1)S(1)}, u32[]{:S(2)}, u32[]{:S(2)}) collective-permute-start(bf16[96,128]{1,0:T(8,128)(2,1)S(1)} %get-tuple-element.23), channel_id=1, source_target_pairs={{0,4},{1,5},{2,6},{3,7},{4,0},{5,1},{6,2},{7,3},{8,12},{9,13},{10,... | collective-permute-start | bytes 73736 | tf_op jit(solution)/shard_map/ppermute | solution.py:27
  18.8 3.8 %copy-start.2 = (s32[8,2,2,8,256]{4,3,2,1,0:T(8,128)S(1)}, s32[8,2,2,8,256]{4,3,2,1,0:T(8,128)}, u32[]{:S(2)}) copy-start(s32[8,2,2,8,256]{4,3,2,1,0:T(8,128)} %offs.3) | copy-start | bytes 786436
  18.8 3.8 %copy-start.4 = (s32[8,2]{0,1:T(2,128)S(1)}, s32[8,2]{0,1:T(2,128)}, u32[]{:S(2)}) copy-start(s32[8,2]{0,1:T(2,128)} %param.8) | copy-start | bytes 196
  21.6 5.0 %collective-permute-start.7 = (f32[16,256]{1,0:T(8,128)S(1)}, f32[16,256]{1,0:T(8,128)S(1)}, u32[]{:S(2)}, u32[]{:S(2)}) collective-permute-start(f32[16,256]{1,0:T(8,128)S(1)} %lower_targets.1.sent), channel_id=1, source_target_pairs={{0,240},{16,0},{32,16},{48,32},{64,48},{80,64},{96,80},{112,96},{1... | collective-permute-start | bytes 49160 | tf_op jit(solution)/shard_map/ppermute | solution.py:27
  24.0 6.5 %collective-permute-start.9 = (f32[16,256]{1,0:T(8,128)S(1)}, f32[16,256]{1,0:T(8,128)S(1)}, u32[]{:S(2)}, u32[]{:S(2)}) collective-permute-start(f32[16,256]{1,0:T(8,128)S(1)} %get-tuple-element.25.part), channel_id=1, source_target_pairs={{0,16},{16,0},{32,48},{48,32},{64,80},{80,64},{96,112},{112,96},{1... | collective-permute-start | bytes 49160 | tf_op jit(solution)/shard_map/ppermute | solution.py:27
  24.1 9.1 %collective-permute-start.8 = (f32[16,256]{1,0:T(8,128)S(1)}, f32[16,256]{1,0:T(8,128)S(1)}, u32[]{:S(2)}, u32[]{:S(2)}) collective-permute-start(f32[16,256]{1,0:T(8,128)S(1)} %get-tuple-element.25.part), channel_id=1, source_target_pairs={{0,240},{16,32},{32,16},{48,64},{64,48},{80,96},{96,80},{112,128},... | collective-permute-start | bytes 49160 | tf_op jit(solution)/shard_map/ppermute | solution.py:27
  26.7 6.5 %collective-permute-start.13 = (f32[16,256]{1,0:T(8,128)S(1)}, f32[16,256]{1,0:T(8,128)S(1)}, u32[]{:S(2)}, u32[]{:S(2)}) collective-permute-start(f32[16,256]{1,0:T(8,128)S(1)} %first_round.1.u1), channel_id=1, source_target_pairs={{0,12},{1,13},{2,14},{3,15},{4,8},{5,9},{6,10},{7,11},{8,4},{9,5},... | collective-permute-start | bytes 49160 | tf_op jit(solution)/shard_map/ppermute | solution.py:27
  29.0 4.6 %collective-permute-start.12 = (f32[16,256]{1,0:T(8,128)S(1)}, f32[16,256]{1,0:T(8,128)S(1)}, u32[]{:S(2)}, u32[]{:S(2)}) collective-permute-start(f32[16,256]{1,0:T(8,128)S(1)} %first_round.1.u1), channel_id=1, source_target_pairs={{0,4},{1,5},{2,6},{3,7},{4,0},{5,1},{6,2},{7,3},{8,12},{9,13},{10,... | collective-permute-start | bytes 49160 | tf_op jit(solution)/shard_map/ppermute | solution.py:27
  30.5 3.7 %collective-permute-start.11 = (f32[16,256]{1,0:T(8,128)S(1)}, f32[16,256]{1,0:T(8,128)S(1)}, u32[]{:S(2)}, u32[]{:S(2)}) collective-permute-start(f32[16,256]{1,0:T(8,128)S(1)} %first_round.1.u1), channel_id=1, source_target_pairs={{0,3},{1,2},{2,1},{3,0},{4,7},{5,6},{6,5},{7,4},{8,11},{9,10},{10,... | collective-permute-start | bytes 49160 | tf_op jit(solution)/shard_map/ppermute | solution.py:27
  30.5 3.8 %collective-permute-start.10 = (f32[16,256]{1,0:T(8,128)S(1)}, f32[16,256]{1,0:T(8,128)S(1)}, u32[]{:S(2)}, u32[]{:S(2)}) collective-permute-start(f32[16,256]{1,0:T(8,128)S(1)} %first_round.1.u1), channel_id=1, source_target_pairs={{0,1},{1,0},{2,3},{3,2},{4,5},{5,4},{6,7},{7,6},{8,9},{9,8},{10,11... | collective-permute-start | bytes 49160 | tf_op jit(solution)/shard_map/ppermute | solution.py:27

commit v4 on v3

--- a/solution.py
+++ b/solution.py
@@ -458,7 +458,8 @@
         pltpu.SemaphoreType.DMA((4 + SEC,)),
     ]
     outs = [shape(SEC, 32, PATCH, dtype=BF)] * 2 + [shape(X_ROWS, PATCH, dtype=BF)] * 2 + [shape(S_ROWS, PATCH, dtype=BF)]
-    rb, ra, xb, xa, lower = call(pack_first, outs, [flat] + held, 1 << 20, 5, far=(0, 1, 2, 3, 4), vmem=62 << 20)(
+    outs = [pltpu.VMEM(a.shape, a.dtype) for a in outs]
+    rb, ra, xb, xa, lower = call(pack_first, outs, [flat] + held, 1 << 20, 5, far=(0, 1, 2, 3, 4), vmem=58 << 20)(
         patches, cand, offs, pairs, start
     )
     rb = swapped(rb, "tile", row_b)

time: 35.6 us -> 34.8 us (0.978)
  Pallas kernels: 6.24 us -> 5.54 us
    pallas_call x1, Pallas kernels: 2.24 us -> 1.53 us  [on_device(): call(pack_first, outs, [flat] + held, 1 << 20, 5, far=(0, 1, 2, 3, 4), vm...]
  transfers between devices with their start and end apart: 14 -> 14, of which waited for: 6 -> 5; matrix products, arithmetic and copies ran while one was open for 0% -> 0% of each run, Pallas kernels for 9% -> 9%
where the time goes in v4:
time: 34.8 us; the launch traced here: 34.2 us
  starting transfers between devices  24.1 us (69%)
  Pallas kernels  5.54 us (16%)
  waiting for transfers between devices  3.74 us (11%)
  between operations  0.76 us (2%)
    ppermute x14, starting transfers between devices, swapped(): lax.ppermute(block, axis, [(i, partner(i)) for i in range(lax.axis_size(a...  24.1 us
    ppermute x14, waiting for transfers between devices, swapped(): lax.ppermute(block, axis, [(i, partner(i)) for i in range(lax.axis_size(a...  3.74 us
    pallas_call x1, Pallas kernels, on_device(): call(pack_first, outs, [flat] + held, 1 << 20, 5, far=(0, 1, 2, 3, 4), vm...  1.53 us
    pallas_call x1, Pallas kernels, on_device(): call(own_targets, [shape(SEC, 2, VT)] * 2 + [shape(16, VT)] + [shape(24,...  1.4 us
    pallas_call x1, Pallas kernels, on_device(): call(inner_scores, [shape(2, SEC + 2, 2, 8, HALF)], [pltpu.VMEM((X_ROWS,...  0.76 us
    pallas_call x1, Pallas kernels, on_device(): call(second_round, [shape(SEC, 2, VT)], [pltpu.VMEM((24, VT), F32)], 1 <<...  0.73 us
  transfers between devices with their start and end apart: 14, of which 5 were waited for; matrix products, arithmetic and copies ran while one was open for 0% of the time, Pallas kernels for 9%

profile of v4, /device:TPU:2, one launch (start us, length us, event | category | flops | bytes accessed | tf_op | source)
XLA Modules:
  0.0 34.2 jit_solution(15320227226685041951)
XLA Ops:
  0.6 1.5 %pack_first.1 = (bf16[8,32,128]{2,1,0:T(8,128)(2,1)S(1)}, bf16[8,32,128]{2,1,0:T(8,128)(2,1)S(1)}, bf16[320,128]{1,0:T(8,128)(2,1)S(1)}, bf16[320,128]{1,0:T(8,128)(2,1)S(1)}, bf16[736,128]{1,0:T(8,128)(2,1)S(1)}) custom-call(bf16[8,256,128]{2,1,0:T(8,128)(2,1)} %patches.5, s32[8,2,8,256]{3,2,1,0:T(8,128)} %cand.5, s32[8,2,2,8,256]{4,3,2,1,0:T(8,128)} %offs.3, ...), custom_call_target="tpu_custom_call" | custom-call | flops 1048576 | bytes 1048576 | tf_op jit(solution)/shard_map/pack_first/pallas_call | solution.py:462
  2.2 0.0 copy-start.3
  2.2 0.1 collective-permute-start.6
  2.3 1.6 %collective-permute-start = (bf16[320,128]{1,0:T(8,128)(2,1)S(1)}, bf16[320,128]{1,0:T(8,128)(2,1)S(1)}, u32[]{:S(2)}, u32[]{:S(2)}) collective-permute-start(bf16[320,128]{1,0:T(8,128)(2,1)S(1)} %get-tuple-element.18), channel_id=1, source_target_pairs={{0,3},{1,2},{2,1},{3,0},{4,7},{5,6},{6,5},{7,4},{8,11},{9,10},{10,... | collective-permute-start | bytes 245768 | tf_op jit(solution)/shard_map/ppermute | solution.py:27
  3.9 1.8 %collective-permute-start.1 = (bf16[320,128]{1,0:T(8,128)(2,1)S(1)}, bf16[320,128]{1,0:T(8,128)(2,1)S(1)}, u32[]{:S(2)}, u32[]{:S(2)}) collective-permute-start(bf16[320,128]{1,0:T(8,128)(2,1)S(1)} %get-tuple-element.19), channel_id=1, source_target_pairs={{0,1},{1,0},{2,3},{3,2},{4,5},{5,4},{6,7},{7,6},{8,9},{9,8},{10,11... | collective-permute-start | bytes 245768 | tf_op jit(solution)/shard_map/ppermute | solution.py:27
  5.7 6.3 %collective-permute-start.2 = (bf16[8,32,128]{2,1,0:T(8,128)(2,1)S(1)}, bf16[8,32,128]{2,1,0:T(8,128)(2,1)S(1)}, u32[]{:S(2)}, u32[]{:S(2)}) collective-permute-start(bf16[8,32,128]{2,1,0:T(8,128)(2,1)S(1)} %get-tuple-element.20), channel_id=1, source_target_pairs={{0,12},{1,13},{2,14},{3,15},{4,8},{5,9},{6,10},{7,11},{8,4},{9,5},... | collective-permute-start | bytes 196616 | tf_op jit(solution)/shard_map/ppermute | solution.py:27
  12.0 1.5 %collective-permute-start.3 = (bf16[8,32,128]{2,1,0:T(8,128)(2,1)S(1)}, bf16[8,32,128]{2,1,0:T(8,128)(2,1)S(1)}, u32[]{:S(2)}, u32[]{:S(2)}) collective-permute-start(bf16[8,32,128]{2,1,0:T(8,128)(2,1)S(1)} %get-tuple-element.21), channel_id=1, source_target_pairs={{0,4},{1,5},{2,6},{3,7},{4,0},{5,1},{6,2},{7,3},{8,12},{9,13},{10,... | collective-permute-start | bytes 196616 | tf_op jit(solution)/shard_map/ppermute | solution.py:27
  13.4 0.0 collective-permute-done.xb
  13.4 0.0 collective-permute-done.1.xa
  13.4 0.2 pack_corners.1
  13.7 2.0 %collective-permute-start.4 = (bf16[96,128]{1,0:T(8,128)(2,1)S(1)}, bf16[96,128]{1,0:T(8,128)(2,1)S(1)}, u32[]{:S(2)}, u32[]{:S(2)}) collective-permute-start(bf16[96,128]{1,0:T(8,128)(2,1)S(1)} %get-tuple-element.22), channel_id=1, source_target_pairs={{0,12},{1,13},{2,14},{3,15},{4,8},{5,9},{6,10},{7,11},{8,4},{9,5},... | collective-permute-start | bytes 73736 | tf_op jit(solution)/shard_map/ppermute | solution.py:27
  15.6 1.5 %collective-permute-start.5 = (bf16[96,128]{1,0:T(8,128)(2,1)S(1)}, bf16[96,128]{1,0:T(8,128)(2,1)S(1)}, u32[]{:S(2)}, u32[]{:S(2)}) collective-permute-start(bf16[96,128]{1,0:T(8,128)(2,1)S(1)} %get-tuple-element.23), channel_id=1, source_target_pairs={{0,4},{1,5},{2,6},{3,7},{4,0},{5,1},{6,2},{7,3},{8,12},{9,13},{10,... | collective-permute-start | bytes 73736 | tf_op jit(solution)/shard_map/ppermute | solution.py:27
  17.1 0.8 %inner_scores.1.inner = f32[2,10,2,8,128]{4,3,2,1,0:T(8,128)S(1)} custom-call(bf16[8,256,128]{2,1,0:T(8,128)(2,1)S(1)} %copy-done, s32[8,2,8,256]{3,2,1,0:T(8,128)S(1)} %copy-done.3, bf16[320,128]{1,0:T(8,128)(2,1)S(1)} %collective-permute-done.xb, bf16[320,128]{1,0:T(8,128)(2,1)S(1)} %collective-permute-done.1.xa, ...), custom_call_target="tpu_custom_call" | custom-call | flops 2147483648 | bytes 1048576 | tf_op jit(solution)/shard_map/inner_scores/pallas_call | solution.py:474
  17.9 0.0 copy-start.2
  17.9 0.0 copy-start.4
  17.9 0.6 %collective-permute-done.3.ra = bf16[8,32,128]{2,1,0:T(8,128)(2,1)S(1)} collective-permute-done((bf16[8,32,128]{2,1,0:T(8,128)(2,1)S(1)}, bf16[8,32,128]{2,1,0:T(8,128)(2,1)S(1)}, u32[]{:S(2)}, u32[]{:S(2)}) %collective-permute-start.3) | collective-permute-done | bytes 65568 | tf_op jit(solution)/shard_map/ppermute | solution.py:27
  18.5 1.2 %collective-permute-done.4.cb = bf16[96,128]{1,0:T(8,128)(2,1)S(1)} collective-permute-done((bf16[96,128]{1,0:T(8,128)(2,1)S(1)}, bf16[96,128]{1,0:T(8,128)(2,1)S(1)}, u32[]{:S(2)}, u32[]{:S(2)}) %collective-permute-start.4) | collective-permute-done | bytes 24608 | tf_op jit(solution)/shard_map/ppermute | solution.py:27
  19.7 0.7 %collective-permute-done.5.ca = bf16[96,128]{1,0:T(8,128)(2,1)S(1)} collective-permute-done((bf16[96,128]{1,0:T(8,128)(2,1)S(1)}, bf16[96,128]{1,0:T(8,128)(2,1)S(1)}, u32[]{:S(2)}, u32[]{:S(2)}) %collective-permute-start.5) | collective-permute-done | bytes 24608 | tf_op jit(solution)/shard_map/ppermute | solution.py:27
  20.4 0.3 lower_targets.1.sent
  20.7 1.0 %collective-permute-start.7 = (f32[16,256]{1,0:T(8,128)S(1)}, f32[16,256]{1,0:T(8,128)S(1)}, u32[]{:S(2)}, u32[]{:S(2)}) collective-permute-start(f32[16,256]{1,0:T(8,128)S(1)} %lower_targets.1.sent), channel_id=1, source_target_pairs={{0,240},{16,0},{32,16},{48,32},{64,48},{80,64},{96,80},{112,96},{1... | collective-permute-start | bytes 49160 | tf_op jit(solution)/shard_map/ppermute | solution.py:27
  21.7 1.4 %own_targets.1 = (f32[8,2,256]{2,1,0:T(2,128)S(1)}, f32[8,2,256]{2,1,0:T(2,128)S(1)}, f32[16,256]{1,0:T(8,128)S(1)}, f32[24,256]{1,0:T(8,128)S(1)}, f32[24,256]{...) custom-call(bf16[8,256,128]{2,1,0:T(8,128)(2,1)S(1)} %copy-done, ...), custom_call_target="tpu_custom_call" | custom-call | flops 2147483648 | bytes 1048576 | tf_op jit(solution)/shard_map/own_targets/pallas_call | solution.py:479
  23.1 0.1 collective-permute-start.9
  23.2 2.6 %collective-permute-start.8 = (f32[16,256]{1,0:T(8,128)S(1)}, f32[16,256]{1,0:T(8,128)S(1)}, u32[]{:S(2)}, u32[]{:S(2)}) collective-permute-start(f32[16,256]{1,0:T(8,128)S(1)} %get-tuple-element.25.part), channel_id=1, source_target_pairs={{0,240},{16,32},{32,16},{48,64},{64,48},{80,96},{96,80},{112,128},... | collective-permute-start | bytes 49160 | tf_op jit(solution)/shard_map/ppermute | solution.py:27
  25.8 2.4 %collective-permute-start.13 = (f32[16,256]{1,0:T(8,128)S(1)}, f32[16,256]{1,0:T(8,128)S(1)}, u32[]{:S(2)}, u32[]{:S(2)}) collective-permute-start(f32[16,256]{1,0:T(8,128)S(1)} %first_round.1.u1), channel_id=1, source_target_pairs={{0,12},{1,13},{2,14},{3,15},{4,8},{5,9},{6,10},{7,11},{8,4},{9,5},... | collective-permute-start | bytes 49160 | tf_op jit(solution)/shard_map/ppermute | solution.py:27
  28.3 1.5 %collective-permute-start.12 = (f32[16,256]{1,0:T(8,128)S(1)}, f32[16,256]{1,0:T(8,128)S(1)}, u32[]{:S(2)}, u32[]{:S(2)}) collective-permute-start(f32[16,256]{1,0:T(8,128)S(1)} %first_round.1.u1), channel_id=1, source_target_pairs={{0,4},{1,5},{2,6},{3,7},{4,0},{5,1},{6,2},{7,3},{8,12},{9,13},{10,... | collective-permute-start | bytes 49160 | tf_op jit(solution)/shard_map/ppermute | solution.py:27
  29.7 0.0 collective-permute-start.11
  29.7 1.9 %collective-permute-start.10 = (f32[16,256]{1,0:T(8,128)S(1)}, f32[16,256]{1,0:T(8,128)S(1)}, u32[]{:S(2)}, u32[]{:S(2)}) collective-permute-start(f32[16,256]{1,0:T(8,128)S(1)} %first_round.1.u1), channel_id=1, source_target_pairs={{0,1},{1,0},{2,3},{3,2},{4,5},{5,4},{6,7},{7,6},{8,9},{9,8},{10,11... | collective-permute-start | bytes 49160 | tf_op jit(solution)/shard_map/ppermute | solution.py:27
  31.7 0.6 %all_targets.1 = f32[8,2,2,256]{3,2,1,0:T(2,128)} custom-call(f32[8,2,256]{2,1,0:T(2,128)S(1)} %get-tuple-element.32.p0, f32[8,2,256]{2,1,0:T(2,128)S(1)} %get-tuple-element.33.p1, f32[16,256]{1,0:T(8,128)S(1)} %collective-permute-done.7.got), custom_call_target="tpu_custom_call" | custom-call | flops 1048576 | bytes 1048576 | tf_op jit(solution)/shard_map/all_targets/pallas_call | solution.py:491
  32.3 0.6 %collective-permute-done.12.ra = f32[16,256]{1,0:T(8,128)S(1)} collective-permute-done((f32[16,256]{1,0:T(8,128)S(1)}, f32[16,256]{1,0:T(8,128)S(1)}, u32[]{:S(2)}, u32[]{:S(2)}) %collective-permute-start.12) | collective-permute-done | bytes 16416 | tf_op jit(solution)/shard_map/ppermute | solution.py:27
  32.9 0.6 %collective-permute-done.11.xb = f32[16,256]{1,0:T(8,128)S(1)} collective-permute-done((f32[16,256]{1,0:T(8,128)S(1)}, f32[16,256]{1,0:T(8,128)S(1)}, u32[]{:S(2)}, u32[]{:S(2)}) %collective-permute-start.11) | collective-permute-done | bytes 16416 | tf_op jit(solution)/shard_map/ppermute | solution.py:27
  33.5 0.0 collective-permute-done.10.xa
  33.5 0.7 %second_round.1 = f32[8,2,256]{2,1,0:T(2,128)} custom-call(f32[16,256]{1,0:T(8,128)S(1)} %first_round.1.u1, f32[16,256]{1,0:T(8,128)S(1)} %collective-permute-done.8.sb, f32[16,256]{1,0:T(8,128)S(1)} %collective-permute-done.9.sa, f32[16,256]{1,0:T(8,128)S(1)} %collective-permute-done.10.xa, f32[16,256]{1,0:T(8,128)S(1)} %collective-permute-done.11.xb, ...), custom_call_target="tpu_custom_call" | custom-call | flops 1048576 | bytes 1048576 | tf_op jit(solution)/shard_map/second_round/pallas_call | solution.py:492
  (14 shorter events, 0.0 us)
Async XLA Ops:
  0.6 12.8 %copy-start.1 = (f32[8,2,256]{2,1,0:T(2,128)S(1)}, f32[8,2,256]{2,1,0:T(2,128)}, u32[]{:S(2)}) copy-start(f32[8,2,256]{2,1,0:T(2,128)} %start.9) | copy-start | bytes 49156
  0.6 16.5 %copy-start = (bf16[8,256,128]{2,1,0:T(8,128)(2,1)S(1)}, bf16[8,256,128]{2,1,0:T(8,128)(2,1)}, u32[]{:S(2)}) copy-start(bf16[8,256,128]{2,1,0:T(8,128)(2,1)} %patches.5) | copy-start | bytes 1572868
  2.2 14.9 %copy-start.3 = (s32[8,2,8,256]{3,2,1,0:T(8,128)S(1)}, s32[8,2,8,256]{3,2,1,0:T(8,128)}, u32[]{:S(2)}) copy-start(s32[8,2,8,256]{3,2,1,0:T(8,128)} %cand.5) | copy-start | bytes 393220
  2.2 14.9 %collective-permute-start.6 = (bf16[736,128]{1,0:T(8,128)(2,1)S(1)}, bf16[736,128]{1,0:T(8,128)(2,1)S(1)}, u32[]{:S(2)}, u32[]{:S(2)}) collective-permute-start(bf16[736,128]{1,0:T(8,128)(2,1)S(1)} %get-tuple-element.24), channel_id=1, source_target_pairs={{0,16},{16,32},{32,48},{48,64},{64,80},{80,96},{96,112},{112,128},... | collective-permute-start | bytes 565256 | tf_op jit(solution)/shard_map/ppermute | solution.py:27
  2.3 11.1 %collective-permute-start = (bf16[320,128]{1,0:T(8,128)(2,1)S(1)}, bf16[320,128]{1,0:T(8,128)(2,1)S(1)}, u32[]{:S(2)}, u32[]{:S(2)}) collective-permute-start(bf16[320,128]{1,0:T(8,128)(2,1)S(1)} %get-tuple-element.18), channel_id=1, source_target_pairs={{0,3},{1,2},{2,1},{3,0},{4,7},{5,6},{6,5},{7,4},{8,11},{9,10},{10,... | collective-permute-start | bytes 245768 | tf_op jit(solution)/shard_map/ppermute | solution.py:27
  3.9 9.6 %collective-permute-start.1 = (bf16[320,128]{1,0:T(8,128)(2,1)S(1)}, bf16[320,128]{1,0:T(8,128)(2,1)S(1)}, u32[]{:S(2)}, u32[]{:S(2)}) collective-permute-start(bf16[320,128]{1,0:T(8,128)(2,1)S(1)} %get-tuple-element.19), channel_id=1, source_target_pairs={{0,1},{1,0},{2,3},{3,2},{4,5},{5,4},{6,7},{7,6},{8,9},{9,8},{10,11... | collective-permute-start | bytes 245768 | tf_op jit(solution)/shard_map/ppermute | solution.py:27
  5.7 12.2 %collective-permute-start.2 = (bf16[8,32,128]{2,1,0:T(8,128)(2,1)S(1)}, bf16[8,32,128]{2,1,0:T(8,128)(2,1)S(1)}, u32[]{:S(2)}, u32[]{:S(2)}) collective-permute-start(bf16[8,32,128]{2,1,0:T(8,128)(2,1)S(1)} %get-tuple-element.20), channel_id=1, source_target_pairs={{0,12},{1,13},{2,14},{3,15},{4,8},{5,9},{6,10},{7,11},{8,4},{9,5},... | collective-permute-start | bytes 196616 | tf_op jit(solution)/shard_map/ppermute | solution.py:27
  12.0 6.6 %collective-permute-start.3 = (bf16[8,32,128]{2,1,0:T(8,128)(2,1)S(1)}, bf16[8,32,128]{2,1,0:T(8,128)(2,1)S(1)}, u32[]{:S(2)}, u32[]{:S(2)}) collective-permute-start(bf16[8,32,128]{2,1,0:T(8,128)(2,1)S(1)} %get-tuple-element.21), channel_id=1, source_target_pairs={{0,4},{1,5},{2,6},{3,7},{4,0},{5,1},{6,2},{7,3},{8,12},{9,13},{10,... | collective-permute-start | bytes 196616 | tf_op jit(solution)/shard_map/ppermute | solution.py:27
  13.7 6.0 %collective-permute-start.4 = (bf16[96,128]{1,0:T(8,128)(2,1)S(1)}, bf16[96,128]{1,0:T(8,128)(2,1)S(1)}, u32[]{:S(2)}, u32[]{:S(2)}) collective-permute-start(bf16[96,128]{1,0:T(8,128)(2,1)S(1)} %get-tuple-element.22), channel_id=1, source_target_pairs={{0,12},{1,13},{2,14},{3,15},{4,8},{5,9},{6,10},{7,11},{8,4},{9,5},... | collective-permute-start | bytes 73736 | tf_op jit(solution)/shard_map/ppermute | solution.py:27
  15.6 4.8 %collective-permute-start.5 = (bf16[96,128]{1,0:T(8,128)(2,1)S(1)}, bf16[96,128]{1,0:T(8,128)(2,1)S(1)}, u32[]{:S(2)}, u32[]{:S(2)}) collective-permute-start(bf16[96,128]{1,0:T(8,128)(2,1)S(1)} %get-tuple-element.23), channel_id=1, source_target_pairs={{0,4},{1,5},{2,6},{3,7},{4,0},{5,1},{6,2},{7,3},{8,12},{9,13},{10,... | collective-permute-start | bytes 73736 | tf_op jit(solution)/shard_map/ppermute | solution.py:27
  17.9 3.8 %copy-start.2 = (s32[8,2,2,8,256]{4,3,2,1,0:T(8,128)S(1)}, s32[8,2,2,8,256]{4,3,2,1,0:T(8,128)}, u32[]{:S(2)}) copy-start(s32[8,2,2,8,256]{4,3,2,1,0:T(8,128)} %offs.3) | copy-start | bytes 786436
  17.9 3.8 %copy-start.4 = (s32[8,2]{0,1:T(2,128)S(1)}, s32[8,2]{0,1:T(2,128)}, u32[]{:S(2)}) copy-start(s32[8,2]{0,1:T(2,128)} %param.8) | copy-start | bytes 196
  20.7 5.1 %collective-permute-start.7 = (f32[16,256]{1,0:T(8,128)S(1)}, f32[16,256]{1,0:T(8,128)S(1)}, u32[]{:S(2)}, u32[]{:S(2)}) collective-permute-start(f32[16,256]{1,0:T(8,128)S(1)} %lower_targets.1.sent), channel_id=1, source_target_pairs={{0,240},{16,0},{32,16},{48,32},{64,48},{80,64},{96,80},{112,96},{1... | collective-permute-start | bytes 49160 | tf_op jit(solution)/shard_map/ppermute | solution.py:27
  23.1 6.6 %collective-permute-start.9 = (f32[16,256]{1,0:T(8,128)S(1)}, f32[16,256]{1,0:T(8,128)S(1)}, u32[]{:S(2)}, u32[]{:S(2)}) collective-permute-start(f32[16,256]{1,0:T(8,128)S(1)} %get-tuple-element.25.part), channel_id=1, source_target_pairs={{0,16},{16,0},{32,48},{48,32},{64,80},{80,64},{96,112},{112,96},{1... | collective-permute-start | bytes 49160 | tf_op jit(solution)/shard_map/ppermute | solution.py:27
  23.2 9.1 %collective-permute-start.8 = (f32[16,256]{1,0:T(8,128)S(1)}, f32[16,256]{1,0:T(8,128)S(1)}, u32[]{:S(2)}, u32[]{:S(2)}) collective-permute-start(f32[16,256]{1,0:T(8,128)S(1)} %get-tuple-element.25.part), channel_id=1, source_target_pairs={{0,240},{16,32},{32,16},{48,64},{64,48},{80,96},{96,80},{112,128},... | collective-permute-start | bytes 49160 | tf_op jit(solution)/shard_map/ppermute | solution.py:27
  25.8 6.4 %collective-permute-start.13 = (f32[16,256]{1,0:T(8,128)S(1)}, f32[16,256]{1,0:T(8,128)S(1)}, u32[]{:S(2)}, u32[]{:S(2)}) collective-permute-start(f32[16,256]{1,0:T(8,128)S(1)} %first_round.1.u1), channel_id=1, source_target_pairs={{0,12},{1,13},{2,14},{3,15},{4,8},{5,9},{6,10},{7,11},{8,4},{9,5},... | collective-permute-start | bytes 49160 | tf_op jit(solution)/shard_map/ppermute | solution.py:27
  28.3 4.6 %collective-permute-start.12 = (f32[16,256]{1,0:T(8,128)S(1)}, f32[16,256]{1,0:T(8,128)S(1)}, u32[]{:S(2)}, u32[]{:S(2)}) collective-permute-start(f32[16,256]{1,0:T(8,128)S(1)} %first_round.1.u1), channel_id=1, source_target_pairs={{0,4},{1,5},{2,6},{3,7},{4,0},{5,1},{6,2},{7,3},{8,12},{9,13},{10,... | collective-permute-start | bytes 49160 | tf_op jit(solution)/shard_map/ppermute | solution.py:27
  29.7 3.7 %collective-permute-start.11 = (f32[16,256]{1,0:T(8,128)S(1)}, f32[16,256]{1,0:T(8,128)S(1)}, u32[]{:S(2)}, u32[]{:S(2)}) collective-permute-start(f32[16,256]{1,0:T(8,128)S(1)} %first_round.1.u1), channel_id=1, source_target_pairs={{0,3},{1,2},{2,1},{3,0},{4,7},{5,6},{6,5},{7,4},{8,11},{9,10},{10,... | collective-permute-start | bytes 49160 | tf_op jit(solution)/shard_map/ppermute | solution.py:27
  29.7 3.7 %collective-permute-start.10 = (f32[16,256]{1,0:T(8,128)S(1)}, f32[16,256]{1,0:T(8,128)S(1)}, u32[]{:S(2)}, u32[]{:S(2)}) collective-permute-start(f32[16,256]{1,0:T(8,128)S(1)} %first_round.1.u1), channel_id=1, source_target_pairs={{0,1},{1,0},{2,3},{3,2},{4,5},{5,4},{6,7},{7,6},{8,9},{9,8},{10,11... | collective-permute-start | bytes 49160 | tf_op jit(solution)/shard_map/ppermute | solution.py:27

commit v5 on v4

--- a/solution.py
+++ b/solution.py
@@ -83,7 +83,7 @@
     scr, held, held_c, held_o, held_p, held_u, sems,
 ):
     sources = [(start, held_u), (pairs, held_p), (cand.at[6:8], held_c), (offs.at[6:8], held_o)]
-    sources += [(patches.at[s : s + 8], held.at[s : s + 8]) for s in range(0, SEC, 8)]
+    sources += [(patches.at[s : s + 4], held.at[s : s + 4]) for s in range(0, SEC, 4)]
     copies = [pltpu.make_async_copy(src, dst, sems.at[n]) for n, (src, dst) in enumerate(sources)]
     for copy in copies:
         copy.start()
@@ -118,8 +118,8 @@
     ).astype(BF)
     first = jnp.where(row % 2 == 0, VT - 32, 0)
     for s in range(SEC):
-        if s % 8 == 0:
-            copies[4 + s // 8].wait()
+        if s % 4 == 0:
+            copies[4 + s // 4].wait()
         strips = dot(pick, held[s]).astype(BF)
         xa[s * 32 : s * 32 + 32, :] = strips[:32]
         xb[s * 32 : s * 32 + 32, :] = strips[32:]

time: 34.8 us -> 34.9 us (level)
  no operation moved by 1% of the time
where the time goes in v5:
time: 34.9 us; the launch traced here: 34.3 us
  starting transfers between devices  24.1 us (69%)
  Pallas kernels  5.61 us (16%)
  waiting for transfers between devices  3.71 us (11%)
  between operations  0.76 us (2%)
    ppermute x14, starting transfers between devices, swapped(): lax.ppermute(block, axis, [(i, partner(i)) for i in range(lax.axis_size(a...  24.1 us
    ppermute x14, waiting for transfers between devices, swapped(): lax.ppermute(block, axis, [(i, partner(i)) for i in range(lax.axis_size(a...  3.71 us
    pallas_call x1, Pallas kernels, on_device(): call(pack_first, outs, [flat] + held, 1 << 20, 5, far=(0, 1, 2, 3, 4), vm...  1.59 us
    pallas_call x1, Pallas kernels, on_device(): call(own_targets, [shape(SEC, 2, VT)] * 2 + [shape(16, VT)] + [shape(24,...  1.4 us
    pallas_call x1, Pallas kernels, on_device(): call(inner_scores, [shape(2, SEC + 2, 2, 8, HALF)], [pltpu.VMEM((X_ROWS,...  0.77 us
    pallas_call x1, Pallas kernels, on_device(): call(second_round, [shape(SEC, 2, VT)], [pltpu.VMEM((24, VT), F32)], 1 <<...  0.73 us
  transfers between devices with their start and end apart: 14, of which 5 were waited for; matrix products, arithmetic and copies ran while one was open for 0% of the time, Pallas kernels for 9%

profile of v5, /device:TPU:2, one launch (start us, length us, event | category | flops | bytes accessed | tf_op | source)
XLA Modules:
  0.0 34.3 jit_solution(12426045343968587957)
XLA Ops:
  0.6 1.6 %pack_first.1 = (bf16[8,32,128]{2,1,0:T(8,128)(2,1)S(1)}, bf16[8,32,128]{2,1,0:T(8,128)(2,1)S(1)}, bf16[320,128]{1,0:T(8,128)(2,1)S(1)}, bf16[320,128]{1,0:T(8,128)(2,1)S(1)}, bf16[736,128]{1,0:T(8,128)(2,1)S(1)}) custom-call(bf16[8,256,128]{2,1,0:T(8,128)(2,1)} %patches.5, s32[8,2,8,256]{3,2,1,0:T(8,128)} %cand.5, s32[8,2,2,8,256]{4,3,2,1,0:T(8,128)} %offs.3, ...), custom_call_target="tpu_custom_call" | custom-call | flops 1048576 | bytes 1048576 | tf_op jit(solution)/shard_map/pack_first/pallas_call | solution.py:462
  2.2 0.0 copy-start.3
  2.3 0.1 collective-permute-start.6
  2.3 1.6 %collective-permute-start = (bf16[320,128]{1,0:T(8,128)(2,1)S(1)}, bf16[320,128]{1,0:T(8,128)(2,1)S(1)}, u32[]{:S(2)}, u32[]{:S(2)}) collective-permute-start(bf16[320,128]{1,0:T(8,128)(2,1)S(1)} %get-tuple-element.18), channel_id=1, source_target_pairs={{0,3},{1,2},{2,1},{3,0},{4,7},{5,6},{6,5},{7,4},{8,11},{9,10},{10,... | collective-permute-start | bytes 245768 | tf_op jit(solution)/shard_map/ppermute | solution.py:27
  3.9 1.8 %collective-permute-start.1 = (bf16[320,128]{1,0:T(8,128)(2,1)S(1)}, bf16[320,128]{1,0:T(8,128)(2,1)S(1)}, u32[]{:S(2)}, u32[]{:S(2)}) collective-permute-start(bf16[320,128]{1,0:T(8,128)(2,1)S(1)} %get-tuple-element.19), channel_id=1, source_target_pairs={{0,1},{1,0},{2,3},{3,2},{4,5},{5,4},{6,7},{7,6},{8,9},{9,8},{10,11... | collective-permute-start | bytes 245768 | tf_op jit(solution)/shard_map/ppermute | solution.py:27
  5.7 6.3 %collective-permute-start.2 = (bf16[8,32,128]{2,1,0:T(8,128)(2,1)S(1)}, bf16[8,32,128]{2,1,0:T(8,128)(2,1)S(1)}, u32[]{:S(2)}, u32[]{:S(2)}) collective-permute-start(bf16[8,32,128]{2,1,0:T(8,128)(2,1)S(1)} %get-tuple-element.20), channel_id=1, source_target_pairs={{0,12},{1,13},{2,14},{3,15},{4,8},{5,9},{6,10},{7,11},{8,4},{9,5},... | collective-permute-start | bytes 196616 | tf_op jit(solution)/shard_map/ppermute | solution.py:27
  12.0 1.5 %collective-permute-start.3 = (bf16[8,32,128]{2,1,0:T(8,128)(2,1)S(1)}, bf16[8,32,128]{2,1,0:T(8,128)(2,1)S(1)}, u32[]{:S(2)}, u32[]{:S(2)}) collective-permute-start(bf16[8,32,128]{2,1,0:T(8,128)(2,1)S(1)} %get-tuple-element.21), channel_id=1, source_target_pairs={{0,4},{1,5},{2,6},{3,7},{4,0},{5,1},{6,2},{7,3},{8,12},{9,13},{10,... | collective-permute-start | bytes 196616 | tf_op jit(solution)/shard_map/ppermute | solution.py:27
  13.5 0.0 collective-permute-done.1.xa
  13.5 0.2 pack_corners.1
  13.7 2.0 %collective-permute-start.4 = (bf16[96,128]{1,0:T(8,128)(2,1)S(1)}, bf16[96,128]{1,0:T(8,128)(2,1)S(1)}, u32[]{:S(2)}, u32[]{:S(2)}) collective-permute-start(bf16[96,128]{1,0:T(8,128)(2,1)S(1)} %get-tuple-element.22), channel_id=1, source_target_pairs={{0,12},{1,13},{2,14},{3,15},{4,8},{5,9},{6,10},{7,11},{8,4},{9,5},... | collective-permute-start | bytes 73736 | tf_op jit(solution)/shard_map/ppermute | solution.py:27
  15.7 1.5 %collective-permute-start.5 = (bf16[96,128]{1,0:T(8,128)(2,1)S(1)}, bf16[96,128]{1,0:T(8,128)(2,1)S(1)}, u32[]{:S(2)}, u32[]{:S(2)}) collective-permute-start(bf16[96,128]{1,0:T(8,128)(2,1)S(1)} %get-tuple-element.23), channel_id=1, source_target_pairs={{0,4},{1,5},{2,6},{3,7},{4,0},{5,1},{6,2},{7,3},{8,12},{9,13},{10,... | collective-permute-start | bytes 73736 | tf_op jit(solution)/shard_map/ppermute | solution.py:27
  17.2 0.8 %inner_scores.1.inner = f32[2,10,2,8,128]{4,3,2,1,0:T(8,128)S(1)} custom-call(bf16[8,256,128]{2,1,0:T(8,128)(2,1)S(1)} %copy-done, s32[8,2,8,256]{3,2,1,0:T(8,128)S(1)} %copy-done.3, bf16[320,128]{1,0:T(8,128)(2,1)S(1)} %collective-permute-done.xb, bf16[320,128]{1,0:T(8,128)(2,1)S(1)} %collective-permute-done.1.xa, ...), custom_call_target="tpu_custom_call" | custom-call | flops 2147483648 | bytes 1048576 | tf_op jit(solution)/shard_map/inner_scores/pallas_call | solution.py:474
  17.9 0.0 copy-start.2
  18.0 0.0 copy-start.4
  18.0 0.0 collective-permute-done.2.rb
  18.0 0.6 %collective-permute-done.3.ra = bf16[8,32,128]{2,1,0:T(8,128)(2,1)S(1)} collective-permute-done((bf16[8,32,128]{2,1,0:T(8,128)(2,1)S(1)}, bf16[8,32,128]{2,1,0:T(8,128)(2,1)S(1)}, u32[]{:S(2)}, u32[]{:S(2)}) %collective-permute-start.3) | collective-permute-done | bytes 65568 | tf_op jit(solution)/shard_map/ppermute | solution.py:27
  18.6 1.2 %collective-permute-done.4.cb = bf16[96,128]{1,0:T(8,128)(2,1)S(1)} collective-permute-done((bf16[96,128]{1,0:T(8,128)(2,1)S(1)}, bf16[96,128]{1,0:T(8,128)(2,1)S(1)}, u32[]{:S(2)}, u32[]{:S(2)}) %collective-permute-start.4) | collective-permute-done | bytes 24608 | tf_op jit(solution)/shard_map/ppermute | solution.py:27
  19.8 0.7 %collective-permute-done.5.ca = bf16[96,128]{1,0:T(8,128)(2,1)S(1)} collective-permute-done((bf16[96,128]{1,0:T(8,128)(2,1)S(1)}, bf16[96,128]{1,0:T(8,128)(2,1)S(1)}, u32[]{:S(2)}, u32[]{:S(2)}) %collective-permute-start.5) | collective-permute-done | bytes 24608 | tf_op jit(solution)/shard_map/ppermute | solution.py:27
  20.5 0.3 lower_targets.1.sent
  20.8 1.0 %collective-permute-start.7 = (f32[16,256]{1,0:T(8,128)S(1)}, f32[16,256]{1,0:T(8,128)S(1)}, u32[]{:S(2)}, u32[]{:S(2)}) collective-permute-start(f32[16,256]{1,0:T(8,128)S(1)} %lower_targets.1.sent), channel_id=1, source_target_pairs={{0,240},{16,0},{32,16},{48,32},{64,48},{80,64},{96,80},{112,96},{1... | collective-permute-start | bytes 49160 | tf_op jit(solution)/shard_map/ppermute | solution.py:27
  21.8 1.4 %own_targets.1 = (f32[8,2,256]{2,1,0:T(2,128)S(1)}, f32[8,2,256]{2,1,0:T(2,128)S(1)}, f32[16,256]{1,0:T(8,128)S(1)}, f32[24,256]{1,0:T(8,128)S(1)}, f32[24,256]{...) custom-call(bf16[8,256,128]{2,1,0:T(8,128)(2,1)S(1)} %copy-done, ...), custom_call_target="tpu_custom_call" | custom-call | flops 2147483648 | bytes 1048576 | tf_op jit(solution)/shard_map/own_targets/pallas_call | solution.py:479
  23.2 0.1 collective-permute-start.9
  23.3 2.6 %collective-permute-start.8 = (f32[16,256]{1,0:T(8,128)S(1)}, f32[16,256]{1,0:T(8,128)S(1)}, u32[]{:S(2)}, u32[]{:S(2)}) collective-permute-start(f32[16,256]{1,0:T(8,128)S(1)} %get-tuple-element.25.part), channel_id=1, source_target_pairs={{0,240},{16,32},{32,16},{48,64},{64,48},{80,96},{96,80},{112,128},... | collective-permute-start | bytes 49160 | tf_op jit(solution)/shard_map/ppermute | solution.py:27
  25.9 2.4 %collective-permute-start.13 = (f32[16,256]{1,0:T(8,128)S(1)}, f32[16,256]{1,0:T(8,128)S(1)}, u32[]{:S(2)}, u32[]{:S(2)}) collective-permute-start(f32[16,256]{1,0:T(8,128)S(1)} %first_round.1.u1), channel_id=1, source_target_pairs={{0,12},{1,13},{2,14},{3,15},{4,8},{5,9},{6,10},{7,11},{8,4},{9,5},... | collective-permute-start | bytes 49160 | tf_op jit(solution)/shard_map/ppermute | solution.py:27
  28.3 1.5 %collective-permute-start.12 = (f32[16,256]{1,0:T(8,128)S(1)}, f32[16,256]{1,0:T(8,128)S(1)}, u32[]{:S(2)}, u32[]{:S(2)}) collective-permute-start(f32[16,256]{1,0:T(8,128)S(1)} %first_round.1.u1), channel_id=1, source_target_pairs={{0,4},{1,5},{2,6},{3,7},{4,0},{5,1},{6,2},{7,3},{8,12},{9,13},{10,... | collective-permute-start | bytes 49160 | tf_op jit(solution)/shard_map/ppermute | solution.py:27
  29.8 0.0 collective-permute-start.11
  29.8 1.9 %collective-permute-start.10 = (f32[16,256]{1,0:T(8,128)S(1)}, f32[16,256]{1,0:T(8,128)S(1)}, u32[]{:S(2)}, u32[]{:S(2)}) collective-permute-start(f32[16,256]{1,0:T(8,128)S(1)} %first_round.1.u1), channel_id=1, source_target_pairs={{0,1},{1,0},{2,3},{3,2},{4,5},{5,4},{6,7},{7,6},{8,9},{9,8},{10,11... | collective-permute-start | bytes 49160 | tf_op jit(solution)/shard_map/ppermute | solution.py:27
  31.7 0.6 %all_targets.1 = f32[8,2,2,256]{3,2,1,0:T(2,128)} custom-call(f32[8,2,256]{2,1,0:T(2,128)S(1)} %get-tuple-element.32.p0, f32[8,2,256]{2,1,0:T(2,128)S(1)} %get-tuple-element.33.p1, f32[16,256]{1,0:T(8,128)S(1)} %collective-permute-done.7.got), custom_call_target="tpu_custom_call" | custom-call | flops 1048576 | bytes 1048576 | tf_op jit(solution)/shard_map/all_targets/pallas_call | solution.py:491
  32.3 0.6 %collective-permute-done.12.ra = f32[16,256]{1,0:T(8,128)S(1)} collective-permute-done((f32[16,256]{1,0:T(8,128)S(1)}, f32[16,256]{1,0:T(8,128)S(1)}, u32[]{:S(2)}, u32[]{:S(2)}) %collective-permute-start.12) | collective-permute-done | bytes 16416 | tf_op jit(solution)/shard_map/ppermute | solution.py:27
  33.0 0.6 %collective-permute-done.11.xb = f32[16,256]{1,0:T(8,128)S(1)} collective-permute-done((f32[16,256]{1,0:T(8,128)S(1)}, f32[16,256]{1,0:T(8,128)S(1)}, u32[]{:S(2)}, u32[]{:S(2)}) %collective-permute-start.11) | collective-permute-done | bytes 16416 | tf_op jit(solution)/shard_map/ppermute | solution.py:27
  33.5 0.0 collective-permute-done.10.xa
  33.5 0.7 %second_round.1 = f32[8,2,256]{2,1,0:T(2,128)} custom-call(f32[16,256]{1,0:T(8,128)S(1)} %first_round.1.u1, f32[16,256]{1,0:T(8,128)S(1)} %collective-permute-done.8.sb, f32[16,256]{1,0:T(8,128)S(1)} %collective-permute-done.9.sa, f32[16,256]{1,0:T(8,128)S(1)} %collective-permute-done.10.xa, f32[16,256]{1,0:T(8,128)S(1)} %collective-permute-done.11.xb, ...), custom_call_target="tpu_custom_call" | custom-call | flops 1048576 | bytes 1048576 | tf_op jit(solution)/shard_map/second_round/pallas_call | solution.py:492
  (14 shorter events, 0.0 us)
Async XLA Ops:
  0.6 12.9 %copy-start.1 = (f32[8,2,256]{2,1,0:T(2,128)S(1)}, f32[8,2,256]{2,1,0:T(2,128)}, u32[]{:S(2)}) copy-start(f32[8,2,256]{2,1,0:T(2,128)} %start.9) | copy-start | bytes 49156
  0.6 16.5 %copy-start = (bf16[8,256,128]{2,1,0:T(8,128)(2,1)S(1)}, bf16[8,256,128]{2,1,0:T(8,128)(2,1)}, u32[]{:S(2)}) copy-start(bf16[8,256,128]{2,1,0:T(8,128)(2,1)} %patches.5) | copy-start | bytes 1572868
  2.2 14.9 %copy-start.3 = (s32[8,2,8,256]{3,2,1,0:T(8,128)S(1)}, s32[8,2,8,256]{3,2,1,0:T(8,128)}, u32[]{:S(2)}) copy-start(s32[8,2,8,256]{3,2,1,0:T(8,128)} %cand.5) | copy-start | bytes 393220
  2.3 14.9 %collective-permute-start.6 = (bf16[736,128]{1,0:T(8,128)(2,1)S(1)}, bf16[736,128]{1,0:T(8,128)(2,1)S(1)}, u32[]{:S(2)}, u32[]{:S(2)}) collective-permute-start(bf16[736,128]{1,0:T(8,128)(2,1)S(1)} %get-tuple-element.24), channel_id=1, source_target_pairs={{0,16},{16,32},{32,48},{48,64},{64,80},{80,96},{96,112},{112,128},... | collective-permute-start | bytes 565256 | tf_op jit(solution)/shard_map/ppermute | solution.py:27
  2.3 11.1 %collective-permute-start = (bf16[320,128]{1,0:T(8,128)(2,1)S(1)}, bf16[320,128]{1,0:T(8,128)(2,1)S(1)}, u32[]{:S(2)}, u32[]{:S(2)}) collective-permute-start(bf16[320,128]{1,0:T(8,128)(2,1)S(1)} %get-tuple-element.18), channel_id=1, source_target_pairs={{0,3},{1,2},{2,1},{3,0},{4,7},{5,6},{6,5},{7,4},{8,11},{9,10},{10,... | collective-permute-start | bytes 245768 | tf_op jit(solution)/shard_map/ppermute | solution.py:27
  3.9 9.6 %collective-permute-start.1 = (bf16[320,128]{1,0:T(8,128)(2,1)S(1)}, bf16[320,128]{1,0:T(8,128)(2,1)S(1)}, u32[]{:S(2)}, u32[]{:S(2)}) collective-permute-start(bf16[320,128]{1,0:T(8,128)(2,1)S(1)} %get-tuple-element.19), channel_id=1, source_target_pairs={{0,1},{1,0},{2,3},{3,2},{4,5},{5,4},{6,7},{7,6},{8,9},{9,8},{10,11... | collective-permute-start | bytes 245768 | tf_op jit(solution)/shard_map/ppermute | solution.py:27
  5.7 12.2 %collective-permute-start.2 = (bf16[8,32,128]{2,1,0:T(8,128)(2,1)S(1)}, bf16[8,32,128]{2,1,0:T(8,128)(2,1)S(1)}, u32[]{:S(2)}, u32[]{:S(2)}) collective-permute-start(bf16[8,32,128]{2,1,0:T(8,128)(2,1)S(1)} %get-tuple-element.20), channel_id=1, source_target_pairs={{0,12},{1,13},{2,14},{3,15},{4,8},{5,9},{6,10},{7,11},{8,4},{9,5},... | collective-permute-start | bytes 196616 | tf_op jit(solution)/shard_map/ppermute | solution.py:27
  12.0 6.6 %collective-permute-start.3 = (bf16[8,32,128]{2,1,0:T(8,128)(2,1)S(1)}, bf16[8,32,128]{2,1,0:T(8,128)(2,1)S(1)}, u32[]{:S(2)}, u32[]{:S(2)}) collective-permute-start(bf16[8,32,128]{2,1,0:T(8,128)(2,1)S(1)} %get-tuple-element.21), channel_id=1, source_target_pairs={{0,4},{1,5},{2,6},{3,7},{4,0},{5,1},{6,2},{7,3},{8,12},{9,13},{10,... | collective-permute-start | bytes 196616 | tf_op jit(solution)/shard_map/ppermute | solution.py:27
  13.7 6.0 %collective-permute-start.4 = (bf16[96,128]{1,0:T(8,128)(2,1)S(1)}, bf16[96,128]{1,0:T(8,128)(2,1)S(1)}, u32[]{:S(2)}, u32[]{:S(2)}) collective-permute-start(bf16[96,128]{1,0:T(8,128)(2,1)S(1)} %get-tuple-element.22), channel_id=1, source_target_pairs={{0,12},{1,13},{2,14},{3,15},{4,8},{5,9},{6,10},{7,11},{8,4},{9,5},... | collective-permute-start | bytes 73736 | tf_op jit(solution)/shard_map/ppermute | solution.py:27
  15.7 4.8 %collective-permute-start.5 = (bf16[96,128]{1,0:T(8,128)(2,1)S(1)}, bf16[96,128]{1,0:T(8,128)(2,1)S(1)}, u32[]{:S(2)}, u32[]{:S(2)}) collective-permute-start(bf16[96,128]{1,0:T(8,128)(2,1)S(1)} %get-tuple-element.23), channel_id=1, source_target_pairs={{0,4},{1,5},{2,6},{3,7},{4,0},{5,1},{6,2},{7,3},{8,12},{9,13},{10,... | collective-permute-start | bytes 73736 | tf_op jit(solution)/shard_map/ppermute | solution.py:27
  17.9 3.8 %copy-start.2 = (s32[8,2,2,8,256]{4,3,2,1,0:T(8,128)S(1)}, s32[8,2,2,8,256]{4,3,2,1,0:T(8,128)}, u32[]{:S(2)}) copy-start(s32[8,2,2,8,256]{4,3,2,1,0:T(8,128)} %offs.3) | copy-start | bytes 786436
  18.0 3.8 %copy-start.4 = (s32[8,2]{0,1:T(2,128)S(1)}, s32[8,2]{0,1:T(2,128)}, u32[]{:S(2)}) copy-start(s32[8,2]{0,1:T(2,128)} %param.8) | copy-start | bytes 196
  20.8 5.1 %collective-permute-start.7 = (f32[16,256]{1,0:T(8,128)S(1)}, f32[16,256]{1,0:T(8,128)S(1)}, u32[]{:S(2)}, u32[]{:S(2)}) collective-permute-start(f32[16,256]{1,0:T(8,128)S(1)} %lower_targets.1.sent), channel_id=1, source_target_pairs={{0,240},{16,0},{32,16},{48,32},{64,48},{80,64},{96,80},{112,96},{1... | collective-permute-start | bytes 49160 | tf_op jit(solution)/shard_map/ppermute | solution.py:27
  23.2 6.6 %collective-permute-start.9 = (f32[16,256]{1,0:T(8,128)S(1)}, f32[16,256]{1,0:T(8,128)S(1)}, u32[]{:S(2)}, u32[]{:S(2)}) collective-permute-start(f32[16,256]{1,0:T(8,128)S(1)} %get-tuple-element.25.part), channel_id=1, source_target_pairs={{0,16},{16,0},{32,48},{48,32},{64,80},{80,64},{96,112},{112,96},{1... | collective-permute-start | bytes 49160 | tf_op jit(solution)/shard_map/ppermute | solution.py:27
  23.3 9.1 %collective-permute-start.8 = (f32[16,256]{1,0:T(8,128)S(1)}, f32[16,256]{1,0:T(8,128)S(1)}, u32[]{:S(2)}, u32[]{:S(2)}) collective-permute-start(f32[16,256]{1,0:T(8,128)S(1)} %get-tuple-element.25.part), channel_id=1, source_target_pairs={{0,240},{16,32},{32,16},{48,64},{64,48},{80,96},{96,80},{112,128},... | collective-permute-start | bytes 49160 | tf_op jit(solution)/shard_map/ppermute | solution.py:27
  25.9 6.4 %collective-permute-start.13 = (f32[16,256]{1,0:T(8,128)S(1)}, f32[16,256]{1,0:T(8,128)S(1)}, u32[]{:S(2)}, u32[]{:S(2)}) collective-permute-start(f32[16,256]{1,0:T(8,128)S(1)} %first_round.1.u1), channel_id=1, source_target_pairs={{0,12},{1,13},{2,14},{3,15},{4,8},{5,9},{6,10},{7,11},{8,4},{9,5},... | collective-permute-start | bytes 49160 | tf_op jit(solution)/shard_map/ppermute | solution.py:27
  28.3 4.6 %collective-permute-start.12 = (f32[16,256]{1,0:T(8,128)S(1)}, f32[16,256]{1,0:T(8,128)S(1)}, u32[]{:S(2)}, u32[]{:S(2)}) collective-permute-start(f32[16,256]{1,0:T(8,128)S(1)} %first_round.1.u1), channel_id=1, source_target_pairs={{0,4},{1,5},{2,6},{3,7},{4,0},{5,1},{6,2},{7,3},{8,12},{9,13},{10,... | collective-permute-start | bytes 49160 | tf_op jit(solution)/shard_map/ppermute | solution.py:27
  29.8 3.7 %collective-permute-start.11 = (f32[16,256]{1,0:T(8,128)S(1)}, f32[16,256]{1,0:T(8,128)S(1)}, u32[]{:S(2)}, u32[]{:S(2)}) collective-permute-start(f32[16,256]{1,0:T(8,128)S(1)} %first_round.1.u1), channel_id=1, source_target_pairs={{0,3},{1,2},{2,1},{3,0},{4,7},{5,6},{6,5},{7,4},{8,11},{9,10},{10,... | collective-permute-start | bytes 49160 | tf_op jit(solution)/shard_map/ppermute | solution.py:27
  29.8 3.7 %collective-permute-start.10 = (f32[16,256]{1,0:T(8,128)S(1)}, f32[16,256]{1,0:T(8,128)S(1)}, u32[]{:S(2)}, u32[]{:S(2)}) collective-permute-start(f32[16,256]{1,0:T(8,128)S(1)} %first_round.1.u1), channel_id=1, source_target_pairs={{0,1},{1,0},{2,3},{3,2},{4,5},{5,4},{6,7},{7,6},{8,9},{9,8},{10,11... | collective-permute-start | bytes 49160 | tf_op jit(solution)/shard_map/ppermute | solution.py:27

commit v6 on v4

--- a/solution.py
+++ b/solution.py
@@ -269,7 +269,8 @@
 ):
     row, col = tile_place()
     stack = lax.axis_index("stack").astype(I32)
-    sort_halos(col, left, right, xa, xb)
+    ends = slice(256, X_ROWS)
+    sort_halos(col, left.at[ends], right.at[ends], xa.at[ends], xb.at[ends])
     sort_halos(row, above, below, ra, rb)
     sort_halos(row, top, bottom, ca, cb)
 

time: 34.8 us -> 34.8 us (level)
  no operation moved by 1% of the time
where the time goes in v6:
time: 34.8 us; the launch traced here: 34.2 us
  starting transfers between devices  24.1 us (69%)
  Pallas kernels  5.54 us (16%)
  waiting for transfers between devices  3.74 us (11%)
  between operations  0.76 us (2%)
    ppermute x14, starting transfers between devices, swapped(): lax.ppermute(block, axis, [(i, partner(i)) for i in range(lax.axis_size(a...  24.1 us
    ppermute x14, waiting for transfers between devices, swapped(): lax.ppermute(block, axis, [(i, partner(i)) for i in range(lax.axis_size(a...  3.74 us
    pallas_call x1, Pallas kernels, on_device(): call(pack_first, outs, [flat] + held, 1 << 20, 5, far=(0, 1, 2, 3, 4), vm...  1.53 us
    pallas_call x1, Pallas kernels, on_device(): call(own_targets, [shape(SEC, 2, VT)] * 2 + [shape(16, VT)] + [shape(24,...  1.4 us
    pallas_call x1, Pallas kernels, on_device(): call(inner_scores, [shape(2, SEC + 2, 2, 8, HALF)], [pltpu.VMEM((X_ROWS,...  0.76 us
    pallas_call x1, Pallas kernels, on_device(): call(second_round, [shape(SEC, 2, VT)], [pltpu.VMEM((24, VT), F32)], 1 <<...  0.73 us
  transfers between devices with their start and end apart: 14, of which 5 were waited for; matrix products, arithmetic and copies ran while one was open for 0% of the time, Pallas kernels for 9%

profile of v6, /device:TPU:2, one launch (start us, length us, event | category | flops | bytes accessed | tf_op | source)
XLA Modules:
  0.0 34.2 jit_solution(5411287666234138827)
XLA Ops:
  0.6 1.5 %pack_first.1 = (bf16[8,32,128]{2,1,0:T(8,128)(2,1)S(1)}, bf16[8,32,128]{2,1,0:T(8,128)(2,1)S(1)}, bf16[320,128]{1,0:T(8,128)(2,1)S(1)}, bf16[320,128]{1,0:T(8,128)(2,1)S(1)}, bf16[736,128]{1,0:T(8,128)(2,1)S(1)}) custom-call(bf16[8,256,128]{2,1,0:T(8,128)(2,1)} %patches.5, s32[8,2,8,256]{3,2,1,0:T(8,128)} %cand.5, s32[8,2,2,8,256]{4,3,2,1,0:T(8,128)} %offs.3, ...), custom_call_target="tpu_custom_call" | custom-call | flops 1048576 | bytes 1048576 | tf_op jit(solution)/shard_map/pack_first/pallas_call | solution.py:463
  2.2 0.0 copy-start.3
  2.2 0.1 collective-permute-start.6
  2.3 1.6 %collective-permute-start = (bf16[320,128]{1,0:T(8,128)(2,1)S(1)}, bf16[320,128]{1,0:T(8,128)(2,1)S(1)}, u32[]{:S(2)}, u32[]{:S(2)}) collective-permute-start(bf16[320,128]{1,0:T(8,128)(2,1)S(1)} %get-tuple-element.18), channel_id=1, source_target_pairs={{0,3},{1,2},{2,1},{3,0},{4,7},{5,6},{6,5},{7,4},{8,11},{9,10},{10,... | collective-permute-start | bytes 245768 | tf_op jit(solution)/shard_map/ppermute | solution.py:27
  3.9 1.8 %collective-permute-start.1 = (bf16[320,128]{1,0:T(8,128)(2,1)S(1)}, bf16[320,128]{1,0:T(8,128)(2,1)S(1)}, u32[]{:S(2)}, u32[]{:S(2)}) collective-permute-start(bf16[320,128]{1,0:T(8,128)(2,1)S(1)} %get-tuple-element.19), channel_id=1, source_target_pairs={{0,1},{1,0},{2,3},{3,2},{4,5},{5,4},{6,7},{7,6},{8,9},{9,8},{10,11... | collective-permute-start | bytes 245768 | tf_op jit(solution)/shard_map/ppermute | solution.py:27
  5.7 6.3 %collective-permute-start.2 = (bf16[8,32,128]{2,1,0:T(8,128)(2,1)S(1)}, bf16[8,32,128]{2,1,0:T(8,128)(2,1)S(1)}, u32[]{:S(2)}, u32[]{:S(2)}) collective-permute-start(bf16[8,32,128]{2,1,0:T(8,128)(2,1)S(1)} %get-tuple-element.20), channel_id=1, source_target_pairs={{0,12},{1,13},{2,14},{3,15},{4,8},{5,9},{6,10},{7,11},{8,4},{9,5},... | collective-permute-start | bytes 196616 | tf_op jit(solution)/shard_map/ppermute | solution.py:27
  12.0 1.5 %collective-permute-start.3 = (bf16[8,32,128]{2,1,0:T(8,128)(2,1)S(1)}, bf16[8,32,128]{2,1,0:T(8,128)(2,1)S(1)}, u32[]{:S(2)}, u32[]{:S(2)}) collective-permute-start(bf16[8,32,128]{2,1,0:T(8,128)(2,1)S(1)} %get-tuple-element.21), channel_id=1, source_target_pairs={{0,4},{1,5},{2,6},{3,7},{4,0},{5,1},{6,2},{7,3},{8,12},{9,13},{10,... | collective-permute-start | bytes 196616 | tf_op jit(solution)/shard_map/ppermute | solution.py:27
  13.4 0.0 collective-permute-done.xb
  13.4 0.0 collective-permute-done.1.xa
  13.4 0.2 pack_corners.1
  13.7 2.0 %collective-permute-start.4 = (bf16[96,128]{1,0:T(8,128)(2,1)S(1)}, bf16[96,128]{1,0:T(8,128)(2,1)S(1)}, u32[]{:S(2)}, u32[]{:S(2)}) collective-permute-start(bf16[96,128]{1,0:T(8,128)(2,1)S(1)} %get-tuple-element.22), channel_id=1, source_target_pairs={{0,12},{1,13},{2,14},{3,15},{4,8},{5,9},{6,10},{7,11},{8,4},{9,5},... | collective-permute-start | bytes 73736 | tf_op jit(solution)/shard_map/ppermute | solution.py:27
  15.6 1.5 %collective-permute-start.5 = (bf16[96,128]{1,0:T(8,128)(2,1)S(1)}, bf16[96,128]{1,0:T(8,128)(2,1)S(1)}, u32[]{:S(2)}, u32[]{:S(2)}) collective-permute-start(bf16[96,128]{1,0:T(8,128)(2,1)S(1)} %get-tuple-element.23), channel_id=1, source_target_pairs={{0,4},{1,5},{2,6},{3,7},{4,0},{5,1},{6,2},{7,3},{8,12},{9,13},{10,... | collective-permute-start | bytes 73736 | tf_op jit(solution)/shard_map/ppermute | solution.py:27
  17.1 0.8 %inner_scores.1.inner = f32[2,10,2,8,128]{4,3,2,1,0:T(8,128)S(1)} custom-call(bf16[8,256,128]{2,1,0:T(8,128)(2,1)S(1)} %copy-done, s32[8,2,8,256]{3,2,1,0:T(8,128)S(1)} %copy-done.3, bf16[320,128]{1,0:T(8,128)(2,1)S(1)} %collective-permute-done.xb, bf16[320,128]{1,0:T(8,128)(2,1)S(1)} %collective-permute-done.1.xa, ...), custom_call_target="tpu_custom_call" | custom-call | flops 2147483648 | bytes 1048576 | tf_op jit(solution)/shard_map/inner_scores/pallas_call | solution.py:475
  17.9 0.0 copy-start.2
  17.9 0.0 copy-start.4
  17.9 0.6 %collective-permute-done.3.ra = bf16[8,32,128]{2,1,0:T(8,128)(2,1)S(1)} collective-permute-done((bf16[8,32,128]{2,1,0:T(8,128)(2,1)S(1)}, bf16[8,32,128]{2,1,0:T(8,128)(2,1)S(1)}, u32[]{:S(2)}, u32[]{:S(2)}) %collective-permute-start.3) | collective-permute-done | bytes 65568 | tf_op jit(solution)/shard_map/ppermute | solution.py:27
  18.5 1.2 %collective-permute-done.4.cb = bf16[96,128]{1,0:T(8,128)(2,1)S(1)} collective-permute-done((bf16[96,128]{1,0:T(8,128)(2,1)S(1)}, bf16[96,128]{1,0:T(8,128)(2,1)S(1)}, u32[]{:S(2)}, u32[]{:S(2)}) %collective-permute-start.4) | collective-permute-done | bytes 24608 | tf_op jit(solution)/shard_map/ppermute | solution.py:27
  19.7 0.7 %collective-permute-done.5.ca = bf16[96,128]{1,0:T(8,128)(2,1)S(1)} collective-permute-done((bf16[96,128]{1,0:T(8,128)(2,1)S(1)}, bf16[96,128]{1,0:T(8,128)(2,1)S(1)}, u32[]{:S(2)}, u32[]{:S(2)}) %collective-permute-start.5) | collective-permute-done | bytes 24608 | tf_op jit(solution)/shard_map/ppermute | solution.py:27
  20.4 0.3 lower_targets.1.sent
  20.7 1.0 %collective-permute-start.7 = (f32[16,256]{1,0:T(8,128)S(1)}, f32[16,256]{1,0:T(8,128)S(1)}, u32[]{:S(2)}, u32[]{:S(2)}) collective-permute-start(f32[16,256]{1,0:T(8,128)S(1)} %lower_targets.1.sent), channel_id=1, source_target_pairs={{0,240},{16,0},{32,16},{48,32},{64,48},{80,64},{96,80},{112,96},{1... | collective-permute-start | bytes 49160 | tf_op jit(solution)/shard_map/ppermute | solution.py:27
  21.7 1.4 %own_targets.1 = (f32[8,2,256]{2,1,0:T(2,128)S(1)}, f32[8,2,256]{2,1,0:T(2,128)S(1)}, f32[16,256]{1,0:T(8,128)S(1)}, f32[24,256]{1,0:T(8,128)S(1)}, f32[24,256]{...) custom-call(bf16[8,256,128]{2,1,0:T(8,128)(2,1)S(1)} %copy-done, ...), custom_call_target="tpu_custom_call" | custom-call | flops 2147483648 | bytes 1048576 | tf_op jit(solution)/shard_map/own_targets/pallas_call | solution.py:480
  23.1 0.1 collective-permute-start.9
  23.2 2.6 %collective-permute-start.8 = (f32[16,256]{1,0:T(8,128)S(1)}, f32[16,256]{1,0:T(8,128)S(1)}, u32[]{:S(2)}, u32[]{:S(2)}) collective-permute-start(f32[16,256]{1,0:T(8,128)S(1)} %get-tuple-element.25.part), channel_id=1, source_target_pairs={{0,240},{16,32},{32,16},{48,64},{64,48},{80,96},{96,80},{112,128},... | collective-permute-start | bytes 49160 | tf_op jit(solution)/shard_map/ppermute | solution.py:27
  25.8 2.4 %collective-permute-start.13 = (f32[16,256]{1,0:T(8,128)S(1)}, f32[16,256]{1,0:T(8,128)S(1)}, u32[]{:S(2)}, u32[]{:S(2)}) collective-permute-start(f32[16,256]{1,0:T(8,128)S(1)} %first_round.1.u1), channel_id=1, source_target_pairs={{0,12},{1,13},{2,14},{3,15},{4,8},{5,9},{6,10},{7,11},{8,4},{9,5},... | collective-permute-start | bytes 49160 | tf_op jit(solution)/shard_map/ppermute | solution.py:27
  28.3 1.5 %collective-permute-start.12 = (f32[16,256]{1,0:T(8,128)S(1)}, f32[16,256]{1,0:T(8,128)S(1)}, u32[]{:S(2)}, u32[]{:S(2)}) collective-permute-start(f32[16,256]{1,0:T(8,128)S(1)} %first_round.1.u1), channel_id=1, source_target_pairs={{0,4},{1,5},{2,6},{3,7},{4,0},{5,1},{6,2},{7,3},{8,12},{9,13},{10,... | collective-permute-start | bytes 49160 | tf_op jit(solution)/shard_map/ppermute | solution.py:27
  29.7 0.0 collective-permute-start.11
  29.7 1.9 %collective-permute-start.10 = (f32[16,256]{1,0:T(8,128)S(1)}, f32[16,256]{1,0:T(8,128)S(1)}, u32[]{:S(2)}, u32[]{:S(2)}) collective-permute-start(f32[16,256]{1,0:T(8,128)S(1)} %first_round.1.u1), channel_id=1, source_target_pairs={{0,1},{1,0},{2,3},{3,2},{4,5},{5,4},{6,7},{7,6},{8,9},{9,8},{10,11... | collective-permute-start | bytes 49160 | tf_op jit(solution)/shard_map/ppermute | solution.py:27
  31.7 0.6 %all_targets.1 = f32[8,2,2,256]{3,2,1,0:T(2,128)} custom-call(f32[8,2,256]{2,1,0:T(2,128)S(1)} %get-tuple-element.32.p0, f32[8,2,256]{2,1,0:T(2,128)S(1)} %get-tuple-element.33.p1, f32[16,256]{1,0:T(8,128)S(1)} %collective-permute-done.7.got), custom_call_target="tpu_custom_call" | custom-call | flops 1048576 | bytes 1048576 | tf_op jit(solution)/shard_map/all_targets/pallas_call | solution.py:492
  32.3 0.6 %collective-permute-done.12.ra = f32[16,256]{1,0:T(8,128)S(1)} collective-permute-done((f32[16,256]{1,0:T(8,128)S(1)}, f32[16,256]{1,0:T(8,128)S(1)}, u32[]{:S(2)}, u32[]{:S(2)}) %collective-permute-start.12) | collective-permute-done | bytes 16416 | tf_op jit(solution)/shard_map/ppermute | solution.py:27
  32.9 0.6 %collective-permute-done.11.xb = f32[16,256]{1,0:T(8,128)S(1)} collective-permute-done((f32[16,256]{1,0:T(8,128)S(1)}, f32[16,256]{1,0:T(8,128)S(1)}, u32[]{:S(2)}, u32[]{:S(2)}) %collective-permute-start.11) | collective-permute-done | bytes 16416 | tf_op jit(solution)/shard_map/ppermute | solution.py:27
  33.5 0.0 collective-permute-done.10.xa
  33.5 0.7 %second_round.1 = f32[8,2,256]{2,1,0:T(2,128)} custom-call(f32[16,256]{1,0:T(8,128)S(1)} %first_round.1.u1, f32[16,256]{1,0:T(8,128)S(1)} %collective-permute-done.8.sb, f32[16,256]{1,0:T(8,128)S(1)} %collective-permute-done.9.sa, f32[16,256]{1,0:T(8,128)S(1)} %collective-permute-done.10.xa, f32[16,256]{1,0:T(8,128)S(1)} %collective-permute-done.11.xb, ...), custom_call_target="tpu_custom_call" | custom-call | flops 1048576 | bytes 1048576 | tf_op jit(solution)/shard_map/second_round/pallas_call | solution.py:493
  (14 shorter events, 0.0 us)
Async XLA Ops:
  0.6 12.8 %copy-start.1 = (f32[8,2,256]{2,1,0:T(2,128)S(1)}, f32[8,2,256]{2,1,0:T(2,128)}, u32[]{:S(2)}) copy-start(f32[8,2,256]{2,1,0:T(2,128)} %start.9) | copy-start | bytes 49156
  0.6 16.5 %copy-start = (bf16[8,256,128]{2,1,0:T(8,128)(2,1)S(1)}, bf16[8,256,128]{2,1,0:T(8,128)(2,1)}, u32[]{:S(2)}) copy-start(bf16[8,256,128]{2,1,0:T(8,128)(2,1)} %patches.5) | copy-start | bytes 1572868
  2.2 14.9 %copy-start.3 = (s32[8,2,8,256]{3,2,1,0:T(8,128)S(1)}, s32[8,2,8,256]{3,2,1,0:T(8,128)}, u32[]{:S(2)}) copy-start(s32[8,2,8,256]{3,2,1,0:T(8,128)} %cand.5) | copy-start | bytes 393220
  2.2 14.9 %collective-permute-start.6 = (bf16[736,128]{1,0:T(8,128)(2,1)S(1)}, bf16[736,128]{1,0:T(8,128)(2,1)S(1)}, u32[]{:S(2)}, u32[]{:S(2)}) collective-permute-start(bf16[736,128]{1,0:T(8,128)(2,1)S(1)} %get-tuple-element.24), channel_id=1, source_target_pairs={{0,16},{16,32},{32,48},{48,64},{64,80},{80,96},{96,112},{112,128},... | collective-permute-start | bytes 565256 | tf_op jit(solution)/shard_map/ppermute | solution.py:27
  2.3 11.1 %collective-permute-start = (bf16[320,128]{1,0:T(8,128)(2,1)S(1)}, bf16[320,128]{1,0:T(8,128)(2,1)S(1)}, u32[]{:S(2)}, u32[]{:S(2)}) collective-permute-start(bf16[320,128]{1,0:T(8,128)(2,1)S(1)} %get-tuple-element.18), channel_id=1, source_target_pairs={{0,3},{1,2},{2,1},{3,0},{4,7},{5,6},{6,5},{7,4},{8,11},{9,10},{10,... | collective-permute-start | bytes 245768 | tf_op jit(solution)/shard_map/ppermute | solution.py:27
  3.9 9.6 %collective-permute-start.1 = (bf16[320,128]{1,0:T(8,128)(2,1)S(1)}, bf16[320,128]{1,0:T(8,128)(2,1)S(1)}, u32[]{:S(2)}, u32[]{:S(2)}) collective-permute-start(bf16[320,128]{1,0:T(8,128)(2,1)S(1)} %get-tuple-element.19), channel_id=1, source_target_pairs={{0,1},{1,0},{2,3},{3,2},{4,5},{5,4},{6,7},{7,6},{8,9},{9,8},{10,11... | collective-permute-start | bytes 245768 | tf_op jit(solution)/shard_map/ppermute | solution.py:27
  5.7 12.2 %collective-permute-start.2 = (bf16[8,32,128]{2,1,0:T(8,128)(2,1)S(1)}, bf16[8,32,128]{2,1,0:T(8,128)(2,1)S(1)}, u32[]{:S(2)}, u32[]{:S(2)}) collective-permute-start(bf16[8,32,128]{2,1,0:T(8,128)(2,1)S(1)} %get-tuple-element.20), channel_id=1, source_target_pairs={{0,12},{1,13},{2,14},{3,15},{4,8},{5,9},{6,10},{7,11},{8,4},{9,5},... | collective-permute-start | bytes 196616 | tf_op jit(solution)/shard_map/ppermute | solution.py:27
  12.0 6.6 %collective-permute-start.3 = (bf16[8,32,128]{2,1,0:T(8,128)(2,1)S(1)}, bf16[8,32,128]{2,1,0:T(8,128)(2,1)S(1)}, u32[]{:S(2)}, u32[]{:S(2)}) collective-permute-start(bf16[8,32,128]{2,1,0:T(8,128)(2,1)S(1)} %get-tuple-element.21), channel_id=1, source_target_pairs={{0,4},{1,5},{2,6},{3,7},{4,0},{5,1},{6,2},{7,3},{8,12},{9,13},{10,... | collective-permute-start | bytes 196616 | tf_op jit(solution)/shard_map/ppermute | solution.py:27
  13.7 6.0 %collective-permute-start.4 = (bf16[96,128]{1,0:T(8,128)(2,1)S(1)}, bf16[96,128]{1,0:T(8,128)(2,1)S(1)}, u32[]{:S(2)}, u32[]{:S(2)}) collective-permute-start(bf16[96,128]{1,0:T(8,128)(2,1)S(1)} %get-tuple-element.22), channel_id=1, source_target_pairs={{0,12},{1,13},{2,14},{3,15},{4,8},{5,9},{6,10},{7,11},{8,4},{9,5},... | collective-permute-start | bytes 73736 | tf_op jit(solution)/shard_map/ppermute | solution.py:27
  15.6 4.8 %collective-permute-start.5 = (bf16[96,128]{1,0:T(8,128)(2,1)S(1)}, bf16[96,128]{1,0:T(8,128)(2,1)S(1)}, u32[]{:S(2)}, u32[]{:S(2)}) collective-permute-start(bf16[96,128]{1,0:T(8,128)(2,1)S(1)} %get-tuple-element.23), channel_id=1, source_target_pairs={{0,4},{1,5},{2,6},{3,7},{4,0},{5,1},{6,2},{7,3},{8,12},{9,13},{10,... | collective-permute-start | bytes 73736 | tf_op jit(solution)/shard_map/ppermute | solution.py:27
  17.9 3.8 %copy-start.2 = (s32[8,2,2,8,256]{4,3,2,1,0:T(8,128)S(1)}, s32[8,2,2,8,256]{4,3,2,1,0:T(8,128)}, u32[]{:S(2)}) copy-start(s32[8,2,2,8,256]{4,3,2,1,0:T(8,128)} %offs.3) | copy-start | bytes 786436
  17.9 3.8 %copy-start.4 = (s32[8,2]{0,1:T(2,128)S(1)}, s32[8,2]{0,1:T(2,128)}, u32[]{:S(2)}) copy-start(s32[8,2]{0,1:T(2,128)} %param.8) | copy-start | bytes 196
  20.7 5.1 %collective-permute-start.7 = (f32[16,256]{1,0:T(8,128)S(1)}, f32[16,256]{1,0:T(8,128)S(1)}, u32[]{:S(2)}, u32[]{:S(2)}) collective-permute-start(f32[16,256]{1,0:T(8,128)S(1)} %lower_targets.1.sent), channel_id=1, source_target_pairs={{0,240},{16,0},{32,16},{48,32},{64,48},{80,64},{96,80},{112,96},{1... | collective-permute-start | bytes 49160 | tf_op jit(solution)/shard_map/ppermute | solution.py:27
  23.1 6.6 %collective-permute-start.9 = (f32[16,256]{1,0:T(8,128)S(1)}, f32[16,256]{1,0:T(8,128)S(1)}, u32[]{:S(2)}, u32[]{:S(2)}) collective-permute-start(f32[16,256]{1,0:T(8,128)S(1)} %get-tuple-element.25.part), channel_id=1, source_target_pairs={{0,16},{16,0},{32,48},{48,32},{64,80},{80,64},{96,112},{112,96},{1... | collective-permute-start | bytes 49160 | tf_op jit(solution)/shard_map/ppermute | solution.py:27
  23.2 9.1 %collective-permute-start.8 = (f32[16,256]{1,0:T(8,128)S(1)}, f32[16,256]{1,0:T(8,128)S(1)}, u32[]{:S(2)}, u32[]{:S(2)}) collective-permute-start(f32[16,256]{1,0:T(8,128)S(1)} %get-tuple-element.25.part), channel_id=1, source_target_pairs={{0,240},{16,32},{32,16},{48,64},{64,48},{80,96},{96,80},{112,128},... | collective-permute-start | bytes 49160 | tf_op jit(solution)/shard_map/ppermute | solution.py:27
  25.8 6.4 %collective-permute-start.13 = (f32[16,256]{1,0:T(8,128)S(1)}, f32[16,256]{1,0:T(8,128)S(1)}, u32[]{:S(2)}, u32[]{:S(2)}) collective-permute-start(f32[16,256]{1,0:T(8,128)S(1)} %first_round.1.u1), channel_id=1, source_target_pairs={{0,12},{1,13},{2,14},{3,15},{4,8},{5,9},{6,10},{7,11},{8,4},{9,5},... | collective-permute-start | bytes 49160 | tf_op jit(solution)/shard_map/ppermute | solution.py:27
  28.3 4.6 %collective-permute-start.12 = (f32[16,256]{1,0:T(8,128)S(1)}, f32[16,256]{1,0:T(8,128)S(1)}, u32[]{:S(2)}, u32[]{:S(2)}) collective-permute-start(f32[16,256]{1,0:T(8,128)S(1)} %first_round.1.u1), channel_id=1, source_target_pairs={{0,4},{1,5},{2,6},{3,7},{4,0},{5,1},{6,2},{7,3},{8,12},{9,13},{10,... | collective-permute-start | bytes 49160 | tf_op jit(solution)/shard_map/ppermute | solution.py:27
  29.7 3.7 %collective-permute-start.11 = (f32[16,256]{1,0:T(8,128)S(1)}, f32[16,256]{1,0:T(8,128)S(1)}, u32[]{:S(2)}, u32[]{:S(2)}) collective-permute-start(f32[16,256]{1,0:T(8,128)S(1)} %first_round.1.u1), channel_id=1, source_target_pairs={{0,3},{1,2},{2,1},{3,0},{4,7},{5,6},{6,5},{7,4},{8,11},{9,10},{10,... | collective-permute-start | bytes 49160 | tf_op jit(solution)/shard_map/ppermute | solution.py:27
  29.7 3.7 %collective-permute-start.10 = (f32[16,256]{1,0:T(8,128)S(1)}, f32[16,256]{1,0:T(8,128)S(1)}, u32[]{:S(2)}, u32[]{:S(2)}) collective-permute-start(f32[16,256]{1,0:T(8,128)S(1)} %first_round.1.u1), channel_id=1, source_target_pairs={{0,1},{1,0},{2,3},{3,2},{4,5},{5,4},{6,7},{7,6},{8,9},{9,8},{10,11... | collective-permute-start | bytes 49160 | tf_op jit(solution)/shard_map/ppermute | solution.py:27
